TPU v7x, 32 devices: a whole 2x2x4 slice. The times are simulated.
32 devices in a mesh: gx: 4 (over y, core), gy: 8 (over z, x).
Axes of the slice: x: 2, y: 2, z: 4, core: 2. Of those that a mesh axis runs over, the one named last changes fastest.
Arguments:
- patches: bfloat16 [2048, 1664], P(('gx', 'gy')), may hold values from -6 to 6
- prompt: bfloat16 [2560, 1664], P(('gx', 'gy')), may hold values from -6 to 6
- image_ids: int32 [4, 128], P('gx'), may hold values from 0 to 3, never falling along the last dimension, each value on 1 to 64 neighbouring positions
- positions: int32 [4, 128], P('gx'), may hold values from 0 to 639, as said below
- norm_gains: float32 [5, 1664], replicated, may hold values from 0.25 to 1.75
- vit_qkv: bfloat16 [1664, 4992], P('gx', 'gy'), may hold values from -0.24514517 to 0.24514517
- vit_out: bfloat16 [1664, 1664], P('gx', 'gy'), may hold values from -0.15625 to 0.15625
- vit_up: bfloat16 [1664, 8192], P('gx', 'gy'), may hold values from -0.15625 to 0.15625
- vit_down: bfloat16 [1664, 8192], P('gx', 'gy'), may hold values from -0.0625 to 0.0625
- merge_proj: bfloat16 [6656, 1664], P('gx', 'gy'), may hold values from -0.078125 to 0.078125
- dec_qkv: bfloat16 [1664, 4992], P('gx', 'gy'), may hold values from -0.24514517 to 0.24514517
- dec_out: bfloat16 [1664, 1664], P('gx', 'gy'), may hold values from -0.15625 to 0.15625
- dec_up: bfloat16 [1664, 8192], P('gx', 'gy'), may hold values from -0.15625 to 0.15625
- dec_down: bfloat16 [1664, 8192], P('gx', 'gy'), may hold values from -0.0625 to 0.0625
Outputs:
- decoded: bfloat16 [2560, 1664], P(('gx', 'gy'))
Inputs may be any that keep to these rules, and one draw needn't show every extreme that they name: `image_ids`: within each sequence image numbers never fall, and each of the 4 images has at least one merged row. Within each sequence the positions strictly increase.
All inputs are finite; a program needn't handle non-finite values.
Results may differ from a plain program's by a relative error of at most 0.03.
Values may be sent and summed in bfloat16 or wider, within the bound.
No kernel may reach another device: no remote copies, remote signals or barrier semaphores. Data moves between devices by JAX's collectives and lax.ppermute only.
A program may use at most 64 MiB of HBM per device.

v0:
```python
import functools
import math

import jax
import jax.numpy as jnp
from jax import lax
from jax.experimental import pallas as pl
from jax.experimental.pallas import tpu as pltpu
from jax.sharding import PartitionSpec as P

HEAD_DIM = 104
BF = jnp.bfloat16
F32 = jnp.float32


def layer_norm(rows, gain):
    values = rows.astype(F32)
    center = values - jnp.mean(values, axis=-1, keepdims=True)
    spread = jnp.mean(center * center, axis=-1, keepdims=True)
    return center * lax.rsqrt(spread + 1e-06) * gain


def rms_norm(rows, gain):
    values = rows.astype(F32)
    return values * lax.rsqrt(jnp.mean(values * values, axis=-1, keepdims=True) + 1e-06) * gain


def grid_of(count):
    fast = 2 ** ((count.bit_length() - 1) // 2)
    return count // fast, fast


def moved(value, dz, dx):
    nz, nx = grid_of(lax.axis_size("gy"))
    pairs = [
        (z * nx + x, ((z + dz) % nz) * nx + (x + dx) % nx) for z in range(nz) for x in range(nx)
    ]
    return lax.ppermute(value, "gy", pairs)


def z_order(nz):
    return sorted(range(nz), key=lambda k: (min(k, nz - k), k))


def start_z(value):
    nz, nx = grid_of(lax.axis_size("gy"))
    found = {(0, 0): value}
    for k in z_order(nz)[1:]:
        found[k, 0] = moved(value, -k, 0)
    return found


def swap_x(found, half):
    nz, nx = grid_of(lax.axis_size("gy"))
    found = dict(found)
    for k in z_order(nz)[half * nz // 2 : (half + 1) * nz // 2]:
        for p in range(1, nx):
            found[k, p] = moved(found[k, 0], 0, -p)
    return found


def joined_blocks(found):
    nz, nx = grid_of(lax.axis_size("gy"))
    return jnp.concatenate([found[k, p] for k in z_order(nz) for p in range(nx)], axis=0)


def start_gather(value):
    nz, nx = grid_of(lax.axis_size("gy"))
    found = start_z(value)
    for p in range(1, nx):
        found[0, p] = moved(value, 0, -p)
    return found


def finish_gather(found):
    nz, nx = grid_of(lax.axis_size("gy"))
    found = dict(found)
    for k in z_order(nz)[1:]:
        for p in range(1, nx):
            found[k, p] = moved(found[k, 0], 0, -p)
    return joined_blocks(found)


def relative_gather(value):
    return finish_gather(start_gather(value))


def relative_owner():
    nz, nx = grid_of(lax.axis_size("gy"))
    me = lax.axis_index("gy")
    z, x = me // nx, me % nx
    return jnp.stack([((z + k) % nz) * nx + (x + p) % nx for k in z_order(nz) for p in range(nx)])


def relative_scatter(term):
    nz, nx = grid_of(lax.axis_size("gy"))
    order = z_order(nz)
    rows = term.shape[0] // (nz * nx)
    arrived, own = [], None
    for at in reversed(range(nz)):
        k = order[at]
        first = at * nx * rows
        total = term[first : first + rows].astype(F32)
        for p in range(1, nx):
            total = total + moved(term[first + p * rows : first + (p + 1) * rows], 0, p).astype(F32)
        if k:
            arrived.append(moved(total.astype(BF), k, 0))
        else:
            own = total
    for value in arrived:
        own = own + value.astype(F32)
    return own


def absolute_rows(value):
    nz, nx = grid_of(lax.axis_size("gy"))
    me = lax.axis_index("gy")
    z, x = me // nx, me % nx
    blocks = value.reshape(nz, nx, value.shape[0] // (nz * nx), value.shape[1])
    order = z_order(nz)
    turn = [order.index(k) for k in range(nz)]
    blocks = jnp.stack([blocks[at] for at in turn + turn])
    blocks = lax.dynamic_slice_in_dim(blocks, (nz - z) % nz, nz, 0)
    blocks = lax.dynamic_slice_in_dim(jnp.concatenate([blocks] * 2, 1), (nx - x) % nx, nx, 1)
    return blocks.reshape(value.shape)


def send_weight(weight):
    count = lax.axis_size("gx")
    found = [weight]
    for j in range(1, count // 2):
        found.append(lax.ppermute(weight, "gx", [(i, (i - 2 * j) % count) for i in range(count)]))
    return found


def pieces_of(found):
    count = lax.axis_size("gx")
    pieces = []
    for along in found:
        pieces += [along, lax.ppermute(along, "gx", [(i, i ^ 1) for i in range(count)])]
    return pieces


def piece_spots():
    count = lax.axis_size("gx")
    me = lax.axis_index("gx")
    spots = []
    for j in range(count // 2):
        along = (me + 2 * j) % count
        spots += [along, along ^ 1]
    return jnp.stack(spots).astype(jnp.int32)


def load_pieces(spots, pieces, whole, sems):
    copies = []
    for at, piece in enumerate(pieces):
        rows = piece.shape[0]
        first = pl.multiple_of(spots[at] * rows, 16) if len(pieces) > 1 else 0
        copy = pltpu.make_async_copy(piece, whole.at[pl.ds(first, rows)], sems.at[at])
        copy.start()
        copies.append(copy)
    return copies


def product_kernel(norm, counts, tile, spots, rows_ref, gain_ref, *refs):
    pieces, (out_ref, whole, sems) = refs[: counts[0]], refs[counts[0] :]
    for copy in load_pieces(spots, pieces, whole, sems):
        copy.wait()

    @pl.loop(0, rows_ref.shape[0] // tile)
    def _(step):
        span = pl.ds(pl.multiple_of(step * tile, 16), tile)
        normed = norm(rows_ref[span, :], gain_ref[...]).astype(BF)
        out_ref[span, :] = jnp.dot(normed, whole[...], preferred_element_type=F32).astype(BF)


def block_kernel(norm, counts, tile, spots, rows_ref, gain_ref, *refs):
    ups, downs = refs[: counts[0]], refs[counts[0] : sum(counts)]
    out_ref, up, down, up_sems, down_sems = refs[sum(counts) :]
    up_copies = load_pieces(spots, ups, up, up_sems)
    down_copies = load_pieces(spots, downs, down, down_sems)
    for copy in up_copies + down_copies:
        copy.wait()

    @pl.loop(0, rows_ref.shape[0] // tile)
    def _(step):
        span = pl.ds(pl.multiple_of(step * tile, 16), tile)
        normed = norm(rows_ref[span, :], gain_ref[...]).astype(BF)
        raised = jnp.dot(normed, up[...], preferred_element_type=F32)
        hidden = (0.5 * raised * (1.0 + lax.erf(raised * math.sqrt(0.5)))).astype(BF)
        out_ref[span, :] = lax.dot_general(
            hidden, down[...], (((1,), (1,)), ((), ())), preferred_element_type=F32
        ).astype(BF)


def tile_of(rows):
    return max(size for size in range(16, 321, 16) if rows % size == 0)


def pieces_call(kernel, norm, rows, gain, groups, columns, flops):
    counts = [len(group) for group in groups]
    wholes = [(group[0].shape[0] * len(group), group[0].shape[1]) for group in groups]
    spec = pl.BlockSpec(memory_space=pltpu.VMEM)
    return pl.pallas_call(
        functools.partial(kernel, norm, counts, tile_of(rows.shape[0])),
        out_shape=jax.ShapeDtypeStruct((rows.shape[0], columns), BF),
        grid_spec=pltpu.PrefetchScalarGridSpec(
            num_scalar_prefetch=1,
            grid=(),
            in_specs=[spec, spec] + [pl.BlockSpec(memory_space=pl.ANY)] * sum(counts),
            out_specs=spec,
            scratch_shapes=[pltpu.VMEM(shape, BF) for shape in wholes]
            + [pltpu.SemaphoreType.DMA((count,)) for count in counts],
        ),
        compiler_params=pltpu.CompilerParams(vmem_limit_bytes=40 * 1024 * 1024),
        cost_estimate=pl.CostEstimate(
            flops=flops,
            bytes_accessed=sum(2 * a * b for a, b in wholes) + 4 * rows.size,
            transcendentals=0,
        ),
    )(piece_spots(), rows, gain[None, :], *[piece for group in groups for piece in group])


def product_of(norm, rows, gain, pieces):
    columns = pieces[0].shape[1]
    return pieces_call(
        product_kernel, norm, rows, gain, [pieces], columns, 2 * rows.size * columns
    )


def block_of(norm, rows, gain, ups, downs):
    flops = 4 * rows.size * ups[0].shape[1]
    return pieces_call(block_kernel, norm, rows, gain, [ups, downs], rows.shape[1], flops)


def weight_block(weight):
    return lax.all_gather(weight, "gx", axis=0, tiled=True)


def tied(first, *later):
    return lax.optimization_barrier((first, *later))


def attend(joined, allowed):
    total = joined.shape[0]
    heads_here = joined.shape[1] // (3 * HEAD_DIM)
    grouped = joined.reshape(total, heads_here, 3, HEAD_DIM)
    query = grouped[:, :, 0]
    keys = grouped[:, :, 1]
    values = grouped[:, :, 2]
    scale = 1.0 / math.sqrt(HEAD_DIM)
    scores = jnp.einsum("qhe,khe->hqk", query, keys, preferred_element_type=F32) * scale
    scores = jnp.where(allowed[None], scores, -1e30)
    top = jnp.max(scores, axis=-1, keepdims=True)
    weights = jnp.exp(scores - top)
    probs = (weights / jnp.sum(weights, axis=-1, keepdims=True)).astype(BF)
    mixed = jnp.einsum("hqk,khe->qhe", probs, values, preferred_element_type=F32)
    return mixed.astype(BF).reshape(total, heads_here * HEAD_DIM)


def out_term(hidden, weight):
    return lax.dot_general(
        hidden, weight, (((1,), (1,)), ((), ())), preferred_element_type=F32
    ).astype(BF)


def shards(
    patches,
    prompt,
    image_ids,
    positions,
    norm_gains,
    vit_qkv,
    vit_out,
    vit_up,
    vit_down,
    merge_proj,
    dec_qkv,
    dec_out,
    dec_up,
    dec_down,
):
    local, width = patches.shape
    seq_local = prompt.shape[0]
    merged_rows = image_ids.shape[1]
    owner = relative_owner()
    window_of = (
        owner[:, None] * (local // 4) + jnp.arange(local // 4, dtype=jnp.int32)[None, :]
    ).reshape(-1)
    picks = window_of[:, None] == jnp.arange(merged_rows, dtype=jnp.int32)[None, :]
    labels = jnp.repeat(jnp.sum(jnp.where(picks, image_ids[0][None, :], 0), axis=1), 4)
    spots_of = (
        owner[:, None] * seq_local + jnp.arange(seq_local, dtype=jnp.int32)[None, :]
    ).reshape(-1)
    hits = positions[0][None, :] == spots_of[:, None]

    patch_found = start_gather(patches)
    sent_qkv = send_weight(vit_qkv)
    sent_down = send_weight(vit_down)
    outs_block = weight_block(jnp.concatenate([vit_out, dec_out], axis=1))
    qkvs = pieces_of(sent_qkv)
    patch_all = finish_gather(patch_found)
    enc_qkv = product_of(layer_norm, patch_all, norm_gains[0], qkvs)
    enc_qkv, outs_block, vit_up, prompt = tied(enc_qkv, outs_block, vit_up, prompt)
    up_block = weight_block(vit_up)
    columns = vit_out.shape[1]
    out_block, dout_block = outs_block[:, :columns], outs_block[:, columns:]
    prompt_found = start_z(prompt)
    enc_mix = attend(enc_qkv, labels[:, None] == labels[None, :])
    summed = relative_scatter(out_term(enc_mix, out_block))
    enc_mid = (patches.astype(F32) + summed).astype(BF)
    enc_mid, up_block, merge_proj, sent_down = tied(enc_mid, up_block, merge_proj, sent_down)
    merge_block = weight_block(merge_proj)
    downs = pieces_of(sent_down)

    mid_all = relative_gather(enc_mid)
    mid_all, prompt_found = tied(mid_all, prompt_found)
    prompt_found = swap_x(prompt_found, 0)
    term = block_of(layer_norm, mid_all, norm_gains[1], [up_block], downs)
    enc_out = (enc_mid.astype(F32) + relative_scatter(term)).astype(BF)
    enc_out, merge_block, dec_qkv, prompt_found, dec_down = tied(
        enc_out, merge_block, dec_qkv, prompt_found, dec_down
    )
    dqkv_block = weight_block(dec_qkv)
    windows = layer_norm(enc_out, norm_gains[2]).astype(BF).reshape(local // 4, 4 * width)
    prompt_found = swap_x(prompt_found, 1)
    windows = relative_gather(windows)
    prompt_all = joined_blocks(prompt_found)
    merged = jnp.dot(windows, merge_block, preferred_element_type=F32).astype(BF)
    merged, dqkv_block, dec_up = tied(merged, dqkv_block, dec_up)
    dup_block = weight_block(dec_up)
    sent_ddown = send_weight(dec_down)
    merged = lax.dot_general(
        merged, picks.astype(BF), (((0,), (0,)), ((), ())), preferred_element_type=F32
    ).astype(BF)
    merged_all = absolute_rows(relative_gather(merged))

    placed = lax.dot_general(
        hits.astype(BF), merged_all, (((1,), (1,)), ((), ())), preferred_element_type=F32
    ).astype(BF)
    dec_all = jnp.where(jnp.any(hits, axis=1)[:, None], placed, prompt_all)
    dec_in = dec_all[:seq_local]
    dec_rows = product_of(rms_norm, dec_all, norm_gains[3], [dqkv_block])
    dec_mix = attend(dec_rows, spots_of[:, None] >= spots_of[None, :])
    summed = relative_scatter(out_term(dec_mix, dout_block))
    dec_mid = (dec_in.astype(F32) + summed).astype(BF)
    dec_mid, dup_block, sent_ddown = tied(dec_mid, dup_block, sent_ddown)
    ddowns = pieces_of(sent_ddown)

    mid_all = relative_gather(dec_mid)
    term = block_of(rms_norm, mid_all, norm_gains[4], [dup_block], ddowns)
    return (dec_mid.astype(F32) + relative_scatter(term)).astype(BF)


def solution(mesh):
    weight = P("gx", "gy")
    rows = P(("gx", "gy"), None)
    in_specs = (rows, rows, P("gx", None), P("gx", None), P()) + (weight,) * 9
    return jax.shard_map(shards, mesh=mesh, in_specs=in_specs, out_specs=rows, check_vma=False)
```

profile of v0, /device:TPU:0, one launch (start us, length us, event | category | flops | bytes accessed | tf_op | source)
XLA Modules:
  0.0 355.0 jit_solution(13113300644749114196)
XLA Ops:
  6.5 5.0 %collective-permute-start.1 = (bf16[64,1664]{1,0:T(8,128)(2,1)}, bf16[64,1664]{1,0:T(8,128)(2,1)S(1)}, u32[]{:S(2)}, u32[]{:S(2)}) collective-permute-start(bf16[64,1664]{1,0:T(8,128)(2,1)} %param.14), channel_id=1, source_target_pairs={{0,6},{1,7},{2,0},{3,1},{4,2},{5,3},{6,4},{7,5},{8,14},{9,15},{10,... | collective-permute-start | bytes 638984 | tf_op jit(solution)/shard_map/ppermute | solution.py:38
  15.6 2.0 pad_maximum_fusion
  21.5 1.8 collective-permute-done.3
  24.5 5.4 %collective-permute-done.5 = bf16[64,1664]{1,0:T(8,128)(2,1)S(1)} collective-permute-done((bf16[64,1664]{1,0:T(8,128)(2,1)}, bf16[64,1664]{1,0:T(8,128)(2,1)S(1)}, u32[]{:S(2)}, u32[]{:S(2)}) %collective-permute-start.5) | collective-permute-done | bytes 213024 | tf_op jit(solution)/shard_map/ppermute | solution.py:38
  32.7 4.0 %collective-permute-done.6 = bf16[64,1664]{1,0:T(8,128)(2,1)S(1)} collective-permute-done((bf16[64,1664]{1,0:T(8,128)(2,1)S(1)}, bf16[64,1664]{1,0:T(8,128)(2,1)S(1)}, u32[]{:S(2)}, u32[]{:S(2)}) %collective-permute-start.6) | collective-permute-done | bytes 213024 | tf_op jit(solution)/shard_map/ppermute | solution.py:38
  36.8 3.4 shard_map.136
  49.7 3.3 collective-permute-done.11
  53.0 4.6 %collective-permute-done.13 = bf16[64,1664]{1,0:T(8,128)(2,1)S(1)} collective-permute-done((bf16[64,1664]{1,0:T(8,128)(2,1)S(1)}, bf16[64,1664]{1,0:T(8,128)(2,1)S(1)}, u32[]{:S(2)}, u32[]{:S(2)}) %collective-permute-start.13) | collective-permute-done | bytes 213024 | tf_op jit(solution)/shard_map/ppermute | solution.py:38
  57.6 4.6 %collective-permute-done.15 = bf16[64,1664]{1,0:T(8,128)(2,1)S(1)} collective-permute-done((bf16[64,1664]{1,0:T(8,128)(2,1)S(1)}, bf16[64,1664]{1,0:T(8,128)(2,1)S(1)}, u32[]{:S(2)}, u32[]{:S(2)}) %collective-permute-start.15) | collective-permute-done | bytes 213024 | tf_op jit(solution)/shard_map/ppermute | solution.py:38
  63.5 4.6 %collective-permute-start.14 = (bf16[64,1664]{1,0:T(8,128)(2,1)S(1)}, bf16[64,1664]{1,0:T(8,128)(2,1)S(1)}, u32[]{:S(2)}, u32[]{:S(2)}) collective-permute-start(bf16[64,1664]{1,0:T(8,128)(2,1)S(1)} %get-tuple-element.94), channel_id=1, source_target_pairs={{0,6},{1,7},{2,0},{3,1},{4,2},{5,3},{6,4},{7,5},{8,14},{9,15},{10,... | collective-permute-start | bytes 638984 | tf_op jit(solution)/shard_map/ppermute | solution.py:38
  68.1 3.8 %collective-permute-start.25 = (bf16[80,1664]{1,0:T(8,128)(2,1)S(1)}, bf16[80,1664]{1,0:T(8,128)(2,1)S(1)}, u32[]{:S(2)}, u32[]{:S(2)}) collective-permute-start(bf16[80,1664]{1,0:T(8,128)(2,1)S(1)} %copy-done.15), channel_id=1, source_target_pairs={{0,6},{1,7},{2,0},{3,1},{4,2},{5,3},{6,4},{7,5},{8,14},{9,15},{10,... | collective-permute-start | bytes 798728 | tf_op jit(solution)/shard_map/ppermute | solution.py:38
  71.9 5.9 %collective-permute-done.12 = bf16[64,1664]{1,0:T(8,128)(2,1)S(1)} collective-permute-done((bf16[64,1664]{1,0:T(8,128)(2,1)S(1)}, bf16[64,1664]{1,0:T(8,128)(2,1)S(1)}, u32[]{:S(2)}, u32[]{:S(2)}) %collective-permute-start.12) | collective-permute-done | bytes 213024 | tf_op jit(solution)/shard_map/ppermute | solution.py:38
  77.8 5.2 %collective-permute-done.16 = bf16[64,1664]{1,0:T(8,128)(2,1)S(1)} collective-permute-done((bf16[64,1664]{1,0:T(8,128)(2,1)S(1)}, bf16[64,1664]{1,0:T(8,128)(2,1)S(1)}, u32[]{:S(2)}, u32[]{:S(2)}) %collective-permute-start.16) | collective-permute-done | bytes 213024 | tf_op jit(solution)/shard_map/ppermute | solution.py:38
  87.5 3.4 collective-permute-start.19
  93.4 7.2 %collective-permute-done.19 = bf16[64,1664]{1,0:T(8,128)(2,1)S(1)} collective-permute-done((bf16[64,1664]{1,0:T(8,128)(2,1)S(1)}, bf16[64,1664]{1,0:T(8,128)(2,1)S(1)}, u32[]{:S(2)}, u32[]{:S(2)}) %collective-permute-start.19) | collective-permute-done | bytes 213024 | tf_op jit(solution)/shard_map/ppermute | solution.py:38
  102.3 5.1 %collective-permute-done.20 = bf16[64,1664]{1,0:T(8,128)(2,1)S(1)} collective-permute-done((bf16[64,1664]{1,0:T(8,128)(2,1)S(1)}, bf16[64,1664]{1,0:T(8,128)(2,1)S(1)}, u32[]{:S(2)}, u32[]{:S(2)}) %collective-permute-start.20) | collective-permute-done | bytes 213024 | tf_op jit(solution)/shard_map/ppermute | solution.py:38
  107.4 4.0 %collective-permute-done.23 = bf16[64,1664]{1,0:T(8,128)(2,1)S(1)} collective-permute-done((bf16[64,1664]{1,0:T(8,128)(2,1)S(1)}, bf16[64,1664]{1,0:T(8,128)(2,1)S(1)}, u32[]{:S(2)}, u32[]{:S(2)}) %collective-permute-start.23) | collective-permute-done | bytes 213024 | tf_op jit(solution)/shard_map/ppermute | solution.py:38
  111.4 3.1 collective-permute-start.26
  114.5 2.0 collective-permute-start.24
  116.5 3.8 %collective-permute-done.24 = bf16[64,1664]{1,0:T(8,128)(2,1)S(1)} collective-permute-done((bf16[64,1664]{1,0:T(8,128)(2,1)S(1)}, bf16[64,1664]{1,0:T(8,128)(2,1)S(1)}, u32[]{:S(2)}, u32[]{:S(2)}) %collective-permute-start.24) | collective-permute-done | bytes 213024 | tf_op jit(solution)/shard_map/ppermute | solution.py:38
  120.3 6.3 %collective-permute-start.27 = (bf16[80,1664]{1,0:T(8,128)(2,1)S(1)}, bf16[80,1664]{1,0:T(8,128)(2,1)S(1)}, u32[]{:S(2)}, u32[]{:S(2)}) collective-permute-start(bf16[80,1664]{1,0:T(8,128)(2,1)S(1)} %copy-done.15), channel_id=1, source_target_pairs={{0,2},{1,3},{2,4},{3,5},{4,6},{5,7},{6,0},{7,1},{8,10},{9,11},{10,... | collective-permute-start | bytes 798728 | tf_op jit(solution)/shard_map/ppermute | solution.py:38
  126.7 4.5 %collective-permute-done.26 = bf16[80,1664]{1,0:T(8,128)(2,1)S(1)} collective-permute-done((bf16[80,1664]{1,0:T(8,128)(2,1)S(1)}, bf16[80,1664]{1,0:T(8,128)(2,1)S(1)}, u32[]{:S(2)}, u32[]{:S(2)}) %collective-permute-start.26) | collective-permute-done | bytes 266272 | tf_op jit(solution)/shard_map/ppermute | solution.py:38
  133.5 6.7 %shard_map.137 = bf16[512,1664]{1,0:T(8,128)(2,1)S(1)} custom-call(s32[4]{0:T(128)S(1)} %pad_add_fusion.spots, bf16[512,1664]{1,0:T(8,128)(2,1)S(1)} %constant_dynamic-update-slice_fusion.8.rows_ref, f32[1,1664]{1,0:T(1,128)S(1)} %get-tuple-element.97.gain_ref, bf16[1664,1024]{1,0:T(8,128)(2,1)S(1)} %copy-done.2, bf16[416,1024]{1,0:T(8,128)(2,1)S(1)} %copy-done.5, ...), custom_call_target="tpu_custom_call" | custom-call | flops 3489660928 | bytes 10223616 | tf_op jit(solution)/shard_map/pallas_call | solution.py:204
  145.6 4.0 %collective-permute-done.31 = bf16[64,1664]{1,0:T(8,128)(2,1)} collective-permute-done((bf16[64,1664]{1,0:T(8,128)(2,1)}, bf16[64,1664]{1,0:T(8,128)(2,1)}, u32[]{:S(2)}, u32[]{:S(2)}) %collective-permute-start.31) | collective-permute-done | bytes 213024 | tf_op jit(solution)/shard_map/ppermute | solution.py:38
  149.6 4.6 %collective-permute-done.33 = bf16[64,1664]{1,0:T(8,128)(2,1)} collective-permute-done((bf16[64,1664]{1,0:T(8,128)(2,1)}, bf16[64,1664]{1,0:T(8,128)(2,1)}, u32[]{:S(2)}, u32[]{:S(2)}) %collective-permute-start.33) | collective-permute-done | bytes 213024 | tf_op jit(solution)/shard_map/ppermute | solution.py:38
  154.1 4.6 %collective-permute-done.35 = bf16[64,1664]{1,0:T(8,128)(2,1)} collective-permute-done((bf16[64,1664]{1,0:T(8,128)(2,1)}, bf16[64,1664]{1,0:T(8,128)(2,1)}, u32[]{:S(2)}, u32[]{:S(2)}) %collective-permute-start.35) | collective-permute-done | bytes 213024 | tf_op jit(solution)/shard_map/ppermute | solution.py:38
  160.3 1.8 collective-permute-start.36
  165.3 7.9 %collective-permute-done.32 = bf16[64,1664]{1,0:T(8,128)(2,1)S(1)} collective-permute-done((bf16[64,1664]{1,0:T(8,128)(2,1)S(1)}, bf16[64,1664]{1,0:T(8,128)(2,1)S(1)}, u32[]{:S(2)}, u32[]{:S(2)}) %collective-permute-start.32) | collective-permute-done | bytes 213024 | tf_op jit(solution)/shard_map/ppermute | solution.py:38
  174.8 3.6 %collective-permute-start.40 = (bf16[16,6656]{1,0:T(8,128)(2,1)S(1)}, bf16[16,6656]{1,0:T(8,128)(2,1)}, u32[]{:S(2)}, u32[]{:S(2)}) collective-permute-start(bf16[16,6656]{1,0:T(8,128)(2,1)S(1)} %reshape.275), channel_id=1, source_target_pairs={{0,6},{1,7},{2,0},{3,1},{4,2},{5,3},{6,4},{7,5},{8,14},{9,15},{10,... | collective-permute-start | bytes 638984 | tf_op jit(solution)/shard_map/ppermute | solution.py:38
  178.4 3.4 collective-permute-start.44
  181.9 2.1 collective-permute-start.53
  186.2 1.9 collective-permute-start.41
  190.6 3.8 %collective-permute-done.44 = bf16[16,6656]{1,0:T(8,128)(2,1)} collective-permute-done((bf16[16,6656]{1,0:T(8,128)(2,1)S(1)}, bf16[16,6656]{1,0:T(8,128)(2,1)}, u32[]{:S(2)}, u32[]{:S(2)}) %collective-permute-start.44) | collective-permute-done | bytes 213024 | tf_op jit(solution)/shard_map/ppermute | solution.py:38
  194.3 1.7 collective-permute-start.45
  196.1 5.0 %collective-permute-done.41 = bf16[16,6656]{1,0:T(8,128)(2,1)S(1)} collective-permute-done((bf16[16,6656]{1,0:T(8,128)(2,1)}, bf16[16,6656]{1,0:T(8,128)(2,1)S(1)}, u32[]{:S(2)}, u32[]{:S(2)}) %collective-permute-start.41) | collective-permute-done | bytes 213024 | tf_op jit(solution)/shard_map/ppermute | solution.py:38
  206.9 1.9 collective-permute-start.47
  208.8 1.7 collective-permute-start.46
  213.5 3.3 collective-permute-done.51
  217.1 1.7 collective-permute-start.50
  218.9 2.6 collective-permute-done.50
  221.9 2.5 fusion.2.rows_ref
  224.5 3.3 shard_map.138
  229.3 4.2 %fusion.44 = (f32[2,640]{1,0:T(2,128)S(1)}, f32[2,640,640]{1,2,0:T(8,128)}) fusion(pred[640,640]{0,1:T(8,128)(4,1)} %broadcast_compare_fusion, bf16[640,2,3,104]{0,3,2,1:T(8,128)(2,1)} %bitcast.112), kind=kOutput, calls=%fused_computation.146 | convolution fusion | flops 173671040 | bytes 4224000 | tf_op jit(solution)/shard_map/sub | solution.py:255
  233.5 2.6 fusion.9
  241.5 5.3 %collective-permute-done.56 = bf16[80,1664]{1,0:T(8,128)(2,1)S(1)} collective-permute-done((bf16[80,1664]{1,0:T(8,128)(2,1)S(1)}, bf16[80,1664]{1,0:T(8,128)(2,1)S(1)}, u32[]{:S(2)}, u32[]{:S(2)}) %collective-permute-start.56) | collective-permute-done | bytes 266272 | tf_op jit(solution)/shard_map/ppermute | solution.py:38
  246.8 5.7 %collective-permute-done.58 = bf16[80,1664]{1,0:T(8,128)(2,1)S(1)} collective-permute-done((bf16[80,1664]{1,0:T(8,128)(2,1)S(1)}, bf16[80,1664]{1,0:T(8,128)(2,1)S(1)}, u32[]{:S(2)}, u32[]{:S(2)}) %collective-permute-start.58) | collective-permute-done | bytes 266272 | tf_op jit(solution)/shard_map/ppermute | solution.py:38
  252.5 3.8 %collective-permute-done.60 = bf16[80,1664]{1,0:T(8,128)(2,1)S(1)} collective-permute-done((bf16[80,1664]{1,0:T(8,128)(2,1)S(1)}, bf16[80,1664]{1,0:T(8,128)(2,1)S(1)}, u32[]{:S(2)}, u32[]{:S(2)}) %collective-permute-start.60) | collective-permute-done | bytes 266272 | tf_op jit(solution)/shard_map/ppermute | solution.py:38
  256.8 2.6 collective-permute-start.59
  259.4 13.0 %collective-permute-done.57 = bf16[80,1664]{1,0:T(8,128)(2,1)S(1)} collective-permute-done((bf16[80,1664]{1,0:T(8,128)(2,1)S(1)}, bf16[80,1664]{1,0:T(8,128)(2,1)S(1)}, u32[]{:S(2)}, u32[]{:S(2)}) %collective-permute-start.57) | collective-permute-done | bytes 266272 | tf_op jit(solution)/shard_map/ppermute | solution.py:38
  273.9 4.0 %collective-permute-start.64 = (bf16[80,1664]{1,0:T(8,128)(2,1)S(1)}, bf16[80,1664]{1,0:T(8,128)(2,1)S(1)}, u32[]{:S(2)}, u32[]{:S(2)}) collective-permute-start(bf16[80,1664]{1,0:T(8,128)(2,1)S(1)} %add_convert_fusion.4), channel_id=1, source_target_pairs={{0,6},{1,7},{2,0},{3,1},{4,2},{5,3},{6,4},{7,5},{8,14},{9,15},{10,... | collective-permute-start | bytes 798728 | tf_op jit(solution)/shard_map/ppermute | solution.py:38
  277.9 3.9 %collective-permute-start.68 = (bf16[80,1664]{1,0:T(8,128)(2,1)S(1)}, bf16[80,1664]{1,0:T(8,128)(2,1)S(1)}, u32[]{:S(2)}, u32[]{:S(2)}) collective-permute-start(bf16[80,1664]{1,0:T(8,128)(2,1)S(1)} %add_convert_fusion.4), channel_id=1, source_target_pairs={{0,4},{1,5},{2,6},{3,7},{4,0},{5,1},{6,2},{7,3},{8,12},{9,13},{10,... | collective-permute-start | bytes 798728 | tf_op jit(solution)/shard_map/ppermute | solution.py:38
  282.5 5.1 %collective-permute-done.64 = bf16[80,1664]{1,0:T(8,128)(2,1)S(1)} collective-permute-done((bf16[80,1664]{1,0:T(8,128)(2,1)S(1)}, bf16[80,1664]{1,0:T(8,128)(2,1)S(1)}, u32[]{:S(2)}, u32[]{:S(2)}) %collective-permute-start.64) | collective-permute-done | bytes 266272 | tf_op jit(solution)/shard_map/ppermute | solution.py:38
  288.9 3.4 collective-permute-done.66
  292.3 1.7 collective-permute-start.67
  294.0 5.7 %collective-permute-done.68 = bf16[80,1664]{1,0:T(8,128)(2,1)S(1)} collective-permute-done((bf16[80,1664]{1,0:T(8,128)(2,1)S(1)}, bf16[80,1664]{1,0:T(8,128)(2,1)S(1)}, u32[]{:S(2)}, u32[]{:S(2)}) %collective-permute-start.68) | collective-permute-done | bytes 266272 | tf_op jit(solution)/shard_map/ppermute | solution.py:38
  299.7 1.7 collective-permute-start.69
  301.6 4.5 %collective-permute-done.69 = bf16[80,1664]{1,0:T(8,128)(2,1)S(1)} collective-permute-done((bf16[80,1664]{1,0:T(8,128)(2,1)S(1)}, bf16[80,1664]{1,0:T(8,128)(2,1)S(1)}, u32[]{:S(2)}, u32[]{:S(2)}) %collective-permute-start.69) | collective-permute-done | bytes 266272 | tf_op jit(solution)/shard_map/ppermute | solution.py:38
  306.1 8.1 %shard_map.139 = bf16[640,1664]{1,0:T(8,128)(2,1)S(1)} custom-call(s32[4]{0:T(128)S(1)} %pad_add_fusion.spots, bf16[640,1664]{1,0:T(8,128)(2,1)S(1)} %constant_dynamic-update-slice_fusion.40.rows_ref, f32[1,1664]{1,0:T(1,128)S(1)} %get-tuple-element.95.gain_ref, bf16[1664,1024]{1,0:T(8,128)(2,1)S(1)} %copy-done.3, bf16[416,1024]{1,0:T(8,128)(2,1)S(1)} %copy-done.6, ...), custom_call_target="tpu_custom_call" | custom-call | flops 4362076160 | bytes 11075584 | tf_op jit(solution)/shard_map/pallas_call | solution.py:204
  314.3 1.7 collective-permute-start.73
  316.4 1.7 collective-permute-start.77
  318.4 5.3 %collective-permute-done.73 = bf16[80,1664]{1,0:T(8,128)(2,1)S(1)} collective-permute-done((bf16[80,1664]{1,0:T(8,128)(2,1)S(1)}, bf16[80,1664]{1,0:T(8,128)(2,1)S(1)}, u32[]{:S(2)}, u32[]{:S(2)}) %collective-permute-start.73) | collective-permute-done | bytes 266272 | tf_op jit(solution)/shard_map/ppermute | solution.py:38
  323.7 5.7 %collective-permute-done.75 = bf16[80,1664]{1,0:T(8,128)(2,1)S(1)} collective-permute-done((bf16[80,1664]{1,0:T(8,128)(2,1)S(1)}, bf16[80,1664]{1,0:T(8,128)(2,1)S(1)}, u32[]{:S(2)}, u32[]{:S(2)}) %collective-permute-start.75) | collective-permute-done | bytes 266272 | tf_op jit(solution)/shard_map/ppermute | solution.py:38
  329.4 2.9 collective-permute-done.77
  335.1 12.4 %collective-permute-done.74 = bf16[80,1664]{1,0:T(8,128)(2,1)S(1)} collective-permute-done((bf16[80,1664]{1,0:T(8,128)(2,1)S(1)}, bf16[80,1664]{1,0:T(8,128)(2,1)S(1)}, u32[]{:S(2)}, u32[]{:S(2)}) %collective-permute-start.74) | collective-permute-done | bytes 266272 | tf_op jit(solution)/shard_map/ppermute | solution.py:38
  (247 shorter events, 75.0 us)
Async XLA Ops:
  6.5 33.6 %all-gather.6.cloned.1.call-start = ((), (), s32[]{:S(2)}) async-start(), calls=%async_computation | async-start | bytes 2129920 | tf_op jit(solution)/shard_map/all_gather | solution.py:237
  6.5 13.3 %collective-permute-start.1 = (bf16[64,1664]{1,0:T(8,128)(2,1)}, bf16[64,1664]{1,0:T(8,128)(2,1)S(1)}, u32[]{:S(2)}, u32[]{:S(2)}) collective-permute-start(bf16[64,1664]{1,0:T(8,128)(2,1)} %param.14), channel_id=1, source_target_pairs={{0,6},{1,7},{2,0},{3,1},{4,2},{5,3},{6,4},{7,5},{8,14},{9,15},{10,... | collective-permute-start | bytes 638984 | tf_op jit(solution)/shard_map/ppermute | solution.py:38
  13.1 10.3 %collective-permute-start.3 = (bf16[64,1664]{1,0:T(8,128)(2,1)}, bf16[64,1664]{1,0:T(8,128)(2,1)S(1)}, u32[]{:S(2)}, u32[]{:S(2)}) collective-permute-start(bf16[64,1664]{1,0:T(8,128)(2,1)} %param.14), channel_id=1, source_target_pairs={{0,2},{1,3},{2,4},{3,5},{4,6},{5,7},{6,0},{7,1},{8,10},{9,11},{10,... | collective-permute-start | bytes 638984 | tf_op jit(solution)/shard_map/ppermute | solution.py:38
  13.1 16.8 %collective-permute-start.5 = (bf16[64,1664]{1,0:T(8,128)(2,1)}, bf16[64,1664]{1,0:T(8,128)(2,1)S(1)}, u32[]{:S(2)}, u32[]{:S(2)}) collective-permute-start(bf16[64,1664]{1,0:T(8,128)(2,1)} %param.14), channel_id=1, source_target_pairs={{0,4},{1,5},{2,6},{3,7},{4,0},{5,1},{6,2},{7,3},{8,12},{9,13},{10,... | collective-permute-start | bytes 638984 | tf_op jit(solution)/shard_map/ppermute | solution.py:38
  14.1 17.4 %collective-permute-start.8 = (bf16[416,624]{1,0:T(8,128)(2,1)}, bf16[416,624]{1,0:T(8,128)(2,1)S(1)}, u32[]{:S(2)}, u32[]{:S(2)}) collective-permute-start(bf16[416,624]{1,0:T(8,128)(2,1)} %refs_0_.1), channel_id=1, source_target_pairs={{0,16},{8,24},{16,0},{24,8},{1,17},{9,25},{17,1},{25,9},{2,18},{10... | collective-permute-start | bytes 1557512 | tf_op jit(solution)/shard_map/ppermute | solution.py:132
  17.6 68.3 %all-gather.8.cloned.1.call-start = ((), (), s32[]{:S(2)}) async-start(), calls=%async_computation.1 | async-start | bytes 4259840 | tf_op jit(solution)/shard_map/all_gather | solution.py:237
  19.8 16.9 %collective-permute-start.7 = (bf16[416,624]{1,0:T(8,128)(2,1)}, bf16[416,624]{1,0:T(8,128)(2,1)S(1)}, u32[]{:S(2)}, u32[]{:S(2)}) collective-permute-start(bf16[416,624]{1,0:T(8,128)(2,1)} %refs_0_.1), channel_id=1, source_target_pairs={{0,8},{8,0},{16,24},{24,16},{1,9},{9,1},{17,25},{25,17},{2,10},{10... | collective-permute-start | bytes 1557512 | tf_op jit(solution)/shard_map/ppermute | solution.py:140
  19.9 11.5 %collective-permute-start.2 = (bf16[64,1664]{1,0:T(8,128)(2,1)S(1)}, bf16[64,1664]{1,0:T(8,128)(2,1)S(1)}, u32[]{:S(2)}, u32[]{:S(2)}) collective-permute-start(bf16[64,1664]{1,0:T(8,128)(2,1)S(1)} %collective-permute-done.1), channel_id=1, source_target_pairs={{0,1},{1,0},{2,3},{3,2},{4,5},{5,4},{6,7},{7,6},{8,9},{9,8},{10,11... | collective-permute-start | bytes 638984 | tf_op jit(solution)/shard_map/ppermute | solution.py:38
  40.2 133.2 %all-gather.10.cloned.1.call-start = ((), (), s32[]{:S(2)}) async-start(), calls=%async_computation.2 | async-start | bytes 3461120 | tf_op jit(solution)/shard_map/all_gather | solution.py:237
  45.7 11.8 %collective-permute-start.13 = (bf16[64,1664]{1,0:T(8,128)(2,1)S(1)}, bf16[64,1664]{1,0:T(8,128)(2,1)S(1)}, u32[]{:S(2)}, u32[]{:S(2)}) collective-permute-start(bf16[64,1664]{1,0:T(8,128)(2,1)S(1)} %get-tuple-element.90), channel_id=1, source_target_pairs={{0,1},{1,0},{2,3},{3,2},{4,5},{5,4},{6,7},{7,6},{8,9},{9,8},{10,11... | collective-permute-start | bytes 638984 | tf_op jit(solution)/shard_map/ppermute | solution.py:38
  46.8 15.3 %collective-permute-start.15 = (bf16[64,1664]{1,0:T(8,128)(2,1)S(1)}, bf16[64,1664]{1,0:T(8,128)(2,1)S(1)}, u32[]{:S(2)}, u32[]{:S(2)}) collective-permute-start(bf16[64,1664]{1,0:T(8,128)(2,1)S(1)} %get-tuple-element.89), channel_id=1, source_target_pairs={{0,1},{1,0},{2,3},{3,2},{4,5},{5,4},{6,7},{7,6},{8,9},{9,8},{10,11... | collective-permute-start | bytes 638984 | tf_op jit(solution)/shard_map/ppermute | solution.py:38
  47.8 36.5 %collective-permute-start.17 = (bf16[416,1024]{1,0:T(8,128)(2,1)S(1)}, bf16[416,1024]{1,0:T(8,128)(2,1)S(1)}, u32[]{:S(2)}, u32[]{:S(2)}) collective-permute-start(bf16[416,1024]{1,0:T(8,128)(2,1)S(1)} %copy-done.4), channel_id=1, source_target_pairs={{0,16},{8,24},{16,0},{24,8},{1,17},{9,25},{17,1},{25,9},{2,18},{10... | collective-permute-start | bytes 2555912 | tf_op jit(solution)/shard_map/ppermute | solution.py:132
  49.3 18.8 %collective-permute-start.10 = (bf16[64,1664]{1,0:T(8,128)(2,1)S(1)}, bf16[64,1664]{1,0:T(8,128)(2,1)S(1)}, u32[]{:S(2)}, u32[]{:S(2)}) collective-permute-start(bf16[64,1664]{1,0:T(8,128)(2,1)S(1)} %get-tuple-element.88), channel_id=1, source_target_pairs={{0,1},{1,0},{2,3},{3,2},{4,5},{5,4},{6,7},{7,6},{8,9},{9,8},{10,11... | collective-permute-start | bytes 638984 | tf_op jit(solution)/shard_map/ppermute | solution.py:38
  62.3 15.5 %collective-permute-start.12 = (bf16[64,1664]{1,0:T(8,128)(2,1)S(1)}, bf16[64,1664]{1,0:T(8,128)(2,1)S(1)}, u32[]{:S(2)}, u32[]{:S(2)}) collective-permute-start(bf16[64,1664]{1,0:T(8,128)(2,1)S(1)} %get-tuple-element.92), channel_id=1, source_target_pairs={{0,4},{1,5},{2,6},{3,7},{4,0},{5,1},{6,2},{7,3},{8,12},{9,13},{10,... | collective-permute-start | bytes 638984 | tf_op jit(solution)/shard_map/ppermute | solution.py:38
  63.5 14.3 %collective-permute-start.14 = (bf16[64,1664]{1,0:T(8,128)(2,1)S(1)}, bf16[64,1664]{1,0:T(8,128)(2,1)S(1)}, u32[]{:S(2)}, u32[]{:S(2)}) collective-permute-start(bf16[64,1664]{1,0:T(8,128)(2,1)S(1)} %get-tuple-element.94), channel_id=1, source_target_pairs={{0,6},{1,7},{2,0},{3,1},{4,2},{5,3},{6,4},{7,5},{8,14},{9,15},{10,... | collective-permute-start | bytes 638984 | tf_op jit(solution)/shard_map/ppermute | solution.py:38
  68.1 14.9 %collective-permute-start.16 = (bf16[64,1664]{1,0:T(8,128)(2,1)S(1)}, bf16[64,1664]{1,0:T(8,128)(2,1)S(1)}, u32[]{:S(2)}, u32[]{:S(2)}) collective-permute-start(bf16[64,1664]{1,0:T(8,128)(2,1)S(1)} %get-tuple-element.93), channel_id=1, source_target_pairs={{0,2},{1,3},{2,4},{3,5},{4,6},{5,7},{6,0},{7,1},{8,10},{9,11},{10,... | collective-permute-start | bytes 638984 | tf_op jit(solution)/shard_map/ppermute | solution.py:38
  68.1 58.6 %collective-permute-start.25 = (bf16[80,1664]{1,0:T(8,128)(2,1)S(1)}, bf16[80,1664]{1,0:T(8,128)(2,1)S(1)}, u32[]{:S(2)}, u32[]{:S(2)}) collective-permute-start(bf16[80,1664]{1,0:T(8,128)(2,1)S(1)} %copy-done.15), channel_id=1, source_target_pairs={{0,6},{1,7},{2,0},{3,1},{4,2},{5,3},{6,4},{7,5},{8,14},{9,15},{10,... | collective-permute-start | bytes 798728 | tf_op jit(solution)/shard_map/ppermute | solution.py:38
  87.5 13.0 %collective-permute-start.19 = (bf16[64,1664]{1,0:T(8,128)(2,1)S(1)}, bf16[64,1664]{1,0:T(8,128)(2,1)S(1)}, u32[]{:S(2)}, u32[]{:S(2)}) collective-permute-start(bf16[64,1664]{1,0:T(8,128)(2,1)S(1)} %add_convert_fusion.12), channel_id=1, source_target_pairs={{0,6},{1,7},{2,0},{3,1},{4,2},{5,3},{6,4},{7,5},{8,14},{9,15},{10,... | collective-permute-start | bytes 638984 | tf_op jit(solution)/shard_map/ppermute | solution.py:38
  91.0 11.3 %collective-permute-start.21 = (bf16[64,1664]{1,0:T(8,128)(2,1)S(1)}, bf16[64,1664]{1,0:T(8,128)(2,1)S(1)}, u32[]{:S(2)}, u32[]{:S(2)}) collective-permute-start(bf16[64,1664]{1,0:T(8,128)(2,1)S(1)} %add_convert_fusion.12), channel_id=1, source_target_pairs={{0,2},{1,3},{2,4},{3,5},{4,6},{5,7},{6,0},{7,1},{8,10},{9,11},{10,... | collective-permute-start | bytes 638984 | tf_op jit(solution)/shard_map/ppermute | solution.py:38
  91.2 20.2 %collective-permute-start.23 = (bf16[64,1664]{1,0:T(8,128)(2,1)S(1)}, bf16[64,1664]{1,0:T(8,128)(2,1)S(1)}, u32[]{:S(2)}, u32[]{:S(2)}) collective-permute-start(bf16[64,1664]{1,0:T(8,128)(2,1)S(1)} %add_convert_fusion.12), channel_id=1, source_target_pairs={{0,4},{1,5},{2,6},{3,7},{4,0},{5,1},{6,2},{7,3},{8,12},{9,13},{10,... | collective-permute-start | bytes 638984 | tf_op jit(solution)/shard_map/ppermute | solution.py:38
  92.7 114.0 %all-gather.12.cloned.1.call-start = ((), (), s32[]{:S(2)}) async-start(), calls=%async_computation.3 | async-start | bytes 2662400 | tf_op jit(solution)/shard_map/all_gather | solution.py:237
  93.4 37.8 %collective-permute-start.28 = (bf16[416,1024]{1,0:T(8,128)(2,1)S(1)}, bf16[416,1024]{1,0:T(8,128)(2,1)S(1)}, u32[]{:S(2)}, u32[]{:S(2)}) collective-permute-start(bf16[416,1024]{1,0:T(8,128)(2,1)S(1)} %copy-done.4), channel_id=1, source_target_pairs={{0,8},{8,0},{16,24},{24,16},{1,9},{9,1},{17,25},{25,17},{2,10},{10... | collective-permute-start | bytes 2555912 | tf_op jit(solution)/shard_map/ppermute | solution.py:140
  102.2 28.9 %collective-permute-start.29 = (bf16[416,1024]{1,0:T(8,128)(2,1)S(1)}, bf16[416,1024]{1,0:T(8,128)(2,1)S(1)}, u32[]{:S(2)}, u32[]{:S(2)}) collective-permute-start(bf16[416,1024]{1,0:T(8,128)(2,1)S(1)} %collective-permute-done.17.refs_3_), channel_id=1, source_target_pairs={{0,8},{8,0},{16,24},{24,16},{1,9},{9,1},{17,25},{25,17},{2,10},{10... | collective-permute-start | bytes 2555912 | tf_op jit(solution)/shard_map/ppermute | solution.py:140
  111.4 19.7 %collective-permute-start.26 = (bf16[80,1664]{1,0:T(8,128)(2,1)S(1)}, bf16[80,1664]{1,0:T(8,128)(2,1)S(1)}, u32[]{:S(2)}, u32[]{:S(2)}) collective-permute-start(bf16[80,1664]{1,0:T(8,128)(2,1)S(1)} %copy-done.15), channel_id=1, source_target_pairs={{0,4},{1,5},{2,6},{3,7},{4,0},{5,1},{6,2},{7,3},{8,12},{9,13},{10,... | collective-permute-start | bytes 798728 | tf_op jit(solution)/shard_map/ppermute | solution.py:38
  120.3 10.8 %collective-permute-start.27 = (bf16[80,1664]{1,0:T(8,128)(2,1)S(1)}, bf16[80,1664]{1,0:T(8,128)(2,1)S(1)}, u32[]{:S(2)}, u32[]{:S(2)}) collective-permute-start(bf16[80,1664]{1,0:T(8,128)(2,1)S(1)} %copy-done.15), channel_id=1, source_target_pairs={{0,2},{1,3},{2,4},{3,5},{4,6},{5,7},{6,0},{7,1},{8,10},{9,11},{10,... | collective-permute-start | bytes 798728 | tf_op jit(solution)/shard_map/ppermute | solution.py:38
  141.6 12.5 %collective-permute-start.33 = (bf16[64,1664]{1,0:T(8,128)(2,1)}, bf16[64,1664]{1,0:T(8,128)(2,1)}, u32[]{:S(2)}, u32[]{:S(2)}) collective-permute-start(bf16[64,1664]{1,0:T(8,128)(2,1)} %get-tuple-element.83), channel_id=1, source_target_pairs={{0,1},{1,0},{2,3},{3,2},{4,5},{5,4},{6,7},{7,6},{8,9},{9,8},{10,11... | collective-permute-start | bytes 638984 | tf_op jit(solution)/shard_map/ppermute | solution.py:38
  143.1 15.6 %collective-permute-start.35 = (bf16[64,1664]{1,0:T(8,128)(2,1)}, bf16[64,1664]{1,0:T(8,128)(2,1)}, u32[]{:S(2)}, u32[]{:S(2)}) collective-permute-start(bf16[64,1664]{1,0:T(8,128)(2,1)} %get-tuple-element.82), channel_id=1, source_target_pairs={{0,1},{1,0},{2,3},{3,2},{4,5},{5,4},{6,7},{7,6},{8,9},{9,8},{10,11... | collective-permute-start | bytes 638984 | tf_op jit(solution)/shard_map/ppermute | solution.py:38
  144.1 19.6 %collective-permute-start.30 = (bf16[64,1664]{1,0:T(8,128)(2,1)S(1)}, bf16[64,1664]{1,0:T(8,128)(2,1)S(1)}, u32[]{:S(2)}, u32[]{:S(2)}) collective-permute-start(bf16[64,1664]{1,0:T(8,128)(2,1)S(1)} %get-tuple-element.81), channel_id=1, source_target_pairs={{0,1},{1,0},{2,3},{3,2},{4,5},{5,4},{6,7},{7,6},{8,9},{9,8},{10,11... | collective-permute-start | bytes 638984 | tf_op jit(solution)/shard_map/ppermute | solution.py:38
  160.0 13.1 %collective-permute-start.32 = (bf16[64,1664]{1,0:T(8,128)(2,1)S(1)}, bf16[64,1664]{1,0:T(8,128)(2,1)S(1)}, u32[]{:S(2)}, u32[]{:S(2)}) collective-permute-start(bf16[64,1664]{1,0:T(8,128)(2,1)S(1)} %get-tuple-element.85), channel_id=1, source_target_pairs={{0,4},{1,5},{2,6},{3,7},{4,0},{5,1},{6,2},{7,3},{8,12},{9,13},{10,... | collective-permute-start | bytes 638984 | tf_op jit(solution)/shard_map/ppermute | solution.py:38
  160.1 13.0 %collective-permute-start.34 = (bf16[64,1664]{1,0:T(8,128)(2,1)S(1)}, bf16[64,1664]{1,0:T(8,128)(2,1)S(1)}, u32[]{:S(2)}, u32[]{:S(2)}) collective-permute-start(bf16[64,1664]{1,0:T(8,128)(2,1)S(1)} %get-tuple-element.87), channel_id=1, source_target_pairs={{0,6},{1,7},{2,0},{3,1},{4,2},{5,3},{6,4},{7,5},{8,14},{9,15},{10,... | collective-permute-start | bytes 638984 | tf_op jit(solution)/shard_map/ppermute | solution.py:38
  160.3 12.8 %collective-permute-start.36 = (bf16[64,1664]{1,0:T(8,128)(2,1)S(1)}, bf16[64,1664]{1,0:T(8,128)(2,1)S(1)}, u32[]{:S(2)}, u32[]{:S(2)}) collective-permute-start(bf16[64,1664]{1,0:T(8,128)(2,1)S(1)} %get-tuple-element.86), channel_id=1, source_target_pairs={{0,2},{1,3},{2,4},{3,5},{4,6},{5,7},{6,0},{7,1},{8,10},{9,11},{10,... | collective-permute-start | bytes 638984 | tf_op jit(solution)/shard_map/ppermute | solution.py:38
  163.2 10.1 %collective-permute-start.37 = (bf16[80,1664]{1,0:T(8,128)(2,1)S(1)}, bf16[80,1664]{1,0:T(8,128)(2,1)}, u32[]{:S(2)}, u32[]{:S(2)}) collective-permute-start(bf16[80,1664]{1,0:T(8,128)(2,1)S(1)} %copy-done.15), channel_id=1, source_target_pairs={{0,1},{1,0},{2,3},{3,2},{4,5},{5,4},{6,7},{7,6},{8,9},{9,8},{10,11... | collective-permute-start | bytes 798728 | tf_op jit(solution)/shard_map/ppermute | solution.py:38
  163.6 9.7 %collective-permute-start.38 = (bf16[80,1664]{1,0:T(8,128)(2,1)S(1)}, bf16[80,1664]{1,0:T(8,128)(2,1)}, u32[]{:S(2)}, u32[]{:S(2)}) collective-permute-start(bf16[80,1664]{1,0:T(8,128)(2,1)S(1)} %collective-permute-done.25), channel_id=1, source_target_pairs={{0,1},{1,0},{2,3},{3,2},{4,5},{5,4},{6,7},{7,6},{8,9},{9,8},{10,11... | collective-permute-start | bytes 798728 | tf_op jit(solution)/shard_map/ppermute | solution.py:38
  174.8 11.2 %collective-permute-start.39 = (bf16[16,6656]{1,0:T(8,128)(2,1)S(1)}, bf16[16,6656]{1,0:T(8,128)(2,1)}, u32[]{:S(2)}, u32[]{:S(2)}) collective-permute-start(bf16[16,6656]{1,0:T(8,128)(2,1)S(1)} %reshape.275), channel_id=1, source_target_pairs={{0,1},{1,0},{2,3},{3,2},{4,5},{5,4},{6,7},{7,6},{8,9},{9,8},{10,11... | collective-permute-start | bytes 638984 | tf_op jit(solution)/shard_map/ppermute | solution.py:38
  174.8 11.4 %collective-permute-start.40 = (bf16[16,6656]{1,0:T(8,128)(2,1)S(1)}, bf16[16,6656]{1,0:T(8,128)(2,1)}, u32[]{:S(2)}, u32[]{:S(2)}) collective-permute-start(bf16[16,6656]{1,0:T(8,128)(2,1)S(1)} %reshape.275), channel_id=1, source_target_pairs={{0,6},{1,7},{2,0},{3,1},{4,2},{5,3},{6,4},{7,5},{8,14},{9,15},{10,... | collective-permute-start | bytes 638984 | tf_op jit(solution)/shard_map/ppermute | solution.py:38
  178.4 11.7 %collective-permute-start.42 = (bf16[16,6656]{1,0:T(8,128)(2,1)S(1)}, bf16[16,6656]{1,0:T(8,128)(2,1)}, u32[]{:S(2)}, u32[]{:S(2)}) collective-permute-start(bf16[16,6656]{1,0:T(8,128)(2,1)S(1)} %reshape.275), channel_id=1, source_target_pairs={{0,2},{1,3},{2,4},{3,5},{4,6},{5,7},{6,0},{7,1},{8,10},{9,11},{10,... | collective-permute-start | bytes 638984 | tf_op jit(solution)/shard_map/ppermute | solution.py:38
  178.4 15.9 %collective-permute-start.44 = (bf16[16,6656]{1,0:T(8,128)(2,1)S(1)}, bf16[16,6656]{1,0:T(8,128)(2,1)}, u32[]{:S(2)}, u32[]{:S(2)}) collective-permute-start(bf16[16,6656]{1,0:T(8,128)(2,1)S(1)} %reshape.275), channel_id=1, source_target_pairs={{0,4},{1,5},{2,6},{3,7},{4,0},{5,1},{6,2},{7,3},{8,12},{9,13},{10,... | collective-permute-start | bytes 638984 | tf_op jit(solution)/shard_map/ppermute | solution.py:38
  181.8 90.9 %all-gather.14.cloned.1.call-start = ((), (), s32[]{:S(2)}) async-start(), calls=%async_computation.4 | async-start | bytes 4259840 | tf_op jit(solution)/shard_map/all_gather | solution.py:237
  181.9 14.2 %collective-permute-start.53 = (bf16[80,1664]{1,0:T(8,128)(2,1)S(1)}, bf16[80,1664]{1,0:T(8,128)(2,1)S(1)}, u32[]{:S(2)}, u32[]{:S(2)}) collective-permute-start(bf16[80,1664]{1,0:T(8,128)(2,1)S(1)} %collective-permute-done.27), channel_id=1, source_target_pairs={{0,1},{1,0},{2,3},{3,2},{4,5},{5,4},{6,7},{7,6},{8,9},{9,8},{10,11... | collective-permute-start | bytes 798728 | tf_op jit(solution)/shard_map/ppermute | solution.py:38
  186.0 24.5 %collective-permute-start.54 = (bf16[80,1664]{1,0:T(8,128)(2,1)S(1)}, bf16[80,1664]{1,0:T(8,128)(2,1)S(1)}, u32[]{:S(2)}, u32[]{:S(2)}) collective-permute-start(bf16[80,1664]{1,0:T(8,128)(2,1)S(1)} %collective-permute-done.26), channel_id=1, source_target_pairs={{0,1},{1,0},{2,3},{3,2},{4,5},{5,4},{6,7},{7,6},{8,9},{9,8},{10,11... | collective-permute-start | bytes 798728 | tf_op jit(solution)/shard_map/ppermute | solution.py:38
  186.2 14.9 %collective-permute-start.41 = (bf16[16,6656]{1,0:T(8,128)(2,1)}, bf16[16,6656]{1,0:T(8,128)(2,1)S(1)}, u32[]{:S(2)}, u32[]{:S(2)}) collective-permute-start(bf16[16,6656]{1,0:T(8,128)(2,1)} %collective-permute-done.40), channel_id=1, source_target_pairs={{0,1},{1,0},{2,3},{3,2},{4,5},{5,4},{6,7},{7,6},{8,9},{9,8},{10,11... | collective-permute-start | bytes 638984 | tf_op jit(solution)/shard_map/ppermute | solution.py:38
  190.1 13.4 %collective-permute-start.43 = (bf16[16,6656]{1,0:T(8,128)(2,1)}, bf16[16,6656]{1,0:T(8,128)(2,1)S(1)}, u32[]{:S(2)}, u32[]{:S(2)}) collective-permute-start(bf16[16,6656]{1,0:T(8,128)(2,1)} %collective-permute-done.42), channel_id=1, source_target_pairs={{0,1},{1,0},{2,3},{3,2},{4,5},{5,4},{6,7},{7,6},{8,9},{9,8},{10,11... | collective-permute-start | bytes 638984 | tf_op jit(solution)/shard_map/ppermute | solution.py:38
  194.3 11.4 %collective-permute-start.45 = (bf16[16,6656]{1,0:T(8,128)(2,1)}, bf16[16,6656]{1,0:T(8,128)(2,1)S(1)}, u32[]{:S(2)}, u32[]{:S(2)}) collective-permute-start(bf16[16,6656]{1,0:T(8,128)(2,1)} %collective-permute-done.44), channel_id=1, source_target_pairs={{0,1},{1,0},{2,3},{3,2},{4,5},{5,4},{6,7},{7,6},{8,9},{9,8},{10,11... | collective-permute-start | bytes 638984 | tf_op jit(solution)/shard_map/ppermute | solution.py:38
  237.4 9.4 %collective-permute-start.56 = (bf16[80,1664]{1,0:T(8,128)(2,1)S(1)}, bf16[80,1664]{1,0:T(8,128)(2,1)S(1)}, u32[]{:S(2)}, u32[]{:S(2)}) collective-permute-start(bf16[80,1664]{1,0:T(8,128)(2,1)S(1)} %get-tuple-element.77), channel_id=1, source_target_pairs={{0,1},{1,0},{2,3},{3,2},{4,5},{5,4},{6,7},{7,6},{8,9},{9,8},{10,11... | collective-permute-start | bytes 798728 | tf_op jit(solution)/shard_map/ppermute | solution.py:38
  238.9 13.6 %collective-permute-start.58 = (bf16[80,1664]{1,0:T(8,128)(2,1)S(1)}, bf16[80,1664]{1,0:T(8,128)(2,1)S(1)}, u32[]{:S(2)}, u32[]{:S(2)}) collective-permute-start(bf16[80,1664]{1,0:T(8,128)(2,1)S(1)} %get-tuple-element.76), channel_id=1, source_target_pairs={{0,1},{1,0},{2,3},{3,2},{4,5},{5,4},{6,7},{7,6},{8,9},{9,8},{10,11... | collective-permute-start | bytes 798728 | tf_op jit(solution)/shard_map/ppermute | solution.py:38
  239.5 16.8 %collective-permute-start.60 = (bf16[80,1664]{1,0:T(8,128)(2,1)S(1)}, bf16[80,1664]{1,0:T(8,128)(2,1)S(1)}, u32[]{:S(2)}, u32[]{:S(2)}) collective-permute-start(bf16[80,1664]{1,0:T(8,128)(2,1)S(1)} %get-tuple-element.75), channel_id=1, source_target_pairs={{0,1},{1,0},{2,3},{3,2},{4,5},{5,4},{6,7},{7,6},{8,9},{9,8},{10,11... | collective-permute-start | bytes 798728 | tf_op jit(solution)/shard_map/ppermute | solution.py:38
  240.9 31.7 %collective-permute-start.62 = (bf16[416,1024]{1,0:T(8,128)(2,1)S(1)}, bf16[416,1024]{1,0:T(8,128)(2,1)}, u32[]{:S(2)}, u32[]{:S(2)}) collective-permute-start(bf16[416,1024]{1,0:T(8,128)(2,1)S(1)} %copy-done.6), channel_id=1, source_target_pairs={{0,16},{8,24},{16,0},{24,8},{1,17},{9,25},{17,1},{25,9},{2,18},{10... | collective-permute-start | bytes 2555912 | tf_op jit(solution)/shard_map/ppermute | solution.py:132
  240.9 18.5 %collective-permute-start.55 = (bf16[80,1664]{1,0:T(8,128)(2,1)S(1)}, bf16[80,1664]{1,0:T(8,128)(2,1)S(1)}, u32[]{:S(2)}, u32[]{:S(2)}) collective-permute-start(bf16[80,1664]{1,0:T(8,128)(2,1)S(1)} %get-tuple-element.74), channel_id=1, source_target_pairs={{0,1},{1,0},{2,3},{3,2},{4,5},{5,4},{6,7},{7,6},{8,9},{9,8},{10,11... | collective-permute-start | bytes 798728 | tf_op jit(solution)/shard_map/ppermute | solution.py:38
  256.5 15.9 %collective-permute-start.57 = (bf16[80,1664]{1,0:T(8,128)(2,1)S(1)}, bf16[80,1664]{1,0:T(8,128)(2,1)S(1)}, u32[]{:S(2)}, u32[]{:S(2)}) collective-permute-start(bf16[80,1664]{1,0:T(8,128)(2,1)S(1)} %get-tuple-element.78), channel_id=1, source_target_pairs={{0,4},{1,5},{2,6},{3,7},{4,0},{5,1},{6,2},{7,3},{8,12},{9,13},{10,... | collective-permute-start | bytes 798728 | tf_op jit(solution)/shard_map/ppermute | solution.py:38
  256.8 15.6 %collective-permute-start.59 = (bf16[80,1664]{1,0:T(8,128)(2,1)S(1)}, bf16[80,1664]{1,0:T(8,128)(2,1)S(1)}, u32[]{:S(2)}, u32[]{:S(2)}) collective-permute-start(bf16[80,1664]{1,0:T(8,128)(2,1)S(1)} %get-tuple-element.80), channel_id=1, source_target_pairs={{0,6},{1,7},{2,0},{3,1},{4,2},{5,3},{6,4},{7,5},{8,14},{9,15},{10,... | collective-permute-start | bytes 798728 | tf_op jit(solution)/shard_map/ppermute | solution.py:38
  259.4 13.0 %collective-permute-start.61 = (bf16[80,1664]{1,0:T(8,128)(2,1)S(1)}, bf16[80,1664]{1,0:T(8,128)(2,1)S(1)}, u32[]{:S(2)}, u32[]{:S(2)}) collective-permute-start(bf16[80,1664]{1,0:T(8,128)(2,1)S(1)} %get-tuple-element.79), channel_id=1, source_target_pairs={{0,2},{1,3},{2,4},{3,5},{4,6},{5,7},{6,0},{7,1},{8,10},{9,11},{10,... | collective-permute-start | bytes 798728 | tf_op jit(solution)/shard_map/ppermute | solution.py:38
  273.9 13.7 %collective-permute-start.64 = (bf16[80,1664]{1,0:T(8,128)(2,1)S(1)}, bf16[80,1664]{1,0:T(8,128)(2,1)S(1)}, u32[]{:S(2)}, u32[]{:S(2)}) collective-permute-start(bf16[80,1664]{1,0:T(8,128)(2,1)S(1)} %add_convert_fusion.4), channel_id=1, source_target_pairs={{0,6},{1,7},{2,0},{3,1},{4,2},{5,3},{6,4},{7,5},{8,14},{9,15},{10,... | collective-permute-start | bytes 798728 | tf_op jit(solution)/shard_map/ppermute | solution.py:38
  277.9 14.4 %collective-permute-start.66 = (bf16[80,1664]{1,0:T(8,128)(2,1)S(1)}, bf16[80,1664]{1,0:T(8,128)(2,1)S(1)}, u32[]{:S(2)}, u32[]{:S(2)}) collective-permute-start(bf16[80,1664]{1,0:T(8,128)(2,1)S(1)} %add_convert_fusion.4), channel_id=1, source_target_pairs={{0,2},{1,3},{2,4},{3,5},{4,6},{5,7},{6,0},{7,1},{8,10},{9,11},{10,... | collective-permute-start | bytes 798728 | tf_op jit(solution)/shard_map/ppermute | solution.py:38
  277.9 21.7 %collective-permute-start.68 = (bf16[80,1664]{1,0:T(8,128)(2,1)S(1)}, bf16[80,1664]{1,0:T(8,128)(2,1)S(1)}, u32[]{:S(2)}, u32[]{:S(2)}) collective-permute-start(bf16[80,1664]{1,0:T(8,128)(2,1)S(1)} %add_convert_fusion.4), channel_id=1, source_target_pairs={{0,4},{1,5},{2,6},{3,7},{4,0},{5,1},{6,2},{7,3},{8,12},{9,13},{10,... | collective-permute-start | bytes 798728 | tf_op jit(solution)/shard_map/ppermute | solution.py:38
  281.9 24.2 %collective-permute-start.70 = (bf16[416,1024]{1,0:T(8,128)(2,1)S(1)}, bf16[416,1024]{1,0:T(8,128)(2,1)S(1)}, u32[]{:S(2)}, u32[]{:S(2)}) collective-permute-start(bf16[416,1024]{1,0:T(8,128)(2,1)S(1)} %copy-done.6), channel_id=1, source_target_pairs={{0,8},{8,0},{16,24},{24,16},{1,9},{9,1},{17,25},{25,17},{2,10},{10... | collective-permute-start | bytes 2555912 | tf_op jit(solution)/shard_map/ppermute | solution.py:140
  281.9 24.2 %collective-permute-start.71 = (bf16[416,1024]{1,0:T(8,128)(2,1)}, bf16[416,1024]{1,0:T(8,128)(2,1)S(1)}, u32[]{:S(2)}, u32[]{:S(2)}) collective-permute-start(bf16[416,1024]{1,0:T(8,128)(2,1)} %collective-permute-done.62.refs_3_), channel_id=1, source_target_pairs={{0,8},{8,0},{16,24},{24,16},{1,9},{9,1},{17,25},{25,17},{2,10},{10... | collective-permute-start | bytes 2555912 | tf_op jit(solution)/shard_map/ppermute | solution.py:140
  287.6 13.8 %collective-permute-start.65 = (bf16[80,1664]{1,0:T(8,128)(2,1)S(1)}, bf16[80,1664]{1,0:T(8,128)(2,1)S(1)}, u32[]{:S(2)}, u32[]{:S(2)}) collective-permute-start(bf16[80,1664]{1,0:T(8,128)(2,1)S(1)} %collective-permute-done.64), channel_id=1, source_target_pairs={{0,1},{1,0},{2,3},{3,2},{4,5},{5,4},{6,7},{7,6},{8,9},{9,8},{10,11... | collective-permute-start | bytes 798728 | tf_op jit(solution)/shard_map/ppermute | solution.py:38
  314.3 9.4 %collective-permute-start.73 = (bf16[80,1664]{1,0:T(8,128)(2,1)S(1)}, bf16[80,1664]{1,0:T(8,128)(2,1)S(1)}, u32[]{:S(2)}, u32[]{:S(2)}) collective-permute-start(bf16[80,1664]{1,0:T(8,128)(2,1)S(1)} %get-tuple-element.70), channel_id=1, source_target_pairs={{0,1},{1,0},{2,3},{3,2},{4,5},{5,4},{6,7},{7,6},{8,9},{9,8},{10,11... | collective-permute-start | bytes 798728 | tf_op jit(solution)/shard_map/ppermute | solution.py:38
  316.1 13.3 %collective-permute-start.75 = (bf16[80,1664]{1,0:T(8,128)(2,1)S(1)}, bf16[80,1664]{1,0:T(8,128)(2,1)S(1)}, u32[]{:S(2)}, u32[]{:S(2)}) collective-permute-start(bf16[80,1664]{1,0:T(8,128)(2,1)S(1)} %get-tuple-element.69), channel_id=1, source_target_pairs={{0,1},{1,0},{2,3},{3,2},{4,5},{5,4},{6,7},{7,6},{8,9},{9,8},{10,11... | collective-permute-start | bytes 798728 | tf_op jit(solution)/shard_map/ppermute | solution.py:38
  316.4 15.8 %collective-permute-start.77 = (bf16[80,1664]{1,0:T(8,128)(2,1)S(1)}, bf16[80,1664]{1,0:T(8,128)(2,1)S(1)}, u32[]{:S(2)}, u32[]{:S(2)}) collective-permute-start(bf16[80,1664]{1,0:T(8,128)(2,1)S(1)} %get-tuple-element.68), channel_id=1, source_target_pairs={{0,1},{1,0},{2,3},{3,2},{4,5},{5,4},{6,7},{7,6},{8,9},{9,8},{10,11... | collective-permute-start | bytes 798728 | tf_op jit(solution)/shard_map/ppermute | solution.py:38
  318.1 17.0 %collective-permute-start.72 = (bf16[80,1664]{1,0:T(8,128)(2,1)S(1)}, bf16[80,1664]{1,0:T(8,128)(2,1)S(1)}, u32[]{:S(2)}, u32[]{:S(2)}) collective-permute-start(bf16[80,1664]{1,0:T(8,128)(2,1)S(1)} %get-tuple-element.67), channel_id=1, source_target_pairs={{0,1},{1,0},{2,3},{3,2},{4,5},{5,4},{6,7},{7,6},{8,9},{9,8},{10,11... | collective-permute-start | bytes 798728 | tf_op jit(solution)/shard_map/ppermute | solution.py:38
  332.5 15.1 %collective-permute-start.74 = (bf16[80,1664]{1,0:T(8,128)(2,1)S(1)}, bf16[80,1664]{1,0:T(8,128)(2,1)S(1)}, u32[]{:S(2)}, u32[]{:S(2)}) collective-permute-start(bf16[80,1664]{1,0:T(8,128)(2,1)S(1)} %get-tuple-element.71), channel_id=1, source_target_pairs={{0,4},{1,5},{2,6},{3,7},{4,0},{5,1},{6,2},{7,3},{8,12},{9,13},{10,... | collective-permute-start | bytes 798728 | tf_op jit(solution)/shard_map/ppermute | solution.py:38
  332.5 15.0 %collective-permute-start.76 = (bf16[80,1664]{1,0:T(8,128)(2,1)S(1)}, bf16[80,1664]{1,0:T(8,128)(2,1)S(1)}, u32[]{:S(2)}, u32[]{:S(2)}) collective-permute-start(bf16[80,1664]{1,0:T(8,128)(2,1)S(1)} %get-tuple-element.73), channel_id=1, source_target_pairs={{0,6},{1,7},{2,0},{3,1},{4,2},{5,3},{6,4},{7,5},{8,14},{9,15},{10,... | collective-permute-start | bytes 798728 | tf_op jit(solution)/shard_map/ppermute | solution.py:38
  333.9 13.7 %collective-permute-start.78 = (bf16[80,1664]{1,0:T(8,128)(2,1)S(1)}, bf16[80,1664]{1,0:T(8,128)(2,1)S(1)}, u32[]{:S(2)}, u32[]{:S(2)}) collective-permute-start(bf16[80,1664]{1,0:T(8,128)(2,1)S(1)} %get-tuple-element.72), channel_id=1, source_target_pairs={{0,2},{1,3},{2,4},{3,5},{4,6},{5,7},{6,0},{7,1},{8,10},{9,11},{10,... | collective-permute-start | bytes 798728 | tf_op jit(solution)/shard_map/ppermute | solution.py:38
  (38 other events, 405.3 us)
Sparse Core Ops, SparseCore 0:
  17.7 19.9 all-gather.5
  40.3 45.5 all-gather.7
  92.8 25.4 all-gather.9
  181.9 22.1 all-gather.11
  212.2 29.6 all-gather.13
where the time goes:
time: 358 us; the launch traced here: 355 us
  waiting for transfers between devices  176 us (49%)
  starting transfers between devices  104 us (29%)
  Pallas kernels  21.4 us (6%)
  local copies, waits for them, and re-layouts  17.4 us (5%)
  matrix products  14.6 us (4%)
  between operations  14.1 us (4%)
  other arithmetic  8.1 us (2%)
    ppermute x70, waiting for transfers between devices, moved(): return lax.ppermute(value, 'gy', pairs)  173 us
    ppermute x70, starting transfers between devices, moved(): return lax.ppermute(value, 'gy', pairs)  99.7 us
    pallas_call x4, Pallas kernels, pieces_call(): pl.pallas_call(functools.partial(kernel, norm, counts, tile_of(rows.shape...  21.4 us
    unnamed x78, local copies, waits for them, and re-layouts  12.6 us
  transfers between devices with their start and end apart: 84, of which 41 were waited for; matrix products, arithmetic and copies ran while one was open for 10% of the time, Pallas kernels for 4%

commit v1 on v0

--- a/solution.py
+++ b/solution.py
@@ -92,24 +92,28 @@
     return jnp.stack([((z + k) % nz) * nx + (x + p) % nx for k in z_order(nz) for p in range(nx)])
 
 
-def relative_scatter(term):
+def relative_scatter(terms, late=None):
     nz, nx = grid_of(lax.axis_size("gy"))
     order = z_order(nz)
-    rows = term.shape[0] // (nz * nx)
-    arrived, own = [], None
+    swapped = {}
     for at in reversed(range(nz)):
-        k = order[at]
-        first = at * nx * rows
-        total = term[first : first + rows].astype(F32)
-        for p in range(1, nx):
-            total = total + moved(term[first + p * rows : first + (p + 1) * rows], 0, p).astype(F32)
-        if k:
-            arrived.append(moved(total.astype(BF), k, 0))
-        else:
-            own = total
-    for value in arrived:
-        own = own + value.astype(F32)
-    return own
+        swapped[at] = [moved(terms[at * nx + p], 0, p) for p in range(1, nx)]
+    arrived = []
+    for at in reversed(range(1, nz)):
+        last = added(terms[at * nx], *swapped[at])
+        arrived.append(moved(last, order[at], 0))
+    total = terms[0].astype(F32)
+    for value in swapped[0] + arrived:
+        total = total + value.astype(F32)
+    return total if late is None else (total, after(late, last))
+
+
+def after(value, first):
+    return lax.optimization_barrier((value, first))[0]
+
+
+def far_z():
+    return z_order(grid_of(lax.axis_size("gy"))[0])[-1]
 
 
 def absolute_rows(value):
@@ -174,41 +178,95 @@
         out_ref[span, :] = jnp.dot(normed, whole[...], preferred_element_type=F32).astype(BF)
 
 
+def store_blocks(out_refs, step, value):
+    rows = out_refs[0].shape[0]
+    tile = value.shape[0] // rows
+    for at in range(tile):
+        out_refs[step * tile + at][...] = value[at * rows : (at + 1) * rows].astype(BF)
+
+
 def block_kernel(norm, counts, tile, spots, rows_ref, gain_ref, *refs):
     ups, downs = refs[: counts[0]], refs[counts[0] : sum(counts)]
-    out_ref, up, down, up_sems, down_sems = refs[sum(counts) :]
+    out_refs, (up, down, up_sems, down_sems) = refs[sum(counts) : -4], refs[-4:]
     up_copies = load_pieces(spots, ups, up, up_sems)
     down_copies = load_pieces(spots, downs, down, down_sems)
     for copy in up_copies + down_copies:
         copy.wait()
-
-    @pl.loop(0, rows_ref.shape[0] // tile)
-    def _(step):
-        span = pl.ds(pl.multiple_of(step * tile, 16), tile)
-        normed = norm(rows_ref[span, :], gain_ref[...]).astype(BF)
+    for step in range(rows_ref.shape[0] // tile):
+        normed = norm(rows_ref[step * tile : (step + 1) * tile, :], gain_ref[...]).astype(BF)
         raised = jnp.dot(normed, up[...], preferred_element_type=F32)
         hidden = (0.5 * raised * (1.0 + lax.erf(raised * math.sqrt(0.5)))).astype(BF)
-        out_ref[span, :] = lax.dot_general(
+        value = lax.dot_general(
             hidden, down[...], (((1,), (1,)), ((), ())), preferred_element_type=F32
-        ).astype(BF)
+        )
+        store_blocks(out_refs, step, value)
+
+
+def out_kernel(tile, mix_ref, weight_ref, *out_refs):
+    for step in range(mix_ref.shape[0] // tile):
+        value = lax.dot_general(
+            mix_ref[step * tile : (step + 1) * tile, :],
+            weight_ref[...],
+            (((1,), (1,)), ((), ())),
+            preferred_element_type=F32,
+        )
+        store_blocks(out_refs, step, value)
+
+
+def add_kernel(*refs):
+    total = refs[0][...].astype(F32)
+    for ref in refs[1:-1]:
+        total = total + ref[...].astype(F32)
+    refs[-1][...] = total.astype(BF)
+
+
+def added(*values):
+    return pl.pallas_call(
+        add_kernel,
+        out_shape=jax.ShapeDtypeStruct(values[0].shape, BF),
+        cost_estimate=pl.CostEstimate(
+            flops=values[0].size, bytes_accessed=6 * values[0].size, transcendentals=0
+        ),
+    )(*values)
+
+
+def block_tile(total):
+    count = lax.axis_size("gy")
+    rows = total // count
+    return rows * max(size for size in range(1, count + 1) if count % size == 0 and rows * size <= 320)
+
+
+def out_term(mix, weight):
+    count = lax.axis_size("gy")
+    total, columns = mix.shape[0], weight.shape[0]
+    return pl.pallas_call(
+        functools.partial(out_kernel, block_tile(total)),
+        out_shape=[jax.ShapeDtypeStruct((total // count, columns), BF)] * count,
+        compiler_params=pltpu.CompilerParams(vmem_limit_bytes=40 * 1024 * 1024),
+        cost_estimate=pl.CostEstimate(
+            flops=2 * mix.size * columns,
+            bytes_accessed=2 * (mix.size + weight.size + total * columns),
+            transcendentals=0,
+        ),
+    )(mix, weight)
 
 
 def tile_of(rows):
     return max(size for size in range(16, 321, 16) if rows % size == 0)
 
 
-def pieces_call(kernel, norm, rows, gain, groups, columns, flops):
+def pieces_call(kernel, norm, rows, gain, groups, tile, outs, flops):
     counts = [len(group) for group in groups]
     wholes = [(group[0].shape[0] * len(group), group[0].shape[1]) for group in groups]
     spec = pl.BlockSpec(memory_space=pltpu.VMEM)
     return pl.pallas_call(
-        functools.partial(kernel, norm, counts, tile_of(rows.shape[0])),
-        out_shape=jax.ShapeDtypeStruct((rows.shape[0], columns), BF),
+        functools.partial(kernel, norm, counts, tile),
+        out_shape=[jax.ShapeDtypeStruct(shape, BF) for shape in outs],
         grid_spec=pltpu.PrefetchScalarGridSpec(
             num_scalar_prefetch=1,
             grid=(),
             in_specs=[spec, spec] + [pl.BlockSpec(memory_space=pl.ANY)] * sum(counts),
-            out_specs=spec,
+            out_specs=[spec] * len(outs),
             scratch_shapes=[pltpu.VMEM(shape, BF) for shape in wholes]
             + [pltpu.SemaphoreType.DMA((count,)) for count in counts],
         ),
@@ -222,15 +280,21 @@
 
 
 def product_of(norm, rows, gain, pieces):
-    columns = pieces[0].shape[1]
+    total, columns = rows.shape[0], pieces[0].shape[1]
+    flops = 2 * rows.size * columns
     return pieces_call(
-        product_kernel, norm, rows, gain, [pieces], columns, 2 * rows.size * columns
+        product_kernel, norm, rows, gain, [pieces], tile_of(total), [(total, columns)], flops
+    )[0]
+
+
+def block_of(norm, rows, gain, ups, downs):
+    count = lax.axis_size("gy")
+    total, width = rows.shape
+    flops = 4 * rows.size * ups[0].shape[1]
+    outs = [(total // count, width)] * count
+    return pieces_call(
+        block_kernel, norm, rows, gain, [ups, downs], block_tile(total), outs, flops
     )
-
-
-def block_of(norm, rows, gain, ups, downs):
-    flops = 4 * rows.size * ups[0].shape[1]
-    return pieces_call(block_kernel, norm, rows, gain, [ups, downs], rows.shape[1], flops)
 
 
 def weight_block(weight):
@@ -256,12 +320,6 @@
     probs = (weights / jnp.sum(weights, axis=-1, keepdims=True)).astype(BF)
     mixed = jnp.einsum("hqk,khe->qhe", probs, values, preferred_element_type=F32)
     return mixed.astype(BF).reshape(total, heads_here * HEAD_DIM)
-
-
-def out_term(hidden, weight):
-    return lax.dot_general(
-        hidden, weight, (((1,), (1,)), ((), ())), preferred_element_type=F32
-    ).astype(BF)
 
 
 def shards(
@@ -296,59 +354,52 @@
 
     patch_found = start_gather(patches)
     sent_qkv = send_weight(vit_qkv)
-    sent_down = send_weight(vit_down)
     outs_block = weight_block(jnp.concatenate([vit_out, dec_out], axis=1))
     qkvs = pieces_of(sent_qkv)
     patch_all = finish_gather(patch_found)
     enc_qkv = product_of(layer_norm, patch_all, norm_gains[0], qkvs)
-    enc_qkv, outs_block, vit_up, prompt = tied(enc_qkv, outs_block, vit_up, prompt)
+    enc_qkv, outs_block, vit_up = tied(enc_qkv, outs_block, vit_up)
     up_block = weight_block(vit_up)
     columns = vit_out.shape[1]
     out_block, dout_block = outs_block[:, :columns], outs_block[:, columns:]
-    prompt_found = start_z(prompt)
     enc_mix = attend(enc_qkv, labels[:, None] == labels[None, :])
     summed = relative_scatter(out_term(enc_mix, out_block))
     enc_mid = (patches.astype(F32) + summed).astype(BF)
-    enc_mid, up_block, merge_proj, sent_down = tied(enc_mid, up_block, merge_proj, sent_down)
+    enc_mid, up_block, vit_down = tied(enc_mid, up_block, vit_down)
+    down_block = weight_block(vit_down)
+
+    mid_all = relative_gather(enc_mid)
+    mid_all, down_block, merge_proj = tied(mid_all, down_block, merge_proj)
     merge_block = weight_block(merge_proj)
-    downs = pieces_of(sent_down)
-
-    mid_all = relative_gather(enc_mid)
-    mid_all, prompt_found = tied(mid_all, prompt_found)
-    prompt_found = swap_x(prompt_found, 0)
-    term = block_of(layer_norm, mid_all, norm_gains[1], [up_block], downs)
+    term = block_of(layer_norm, mid_all, norm_gains[1], [up_block], [down_block])
     enc_out = (enc_mid.astype(F32) + relative_scatter(term)).astype(BF)
-    enc_out, merge_block, dec_qkv, prompt_found, dec_down = tied(
-        enc_out, merge_block, dec_qkv, prompt_found, dec_down
-    )
+    enc_out, merge_block, dec_qkv = tied(enc_out, merge_block, dec_qkv)
     dqkv_block = weight_block(dec_qkv)
     windows = layer_norm(enc_out, norm_gains[2]).astype(BF).reshape(local // 4, 4 * width)
-    prompt_found = swap_x(prompt_found, 1)
     windows = relative_gather(windows)
-    prompt_all = joined_blocks(prompt_found)
     merged = jnp.dot(windows, merge_block, preferred_element_type=F32).astype(BF)
     merged, dqkv_block, dec_up = tied(merged, dqkv_block, dec_up)
     dup_block = weight_block(dec_up)
-    sent_ddown = send_weight(dec_down)
     merged = lax.dot_general(
         merged, picks.astype(BF), (((0,), (0,)), ((), ())), preferred_element_type=F32
     ).astype(BF)
     merged_all = absolute_rows(relative_gather(merged))
 
+    mine = hits[:seq_local]
     placed = lax.dot_general(
-        hits.astype(BF), merged_all, (((1,), (1,)), ((), ())), preferred_element_type=F32
+        mine.astype(BF), merged_all, (((1,), (1,)), ((), ())), preferred_element_type=F32
     ).astype(BF)
-    dec_all = jnp.where(jnp.any(hits, axis=1)[:, None], placed, prompt_all)
-    dec_in = dec_all[:seq_local]
+    dec_in = jnp.where(jnp.any(mine, axis=1)[:, None], placed, prompt)
+    dec_all = relative_gather(dec_in)
     dec_rows = product_of(rms_norm, dec_all, norm_gains[3], [dqkv_block])
     dec_mix = attend(dec_rows, spots_of[:, None] >= spots_of[None, :])
+    dec_mix, dup_block, dec_down = tied(dec_mix, dup_block, dec_down)
+    ddown_block = weight_block(dec_down)
     summed = relative_scatter(out_term(dec_mix, dout_block))
     dec_mid = (dec_in.astype(F32) + summed).astype(BF)
-    dec_mid, dup_block, sent_ddown = tied(dec_mid, dup_block, sent_ddown)
-    ddowns = pieces_of(sent_ddown)
 
     mid_all = relative_gather(dec_mid)
-    term = block_of(rms_norm, mid_all, norm_gains[4], [dup_block], ddowns)
+    term = block_of(rms_norm, mid_all, norm_gains[4], [dup_block], [ddown_block])
     return (dec_mid.astype(F32) + relative_scatter(term)).astype(BF)
 
 

time: 358 us -> 353 us (0.986)
  waiting for transfers between devices: 176 us -> 148 us
  Pallas kernels: 21.4 us -> 42.6 us
  local copies, waits for them, and re-layouts: 17.4 us -> 33 us
  starting transfers between devices: 104 us -> 97.4 us
  matrix products: 14.6 us -> 9.2 us
    ppermute x70, waiting for transfers between devices: 173 us -> 146 us  [moved(): return lax.ppermute(value, 'gy', pairs)]
    pallas_call x4 -> x18, Pallas kernels: 21.4 us -> 42.6 us  [the longest x12 21.6 us: added(): pl.pallas_call(add_kernel, out_shape=jax.ShapeDtypeStruct(values[0].shape...]
    unnamed x78 -> x124, local copies, waits for them, and re-layouts: 12.6 us -> 29.3 us
    ppermute x70, starting transfers between devices: 99.7 us -> 95.3 us  [moved(): return lax.ppermute(value, 'gy', pairs)]
    dot_general x3 -> x1, matrix products: 4.38 us -> 0.32 us  [shards(): lax.dot_general(mine.astype(BF), merged_all, (((1,), (1,)), ((), ())), pr...]
  transfers between devices with their start and end apart: 84 -> 80, of which waited for: 41 -> 43; matrix products, arithmetic and copies ran while one was open for 10% -> 7% of each run, Pallas kernels for 4% -> 10%
where the time goes in v1:
time: 353 us; the launch traced here: 352 us
  waiting for transfers between devices  148 us (42%)
  starting transfers between devices  97.4 us (28%)
  Pallas kernels  42.6 us (12%)
  local copies, waits for them, and re-layouts  33 us (9%)
  between operations  14.5 us (4%)
  matrix products  9.2 us (3%)
  other arithmetic  7.33 us (2%)
    ppermute x70, waiting for transfers between devices, moved(): return lax.ppermute(value, 'gy', pairs)  146 us
    ppermute x70, starting transfers between devices, moved(): return lax.ppermute(value, 'gy', pairs)  95.3 us
    unnamed x124, local copies, waits for them, and re-layouts  29.3 us
    pallas_call x12, Pallas kernels, added(): pl.pallas_call(add_kernel, out_shape=jax.ShapeDtypeStruct(values[0].shape...  21.6 us
    pallas_call x4, Pallas kernels, pieces_call(): pl.pallas_call(functools.partial(kernel, norm, counts, tile), out_shape=[...  19.6 us
  transfers between devices with their start and end apart: 80, of which 43 were waited for; matrix products, arithmetic and copies ran while one was open for 7% of the time, Pallas kernels for 10%

profile of v1, /device:TPU:0, one launch (start us, length us, event | category | flops | bytes accessed | tf_op | source)
XLA Modules:
  0.0 351.8 jit_solution(16154316555020833602)
XLA Ops:
  6.5 5.0 %collective-permute-start.1 = (bf16[64,1664]{1,0:T(8,128)(2,1)}, bf16[64,1664]{1,0:T(8,128)(2,1)S(1)}, u32[]{:S(2)}, u32[]{:S(2)}) collective-permute-start(bf16[64,1664]{1,0:T(8,128)(2,1)} %param.14), channel_id=1, source_target_pairs={{0,6},{1,7},{2,0},{3,1},{4,2},{5,3},{6,4},{7,5},{8,14},{9,15},{10,... | collective-permute-start | bytes 638984 | tf_op jit(solution)/shard_map/ppermute | solution.py:38
  15.6 2.0 pad_maximum_fusion
  21.5 1.8 collective-permute-done.3
  24.5 5.4 %collective-permute-done.5 = bf16[64,1664]{1,0:T(8,128)(2,1)S(1)} collective-permute-done((bf16[64,1664]{1,0:T(8,128)(2,1)}, bf16[64,1664]{1,0:T(8,128)(2,1)S(1)}, u32[]{:S(2)}, u32[]{:S(2)}) %collective-permute-start.5) | collective-permute-done | bytes 213024 | tf_op jit(solution)/shard_map/ppermute | solution.py:38
  32.7 4.0 %collective-permute-done.6 = bf16[64,1664]{1,0:T(8,128)(2,1)S(1)} collective-permute-done((bf16[64,1664]{1,0:T(8,128)(2,1)S(1)}, bf16[64,1664]{1,0:T(8,128)(2,1)S(1)}, u32[]{:S(2)}, u32[]{:S(2)}) %collective-permute-start.6) | collective-permute-done | bytes 213024 | tf_op jit(solution)/shard_map/ppermute | solution.py:38
  36.8 3.4 shard_map.136
  51.2 4.1 %collective-permute-done.11.refs_1_ = bf16[64,1664]{1,0:T(8,128)(2,1)S(1)} collective-permute-done((bf16[64,1664]{1,0:T(8,128)(2,1)S(1)}, bf16[64,1664]{1,0:T(8,128)(2,1)S(1)}, u32[]{:S(2)}, u32[]{:S(2)}) %collective-permute-start.11) | collective-permute-done | bytes 213024 | tf_op jit(solution)/shard_map/ppermute | solution.py:38
  56.0 1.8 shard_map.138
  57.8 1.9 collective-permute-start.12
  60.6 1.8 shard_map.139
  62.4 3.6 %collective-permute-start.14 = (bf16[64,1664]{1,0:T(8,128)(2,1)}, bf16[64,1664]{1,0:T(8,128)(2,1)S(1)}, u32[]{:S(2)}, u32[]{:S(2)}) collective-permute-start(bf16[64,1664]{1,0:T(8,128)(2,1)} %shard_map.139), channel_id=1, source_target_pairs={{0,6},{1,7},{2,0},{3,1},{4,2},{5,3},{6,4},{7,5},{8,14},{9,15},{10,... | collective-permute-start | bytes 638984 | tf_op jit(solution)/shard_map/ppermute | solution.py:38
  68.4 1.8 collective-permute-start.16
  71.9 4.5 %collective-permute-done.16 = bf16[64,1664]{1,0:T(8,128)(2,1)S(1)} collective-permute-done((bf16[64,1664]{1,0:T(8,128)(2,1)}, bf16[64,1664]{1,0:T(8,128)(2,1)S(1)}, u32[]{:S(2)}, u32[]{:S(2)}) %collective-permute-start.16) | collective-permute-done | bytes 213024 | tf_op jit(solution)/shard_map/ppermute | solution.py:38
  77.2 3.0 collective-permute-start.18
  81.4 4.5 %collective-permute-done.18 = bf16[64,1664]{1,0:T(8,128)(2,1)S(1)} collective-permute-done((bf16[64,1664]{1,0:T(8,128)(2,1)S(1)}, bf16[64,1664]{1,0:T(8,128)(2,1)S(1)}, u32[]{:S(2)}, u32[]{:S(2)}) %collective-permute-start.18) | collective-permute-done | bytes 213024 | tf_op jit(solution)/shard_map/ppermute | solution.py:38
  87.4 3.5 collective-permute-done.20
  92.2 6.2 %collective-permute-done.22 = bf16[64,1664]{1,0:T(8,128)(2,1)S(1)} collective-permute-done((bf16[64,1664]{1,0:T(8,128)(2,1)S(1)}, bf16[64,1664]{1,0:T(8,128)(2,1)S(1)}, u32[]{:S(2)}, u32[]{:S(2)}) %collective-permute-start.22) | collective-permute-done | bytes 213024 | tf_op jit(solution)/shard_map/ppermute | solution.py:38
  100.1 4.2 %collective-permute-done.23 = bf16[64,1664]{1,0:T(8,128)(2,1)S(1)} collective-permute-done((bf16[64,1664]{1,0:T(8,128)(2,1)S(1)}, bf16[64,1664]{1,0:T(8,128)(2,1)S(1)}, u32[]{:S(2)}, u32[]{:S(2)}) %collective-permute-start.23) | collective-permute-done | bytes 213024 | tf_op jit(solution)/shard_map/ppermute | solution.py:38
  104.3 2.0 all-gather.12.cloned.1.call-done.refs_1_
  106.5 2.0 copy-done.15
  108.5 2.0 copy-done.17
  110.4 6.5 %shard_map.141 = (bf16[64,1664]{1,0:T(8,128)(2,1)S(1)}, bf16[64,1664]{1,0:T(8,128)(2,1)S(1)}, bf16[64,1664]{1,0:T(8,128)(2,1)S(1)}, bf16[64,1664]{1,0:T(8,128)(2...) custom-call(s32[4]{0:T(128)S(1)} %pad_add_fusion.spots, ...), custom_call_target="tpu_custom_call" | custom-call | flops 3489660928 | bytes 10223616 | tf_op jit(solution)/shard_map/pallas_call | solution.py:262
  123.0 4.0 %collective-permute-done.25.refs_1_ = bf16[64,1664]{1,0:T(8,128)(2,1)S(1)} collective-permute-done((bf16[64,1664]{1,0:T(8,128)(2,1)S(1)}, bf16[64,1664]{1,0:T(8,128)(2,1)S(1)}, u32[]{:S(2)}, u32[]{:S(2)}) %collective-permute-start.25) | collective-permute-done | bytes 213024 | tf_op jit(solution)/shard_map/ppermute | solution.py:38
  129.5 2.4 collective-permute-start.26
  134.3 3.0 collective-permute-start.28
  143.8 4.3 %collective-permute-done.30 = bf16[64,1664]{1,0:T(8,128)(2,1)S(1)} collective-permute-done((bf16[64,1664]{1,0:T(8,128)(2,1)}, bf16[64,1664]{1,0:T(8,128)(2,1)S(1)}, u32[]{:S(2)}, u32[]{:S(2)}) %collective-permute-start.30) | collective-permute-done | bytes 213024 | tf_op jit(solution)/shard_map/ppermute | solution.py:38
  151.6 5.3 %collective-permute-start.32 = (bf16[16,6656]{1,0:T(8,128)(2,1)S(1)}, bf16[16,6656]{1,0:T(8,128)(2,1)}, u32[]{:S(2)}, u32[]{:S(2)}) collective-permute-start(bf16[16,6656]{1,0:T(8,128)(2,1)S(1)} %reshape.275), channel_id=1, source_target_pairs={{0,6},{1,7},{2,0},{3,1},{4,2},{5,3},{6,4},{7,5},{8,14},{9,15},{10,... | collective-permute-start | bytes 638984 | tf_op jit(solution)/shard_map/ppermute | solution.py:38
  158.3 4.4 %collective-permute-done.32 = bf16[16,6656]{1,0:T(8,128)(2,1)} collective-permute-done((bf16[16,6656]{1,0:T(8,128)(2,1)S(1)}, bf16[16,6656]{1,0:T(8,128)(2,1)}, u32[]{:S(2)}, u32[]{:S(2)}) %collective-permute-start.32) | collective-permute-done | bytes 213024 | tf_op jit(solution)/shard_map/ppermute | solution.py:38
  165.2 3.2 collective-permute-done.34
  168.9 6.0 %collective-permute-done.36 = bf16[16,6656]{1,0:T(8,128)(2,1)S(1)} collective-permute-done((bf16[16,6656]{1,0:T(8,128)(2,1)S(1)}, bf16[16,6656]{1,0:T(8,128)(2,1)S(1)}, u32[]{:S(2)}, u32[]{:S(2)}) %collective-permute-start.36) | collective-permute-done | bytes 213024 | tf_op jit(solution)/shard_map/ppermute | solution.py:38
  175.6 5.7 %collective-permute-done.37 = bf16[16,6656]{1,0:T(8,128)(2,1)S(1)} collective-permute-done((bf16[16,6656]{1,0:T(8,128)(2,1)S(1)}, bf16[16,6656]{1,0:T(8,128)(2,1)S(1)}, u32[]{:S(2)}, u32[]{:S(2)}) %collective-permute-start.37) | collective-permute-done | bytes 213024 | tf_op jit(solution)/shard_map/ppermute | solution.py:38
  182.7 2.4 collective-permute-start.39
  189.7 2.2 collective-permute-done.43
  194.0 3.5 collective-permute-done.42
  202.4 8.4 %collective-permute-done.46 = bf16[80,1664]{1,0:T(8,128)(2,1)S(1)} collective-permute-done((bf16[80,1664]{1,0:T(8,128)(2,1)S(1)}, bf16[80,1664]{1,0:T(8,128)(2,1)S(1)}, u32[]{:S(2)}, u32[]{:S(2)}) %collective-permute-start.46) | collective-permute-done | bytes 266272 | tf_op jit(solution)/shard_map/ppermute | solution.py:38
  210.9 1.9 collective-permute-done.48
  213.7 7.3 %collective-permute-done.50 = bf16[80,1664]{1,0:T(8,128)(2,1)S(1)} collective-permute-done((bf16[80,1664]{1,0:T(8,128)(2,1)S(1)}, bf16[80,1664]{1,0:T(8,128)(2,1)S(1)}, u32[]{:S(2)}, u32[]{:S(2)}) %collective-permute-start.50) | collective-permute-done | bytes 266272 | tf_op jit(solution)/shard_map/ppermute | solution.py:38
  221.6 5.8 %collective-permute-done.51 = bf16[80,1664]{1,0:T(8,128)(2,1)S(1)} collective-permute-done((bf16[80,1664]{1,0:T(8,128)(2,1)S(1)}, bf16[80,1664]{1,0:T(8,128)(2,1)S(1)}, u32[]{:S(2)}, u32[]{:S(2)}) %collective-permute-start.51) | collective-permute-done | bytes 266272 | tf_op jit(solution)/shard_map/ppermute | solution.py:38
  227.4 3.3 shard_map.145
  231.7 3.1 fusion.39
  234.8 2.4 fusion.9
  244.4 5.3 %collective-permute-done.53.refs_1_ = bf16[80,1664]{1,0:T(8,128)(2,1)S(1)} collective-permute-done((bf16[80,1664]{1,0:T(8,128)(2,1)S(1)}, bf16[80,1664]{1,0:T(8,128)(2,1)S(1)}, u32[]{:S(2)}, u32[]{:S(2)}) %collective-permute-start.53) | collective-permute-done | bytes 266272 | tf_op jit(solution)/shard_map/ppermute | solution.py:38
  250.4 1.8 shard_map.147
  252.2 4.7 %collective-permute-start.54 = (bf16[80,1664]{1,0:T(8,128)(2,1)}, bf16[80,1664]{1,0:T(8,128)(2,1)S(1)}, u32[]{:S(2)}, u32[]{:S(2)}) collective-permute-start(bf16[80,1664]{1,0:T(8,128)(2,1)} %shard_map.147), channel_id=1, source_target_pairs={{0,4},{1,5},{2,6},{3,7},{4,0},{5,1},{6,2},{7,3},{8,12},{9,13},{10,... | collective-permute-start | bytes 798728 | tf_op jit(solution)/shard_map/ppermute | solution.py:38
  257.6 1.8 shard_map.148
  259.4 3.4 collective-permute-start.56
  263.5 1.8 shard_map.149
  265.3 2.0 collective-permute-done.54
  268.2 8.1 %collective-permute-done.58 = bf16[80,1664]{1,0:T(8,128)(2,1)S(1)} collective-permute-done((bf16[80,1664]{1,0:T(8,128)(2,1)}, bf16[80,1664]{1,0:T(8,128)(2,1)S(1)}, u32[]{:S(2)}, u32[]{:S(2)}) %collective-permute-start.58) | collective-permute-done | bytes 266272 | tf_op jit(solution)/shard_map/ppermute | solution.py:38
  277.7 4.5 %collective-permute-start.60 = (bf16[80,1664]{1,0:T(8,128)(2,1)S(1)}, bf16[80,1664]{1,0:T(8,128)(2,1)S(1)}, u32[]{:S(2)}, u32[]{:S(2)}) collective-permute-start(bf16[80,1664]{1,0:T(8,128)(2,1)S(1)} %get-tuple-element.106), channel_id=1, source_target_pairs={{0,6},{1,7},{2,0},{3,1},{4,2},{5,3},{6,4},{7,5},{8,14},{9,15},{10,... | collective-permute-start | bytes 798728 | tf_op jit(solution)/shard_map/ppermute | solution.py:38
  282.7 3.5 collective-permute-start.64
  288.2 4.7 %collective-permute-done.62 = bf16[80,1664]{1,0:T(8,128)(2,1)S(1)} collective-permute-done((bf16[80,1664]{1,0:T(8,128)(2,1)S(1)}, bf16[80,1664]{1,0:T(8,128)(2,1)S(1)}, u32[]{:S(2)}, u32[]{:S(2)}) %collective-permute-start.62) | collective-permute-done | bytes 266272 | tf_op jit(solution)/shard_map/ppermute | solution.py:38
  293.0 4.1 %collective-permute-done.64 = bf16[80,1664]{1,0:T(8,128)(2,1)S(1)} collective-permute-done((bf16[80,1664]{1,0:T(8,128)(2,1)S(1)}, bf16[80,1664]{1,0:T(8,128)(2,1)S(1)}, u32[]{:S(2)}, u32[]{:S(2)}) %collective-permute-start.64) | collective-permute-done | bytes 266272 | tf_op jit(solution)/shard_map/ppermute | solution.py:38
  297.3 2.1 collective-permute-done.63
  299.5 4.1 %collective-permute-done.65 = bf16[80,1664]{1,0:T(8,128)(2,1)S(1)} collective-permute-done((bf16[80,1664]{1,0:T(8,128)(2,1)S(1)}, bf16[80,1664]{1,0:T(8,128)(2,1)S(1)}, u32[]{:S(2)}, u32[]{:S(2)}) %collective-permute-start.65) | collective-permute-done | bytes 266272 | tf_op jit(solution)/shard_map/ppermute | solution.py:38
  303.6 2.0 copy-done.14
  305.6 2.0 copy-done.16
  307.6 6.5 %shard_map.150 = (bf16[80,1664]{1,0:T(8,128)(2,1)S(1)}, bf16[80,1664]{1,0:T(8,128)(2,1)S(1)}, bf16[80,1664]{1,0:T(8,128)(2,1)S(1)}, bf16[80,1664]{1,0:T(8,128)(2...) custom-call(s32[4]{0:T(128)S(1)} %pad_add_fusion.spots, ...), custom_call_target="tpu_custom_call" | custom-call | flops 4362076160 | bytes 11075584 | tf_op jit(solution)/shard_map/pallas_call | solution.py:262
  316.2 2.0 collective-permute-start.69
  318.2 2.0 collective-permute-start.66
  320.2 2.4 collective-permute-done.67.refs_1_
  327.9 5.2 %collective-permute-start.70 = (bf16[80,1664]{1,0:T(8,128)(2,1)}, bf16[80,1664]{1,0:T(8,128)(2,1)S(1)}, u32[]{:S(2)}, u32[]{:S(2)}) collective-permute-start(bf16[80,1664]{1,0:T(8,128)(2,1)} %shard_map.152), channel_id=1, source_target_pairs={{0,6},{1,7},{2,0},{3,1},{4,2},{5,3},{6,4},{7,5},{8,14},{9,15},{10,... | collective-permute-start | bytes 798728 | tf_op jit(solution)/shard_map/ppermute | solution.py:38
  337.0 2.6 collective-permute-done.70
  339.6 4.4 %collective-permute-done.72 = bf16[80,1664]{1,0:T(8,128)(2,1)S(1)} collective-permute-done((bf16[80,1664]{1,0:T(8,128)(2,1)}, bf16[80,1664]{1,0:T(8,128)(2,1)S(1)}, u32[]{:S(2)}, u32[]{:S(2)}) %collective-permute-start.72) | collective-permute-done | bytes 266272 | tf_op jit(solution)/shard_map/ppermute | solution.py:38
  (295 shorter events, 102.9 us)
Async XLA Ops:
  6.5 33.6 %all-gather.8.cloned.1.call-start = ((), (), s32[]{:S(2)}) async-start(), calls=%async_computation | async-start | bytes 2129920 | tf_op jit(solution)/shard_map/all_gather | solution.py:301
  6.5 13.3 %collective-permute-start.1 = (bf16[64,1664]{1,0:T(8,128)(2,1)}, bf16[64,1664]{1,0:T(8,128)(2,1)S(1)}, u32[]{:S(2)}, u32[]{:S(2)}) collective-permute-start(bf16[64,1664]{1,0:T(8,128)(2,1)} %param.14), channel_id=1, source_target_pairs={{0,6},{1,7},{2,0},{3,1},{4,2},{5,3},{6,4},{7,5},{8,14},{9,15},{10,... | collective-permute-start | bytes 638984 | tf_op jit(solution)/shard_map/ppermute | solution.py:38
  11.6 8.3 %collective-permute-start = (bf16[64,1664]{1,0:T(8,128)(2,1)}, bf16[64,1664]{1,0:T(8,128)(2,1)}, u32[]{:S(2)}, u32[]{:S(2)}) collective-permute-start(bf16[64,1664]{1,0:T(8,128)(2,1)} %param.14), channel_id=1, source_target_pairs={{0,1},{1,0},{2,3},{3,2},{4,5},{5,4},{6,7},{7,6},{8,9},{9,8},{10,11... | collective-permute-start | bytes 638984 | tf_op jit(solution)/shard_map/ppermute | solution.py:38
  13.1 10.3 %collective-permute-start.3 = (bf16[64,1664]{1,0:T(8,128)(2,1)}, bf16[64,1664]{1,0:T(8,128)(2,1)S(1)}, u32[]{:S(2)}, u32[]{:S(2)}) collective-permute-start(bf16[64,1664]{1,0:T(8,128)(2,1)} %param.14), channel_id=1, source_target_pairs={{0,2},{1,3},{2,4},{3,5},{4,6},{5,7},{6,0},{7,1},{8,10},{9,11},{10,... | collective-permute-start | bytes 638984 | tf_op jit(solution)/shard_map/ppermute | solution.py:38
  13.1 16.8 %collective-permute-start.5 = (bf16[64,1664]{1,0:T(8,128)(2,1)}, bf16[64,1664]{1,0:T(8,128)(2,1)S(1)}, u32[]{:S(2)}, u32[]{:S(2)}) collective-permute-start(bf16[64,1664]{1,0:T(8,128)(2,1)} %param.14), channel_id=1, source_target_pairs={{0,4},{1,5},{2,6},{3,7},{4,0},{5,1},{6,2},{7,3},{8,12},{9,13},{10,... | collective-permute-start | bytes 638984 | tf_op jit(solution)/shard_map/ppermute | solution.py:38
  14.1 17.4 %collective-permute-start.8 = (bf16[416,624]{1,0:T(8,128)(2,1)}, bf16[416,624]{1,0:T(8,128)(2,1)S(1)}, u32[]{:S(2)}, u32[]{:S(2)}) collective-permute-start(bf16[416,624]{1,0:T(8,128)(2,1)} %refs_0_.1), channel_id=1, source_target_pairs={{0,16},{8,24},{16,0},{24,8},{1,17},{9,25},{17,1},{25,9},{2,18},{10... | collective-permute-start | bytes 1557512 | tf_op jit(solution)/shard_map/ppermute | solution.py:136
  17.6 58.9 %all-gather.10.cloned.1.call-start = ((), (), s32[]{:S(2)}) async-start(), calls=%async_computation.1 | async-start | bytes 4259840 | tf_op jit(solution)/shard_map/all_gather | solution.py:301
  19.8 16.9 %collective-permute-start.7 = (bf16[416,624]{1,0:T(8,128)(2,1)}, bf16[416,624]{1,0:T(8,128)(2,1)S(1)}, u32[]{:S(2)}, u32[]{:S(2)}) collective-permute-start(bf16[416,624]{1,0:T(8,128)(2,1)} %refs_0_.1), channel_id=1, source_target_pairs={{0,8},{8,0},{16,24},{24,16},{1,9},{9,1},{17,25},{25,17},{2,10},{10... | collective-permute-start | bytes 1557512 | tf_op jit(solution)/shard_map/ppermute | solution.py:144
  19.9 11.5 %collective-permute-start.2 = (bf16[64,1664]{1,0:T(8,128)(2,1)S(1)}, bf16[64,1664]{1,0:T(8,128)(2,1)S(1)}, u32[]{:S(2)}, u32[]{:S(2)}) collective-permute-start(bf16[64,1664]{1,0:T(8,128)(2,1)S(1)} %collective-permute-done.1), channel_id=1, source_target_pairs={{0,1},{1,0},{2,3},{3,2},{4,5},{5,4},{6,7},{7,6},{8,9},{9,8},{10,11... | collective-permute-start | bytes 638984 | tf_op jit(solution)/shard_map/ppermute | solution.py:38
  23.3 9.3 %collective-permute-start.4 = (bf16[64,1664]{1,0:T(8,128)(2,1)S(1)}, bf16[64,1664]{1,0:T(8,128)(2,1)S(1)}, u32[]{:S(2)}, u32[]{:S(2)}) collective-permute-start(bf16[64,1664]{1,0:T(8,128)(2,1)S(1)} %collective-permute-done.3), channel_id=1, source_target_pairs={{0,1},{1,0},{2,3},{3,2},{4,5},{5,4},{6,7},{7,6},{8,9},{9,8},{10,11... | collective-permute-start | bytes 638984 | tf_op jit(solution)/shard_map/ppermute | solution.py:38
  40.2 66.0 %all-gather.12.cloned.1.call-start = ((), (), s32[]{:S(2)}) async-start(), calls=%async_computation.2 | async-start | bytes 4259840 | tf_op jit(solution)/shard_map/all_gather | solution.py:301
  47.1 8.2 %collective-permute-start.11 = (bf16[64,1664]{1,0:T(8,128)(2,1)S(1)}, bf16[64,1664]{1,0:T(8,128)(2,1)S(1)}, u32[]{:S(2)}, u32[]{:S(2)}) collective-permute-start(bf16[64,1664]{1,0:T(8,128)(2,1)S(1)} %get-tuple-element.60), channel_id=1, source_target_pairs={{0,1},{1,0},{2,3},{3,2},{4,5},{5,4},{6,7},{7,6},{8,9},{9,8},{10,11... | collective-permute-start | bytes 638984 | tf_op jit(solution)/shard_map/ppermute | solution.py:38
  48.0 11.9 %collective-permute-start.13 = (bf16[64,1664]{1,0:T(8,128)(2,1)S(1)}, bf16[64,1664]{1,0:T(8,128)(2,1)S(1)}, u32[]{:S(2)}, u32[]{:S(2)}) collective-permute-start(bf16[64,1664]{1,0:T(8,128)(2,1)S(1)} %get-tuple-element.62), channel_id=1, source_target_pairs={{0,1},{1,0},{2,3},{3,2},{4,5},{5,4},{6,7},{7,6},{8,9},{9,8},{10,11... | collective-permute-start | bytes 638984 | tf_op jit(solution)/shard_map/ppermute | solution.py:38
  49.1 16.8 %collective-permute-start.15 = (bf16[64,1664]{1,0:T(8,128)(2,1)S(1)}, bf16[64,1664]{1,0:T(8,128)(2,1)S(1)}, u32[]{:S(2)}, u32[]{:S(2)}) collective-permute-start(bf16[64,1664]{1,0:T(8,128)(2,1)S(1)} %get-tuple-element.64), channel_id=1, source_target_pairs={{0,1},{1,0},{2,3},{3,2},{4,5},{5,4},{6,7},{7,6},{8,9},{9,8},{10,11... | collective-permute-start | bytes 638984 | tf_op jit(solution)/shard_map/ppermute | solution.py:38
  50.0 20.2 %collective-permute-start.10 = (bf16[64,1664]{1,0:T(8,128)(2,1)S(1)}, bf16[64,1664]{1,0:T(8,128)(2,1)S(1)}, u32[]{:S(2)}, u32[]{:S(2)}) collective-permute-start(bf16[64,1664]{1,0:T(8,128)(2,1)S(1)} %get-tuple-element.58), channel_id=1, source_target_pairs={{0,1},{1,0},{2,3},{3,2},{4,5},{5,4},{6,7},{7,6},{8,9},{9,8},{10,11... | collective-permute-start | bytes 638984 | tf_op jit(solution)/shard_map/ppermute | solution.py:38
  57.8 12.4 %collective-permute-start.12 = (bf16[64,1664]{1,0:T(8,128)(2,1)}, bf16[64,1664]{1,0:T(8,128)(2,1)S(1)}, u32[]{:S(2)}, u32[]{:S(2)}) collective-permute-start(bf16[64,1664]{1,0:T(8,128)(2,1)} %shard_map.138), channel_id=1, source_target_pairs={{0,4},{1,5},{2,6},{3,7},{4,0},{5,1},{6,2},{7,3},{8,12},{9,13},{10,... | collective-permute-start | bytes 638984 | tf_op jit(solution)/shard_map/ppermute | solution.py:38
  62.4 9.5 %collective-permute-start.14 = (bf16[64,1664]{1,0:T(8,128)(2,1)}, bf16[64,1664]{1,0:T(8,128)(2,1)S(1)}, u32[]{:S(2)}, u32[]{:S(2)}) collective-permute-start(bf16[64,1664]{1,0:T(8,128)(2,1)} %shard_map.139), channel_id=1, source_target_pairs={{0,6},{1,7},{2,0},{3,1},{4,2},{5,3},{6,4},{7,5},{8,14},{9,15},{10,... | collective-permute-start | bytes 638984 | tf_op jit(solution)/shard_map/ppermute | solution.py:38
  68.4 7.9 %collective-permute-start.16 = (bf16[64,1664]{1,0:T(8,128)(2,1)}, bf16[64,1664]{1,0:T(8,128)(2,1)S(1)}, u32[]{:S(2)}, u32[]{:S(2)}) collective-permute-start(bf16[64,1664]{1,0:T(8,128)(2,1)} %shard_map.140), channel_id=1, source_target_pairs={{0,2},{1,3},{2,4},{3,5},{4,6},{5,7},{6,0},{7,1},{8,10},{9,11},{10,... | collective-permute-start | bytes 638984 | tf_op jit(solution)/shard_map/ppermute | solution.py:38
  76.5 72.6 %all-gather.14.cloned.1.call-start = ((), (), s32[]{:S(2)}) async-start(), calls=%async_computation.3 | async-start | bytes 3461120 | tf_op jit(solution)/shard_map/all_gather | solution.py:301
  76.6 23.3 %collective-permute-start.17 = (bf16[64,1664]{1,0:T(8,128)(2,1)S(1)}, bf16[64,1664]{1,0:T(8,128)(2,1)S(1)}, u32[]{:S(2)}, u32[]{:S(2)}) collective-permute-start(bf16[64,1664]{1,0:T(8,128)(2,1)S(1)} %add_convert_fusion.3), channel_id=1, source_target_pairs={{0,1},{1,0},{2,3},{3,2},{4,5},{5,4},{6,7},{7,6},{8,9},{9,8},{10,11... | collective-permute-start | bytes 638984 | tf_op jit(solution)/shard_map/ppermute | solution.py:38
  77.2 8.7 %collective-permute-start.18 = (bf16[64,1664]{1,0:T(8,128)(2,1)S(1)}, bf16[64,1664]{1,0:T(8,128)(2,1)S(1)}, u32[]{:S(2)}, u32[]{:S(2)}) collective-permute-start(bf16[64,1664]{1,0:T(8,128)(2,1)S(1)} %add_convert_fusion.3), channel_id=1, source_target_pairs={{0,6},{1,7},{2,0},{3,1},{4,2},{5,3},{6,4},{7,5},{8,14},{9,15},{10,... | collective-permute-start | bytes 638984 | tf_op jit(solution)/shard_map/ppermute | solution.py:38
  80.2 10.7 %collective-permute-start.20 = (bf16[64,1664]{1,0:T(8,128)(2,1)S(1)}, bf16[64,1664]{1,0:T(8,128)(2,1)S(1)}, u32[]{:S(2)}, u32[]{:S(2)}) collective-permute-start(bf16[64,1664]{1,0:T(8,128)(2,1)S(1)} %add_convert_fusion.3), channel_id=1, source_target_pairs={{0,2},{1,3},{2,4},{3,5},{4,6},{5,7},{6,0},{7,1},{8,10},{9,11},{10,... | collective-permute-start | bytes 638984 | tf_op jit(solution)/shard_map/ppermute | solution.py:38
  80.2 18.2 %collective-permute-start.22 = (bf16[64,1664]{1,0:T(8,128)(2,1)S(1)}, bf16[64,1664]{1,0:T(8,128)(2,1)S(1)}, u32[]{:S(2)}, u32[]{:S(2)}) collective-permute-start(bf16[64,1664]{1,0:T(8,128)(2,1)S(1)} %add_convert_fusion.3), channel_id=1, source_target_pairs={{0,4},{1,5},{2,6},{3,7},{4,0},{5,1},{6,2},{7,3},{8,12},{9,13},{10,... | collective-permute-start | bytes 638984 | tf_op jit(solution)/shard_map/ppermute | solution.py:38
  85.9 14.0 %collective-permute-start.19 = (bf16[64,1664]{1,0:T(8,128)(2,1)S(1)}, bf16[64,1664]{1,0:T(8,128)(2,1)S(1)}, u32[]{:S(2)}, u32[]{:S(2)}) collective-permute-start(bf16[64,1664]{1,0:T(8,128)(2,1)S(1)} %collective-permute-done.18), channel_id=1, source_target_pairs={{0,1},{1,0},{2,3},{3,2},{4,5},{5,4},{6,7},{7,6},{8,9},{9,8},{10,11... | collective-permute-start | bytes 638984 | tf_op jit(solution)/shard_map/ppermute | solution.py:38
  90.9 9.1 %collective-permute-start.21 = (bf16[64,1664]{1,0:T(8,128)(2,1)S(1)}, bf16[64,1664]{1,0:T(8,128)(2,1)S(1)}, u32[]{:S(2)}, u32[]{:S(2)}) collective-permute-start(bf16[64,1664]{1,0:T(8,128)(2,1)S(1)} %collective-permute-done.20), channel_id=1, source_target_pairs={{0,1},{1,0},{2,3},{3,2},{4,5},{5,4},{6,7},{7,6},{8,9},{9,8},{10,11... | collective-permute-start | bytes 638984 | tf_op jit(solution)/shard_map/ppermute | solution.py:38
  106.3 76.0 %all-gather.16.cloned.1.call-start = ((), (), s32[]{:S(2)}) async-start(), calls=%async_computation.4 | async-start | bytes 2662400 | tf_op jit(solution)/shard_map/all_gather | solution.py:301
  119.0 8.1 %collective-permute-start.25 = (bf16[64,1664]{1,0:T(8,128)(2,1)S(1)}, bf16[64,1664]{1,0:T(8,128)(2,1)S(1)}, u32[]{:S(2)}, u32[]{:S(2)}) collective-permute-start(bf16[64,1664]{1,0:T(8,128)(2,1)S(1)} %get-tuple-element.74), channel_id=1, source_target_pairs={{0,1},{1,0},{2,3},{3,2},{4,5},{5,4},{6,7},{7,6},{8,9},{9,8},{10,11... | collective-permute-start | bytes 638984 | tf_op jit(solution)/shard_map/ppermute | solution.py:38
  120.4 11.5 %collective-permute-start.27 = (bf16[64,1664]{1,0:T(8,128)(2,1)}, bf16[64,1664]{1,0:T(8,128)(2,1)S(1)}, u32[]{:S(2)}, u32[]{:S(2)}) collective-permute-start(bf16[64,1664]{1,0:T(8,128)(2,1)} %get-tuple-element.76), channel_id=1, source_target_pairs={{0,1},{1,0},{2,3},{3,2},{4,5},{5,4},{6,7},{7,6},{8,9},{9,8},{10,11... | collective-permute-start | bytes 638984 | tf_op jit(solution)/shard_map/ppermute | solution.py:38
  121.0 16.4 %collective-permute-start.29 = (bf16[64,1664]{1,0:T(8,128)(2,1)S(1)}, bf16[64,1664]{1,0:T(8,128)(2,1)S(1)}, u32[]{:S(2)}, u32[]{:S(2)}) collective-permute-start(bf16[64,1664]{1,0:T(8,128)(2,1)S(1)} %get-tuple-element.78), channel_id=1, source_target_pairs={{0,1},{1,0},{2,3},{3,2},{4,5},{5,4},{6,7},{7,6},{8,9},{9,8},{10,11... | collective-permute-start | bytes 638984 | tf_op jit(solution)/shard_map/ppermute | solution.py:38
  122.5 19.1 %collective-permute-start.24 = (bf16[64,1664]{1,0:T(8,128)(2,1)S(1)}, bf16[64,1664]{1,0:T(8,128)(2,1)S(1)}, u32[]{:S(2)}, u32[]{:S(2)}) collective-permute-start(bf16[64,1664]{1,0:T(8,128)(2,1)S(1)} %get-tuple-element.72), channel_id=1, source_target_pairs={{0,1},{1,0},{2,3},{3,2},{4,5},{5,4},{6,7},{7,6},{8,9},{9,8},{10,11... | collective-permute-start | bytes 638984 | tf_op jit(solution)/shard_map/ppermute | solution.py:38
  129.5 12.5 %collective-permute-start.26 = (bf16[64,1664]{1,0:T(8,128)(2,1)}, bf16[64,1664]{1,0:T(8,128)(2,1)S(1)}, u32[]{:S(2)}, u32[]{:S(2)}) collective-permute-start(bf16[64,1664]{1,0:T(8,128)(2,1)} %shard_map.142), channel_id=1, source_target_pairs={{0,4},{1,5},{2,6},{3,7},{4,0},{5,1},{6,2},{7,3},{8,12},{9,13},{10,... | collective-permute-start | bytes 638984 | tf_op jit(solution)/shard_map/ppermute | solution.py:38
  134.3 9.4 %collective-permute-start.28 = (bf16[64,1664]{1,0:T(8,128)(2,1)}, bf16[64,1664]{1,0:T(8,128)(2,1)S(1)}, u32[]{:S(2)}, u32[]{:S(2)}) collective-permute-start(bf16[64,1664]{1,0:T(8,128)(2,1)} %shard_map.143), channel_id=1, source_target_pairs={{0,6},{1,7},{2,0},{3,1},{4,2},{5,3},{6,4},{7,5},{8,14},{9,15},{10,... | collective-permute-start | bytes 638984 | tf_op jit(solution)/shard_map/ppermute | solution.py:38
  139.8 8.2 %collective-permute-start.30 = (bf16[64,1664]{1,0:T(8,128)(2,1)}, bf16[64,1664]{1,0:T(8,128)(2,1)S(1)}, u32[]{:S(2)}, u32[]{:S(2)}) collective-permute-start(bf16[64,1664]{1,0:T(8,128)(2,1)} %shard_map.144), channel_id=1, source_target_pairs={{0,2},{1,3},{2,4},{3,5},{4,6},{5,7},{6,0},{7,1},{8,10},{9,11},{10,... | collective-permute-start | bytes 638984 | tf_op jit(solution)/shard_map/ppermute | solution.py:38
  149.9 13.3 %collective-permute-start.31 = (bf16[16,6656]{1,0:T(8,128)(2,1)S(1)}, bf16[16,6656]{1,0:T(8,128)(2,1)}, u32[]{:S(2)}, u32[]{:S(2)}) collective-permute-start(bf16[16,6656]{1,0:T(8,128)(2,1)S(1)} %reshape.275), channel_id=1, source_target_pairs={{0,1},{1,0},{2,3},{3,2},{4,5},{5,4},{6,7},{7,6},{8,9},{9,8},{10,11... | collective-permute-start | bytes 638984 | tf_op jit(solution)/shard_map/ppermute | solution.py:38
  151.6 11.0 %collective-permute-start.32 = (bf16[16,6656]{1,0:T(8,128)(2,1)S(1)}, bf16[16,6656]{1,0:T(8,128)(2,1)}, u32[]{:S(2)}, u32[]{:S(2)}) collective-permute-start(bf16[16,6656]{1,0:T(8,128)(2,1)S(1)} %reshape.275), channel_id=1, source_target_pairs={{0,6},{1,7},{2,0},{3,1},{4,2},{5,3},{6,4},{7,5},{8,14},{9,15},{10,... | collective-permute-start | bytes 638984 | tf_op jit(solution)/shard_map/ppermute | solution.py:38
  157.0 11.4 %collective-permute-start.34 = (bf16[16,6656]{1,0:T(8,128)(2,1)S(1)}, bf16[16,6656]{1,0:T(8,128)(2,1)S(1)}, u32[]{:S(2)}, u32[]{:S(2)}) collective-permute-start(bf16[16,6656]{1,0:T(8,128)(2,1)S(1)} %reshape.275), channel_id=1, source_target_pairs={{0,2},{1,3},{2,4},{3,5},{4,6},{5,7},{6,0},{7,1},{8,10},{9,11},{10,... | collective-permute-start | bytes 638984 | tf_op jit(solution)/shard_map/ppermute | solution.py:38
  157.1 17.9 %collective-permute-start.36 = (bf16[16,6656]{1,0:T(8,128)(2,1)S(1)}, bf16[16,6656]{1,0:T(8,128)(2,1)S(1)}, u32[]{:S(2)}, u32[]{:S(2)}) collective-permute-start(bf16[16,6656]{1,0:T(8,128)(2,1)S(1)} %reshape.275), channel_id=1, source_target_pairs={{0,4},{1,5},{2,6},{3,7},{4,0},{5,1},{6,2},{7,3},{8,12},{9,13},{10,... | collective-permute-start | bytes 638984 | tf_op jit(solution)/shard_map/ppermute | solution.py:38
  158.2 78.9 %all-gather.18.cloned.1.call-start = ((), (), s32[]{:S(2)}) async-start(), calls=%async_computation.5 | async-start | bytes 4259840 | tf_op jit(solution)/shard_map/all_gather | solution.py:301
  162.6 12.9 %collective-permute-start.33 = (bf16[16,6656]{1,0:T(8,128)(2,1)}, bf16[16,6656]{1,0:T(8,128)(2,1)S(1)}, u32[]{:S(2)}, u32[]{:S(2)}) collective-permute-start(bf16[16,6656]{1,0:T(8,128)(2,1)} %collective-permute-done.32), channel_id=1, source_target_pairs={{0,1},{1,0},{2,3},{3,2},{4,5},{5,4},{6,7},{7,6},{8,9},{9,8},{10,11... | collective-permute-start | bytes 638984 | tf_op jit(solution)/shard_map/ppermute | solution.py:38
  182.3 121.4 %all-gather.20.cloned.1.call-start = ((), (), s32[]{:S(2)}) async-start(), calls=%async_computation.6 | async-start | bytes 4259840 | tf_op jit(solution)/shard_map/all_gather | solution.py:301
  198.3 12.6 %collective-permute-start.46 = (bf16[80,1664]{1,0:T(8,128)(2,1)S(1)}, bf16[80,1664]{1,0:T(8,128)(2,1)S(1)}, u32[]{:S(2)}, u32[]{:S(2)}) collective-permute-start(bf16[80,1664]{1,0:T(8,128)(2,1)S(1)} %get-tuple-element.117), channel_id=1, source_target_pairs={{0,6},{1,7},{2,0},{3,1},{4,2},{5,3},{6,4},{7,5},{8,14},{9,15},{10,... | collective-permute-start | bytes 798728 | tf_op jit(solution)/shard_map/ppermute | solution.py:38
  199.8 13.0 %collective-permute-start.48 = (bf16[80,1664]{1,0:T(8,128)(2,1)S(1)}, bf16[80,1664]{1,0:T(8,128)(2,1)S(1)}, u32[]{:S(2)}, u32[]{:S(2)}) collective-permute-start(bf16[80,1664]{1,0:T(8,128)(2,1)S(1)} %get-tuple-element.117), channel_id=1, source_target_pairs={{0,2},{1,3},{2,4},{3,5},{4,6},{5,7},{6,0},{7,1},{8,10},{9,11},{10,... | collective-permute-start | bytes 798728 | tf_op jit(solution)/shard_map/ppermute | solution.py:38
  200.4 20.6 %collective-permute-start.50 = (bf16[80,1664]{1,0:T(8,128)(2,1)S(1)}, bf16[80,1664]{1,0:T(8,128)(2,1)S(1)}, u32[]{:S(2)}, u32[]{:S(2)}) collective-permute-start(bf16[80,1664]{1,0:T(8,128)(2,1)S(1)} %get-tuple-element.117), channel_id=1, source_target_pairs={{0,4},{1,5},{2,6},{3,7},{4,0},{5,1},{6,2},{7,3},{8,12},{9,13},{10,... | collective-permute-start | bytes 798728 | tf_op jit(solution)/shard_map/ppermute | solution.py:38
  200.7 20.8 %collective-permute-start.45 = (bf16[80,1664]{1,0:T(8,128)(2,1)S(1)}, bf16[80,1664]{1,0:T(8,128)(2,1)S(1)}, u32[]{:S(2)}, u32[]{:S(2)}) collective-permute-start(bf16[80,1664]{1,0:T(8,128)(2,1)S(1)} %get-tuple-element.117), channel_id=1, source_target_pairs={{0,1},{1,0},{2,3},{3,2},{4,5},{5,4},{6,7},{7,6},{8,9},{9,8},{10,11... | collective-permute-start | bytes 798728 | tf_op jit(solution)/shard_map/ppermute | solution.py:38
  210.8 10.6 %collective-permute-start.47 = (bf16[80,1664]{1,0:T(8,128)(2,1)S(1)}, bf16[80,1664]{1,0:T(8,128)(2,1)S(1)}, u32[]{:S(2)}, u32[]{:S(2)}) collective-permute-start(bf16[80,1664]{1,0:T(8,128)(2,1)S(1)} %collective-permute-done.46), channel_id=1, source_target_pairs={{0,1},{1,0},{2,3},{3,2},{4,5},{5,4},{6,7},{7,6},{8,9},{9,8},{10,11... | collective-permute-start | bytes 798728 | tf_op jit(solution)/shard_map/ppermute | solution.py:38
  212.8 8.7 %collective-permute-start.49 = (bf16[80,1664]{1,0:T(8,128)(2,1)S(1)}, bf16[80,1664]{1,0:T(8,128)(2,1)S(1)}, u32[]{:S(2)}, u32[]{:S(2)}) collective-permute-start(bf16[80,1664]{1,0:T(8,128)(2,1)S(1)} %collective-permute-done.48), channel_id=1, source_target_pairs={{0,1},{1,0},{2,3},{3,2},{4,5},{5,4},{6,7},{7,6},{8,9},{9,8},{10,11... | collective-permute-start | bytes 798728 | tf_op jit(solution)/shard_map/ppermute | solution.py:38
  240.4 9.3 %collective-permute-start.53 = (bf16[80,1664]{1,0:T(8,128)(2,1)S(1)}, bf16[80,1664]{1,0:T(8,128)(2,1)S(1)}, u32[]{:S(2)}, u32[]{:S(2)}) collective-permute-start(bf16[80,1664]{1,0:T(8,128)(2,1)S(1)} %get-tuple-element.90), channel_id=1, source_target_pairs={{0,1},{1,0},{2,3},{3,2},{4,5},{5,4},{6,7},{7,6},{8,9},{9,8},{10,11... | collective-permute-start | bytes 798728 | tf_op jit(solution)/shard_map/ppermute | solution.py:38
  240.8 16.1 %collective-permute-start.55 = (bf16[80,1664]{1,0:T(8,128)(2,1)S(1)}, bf16[80,1664]{1,0:T(8,128)(2,1)S(1)}, u32[]{:S(2)}, u32[]{:S(2)}) collective-permute-start(bf16[80,1664]{1,0:T(8,128)(2,1)S(1)} %get-tuple-element.92), channel_id=1, source_target_pairs={{0,1},{1,0},{2,3},{3,2},{4,5},{5,4},{6,7},{7,6},{8,9},{9,8},{10,11... | collective-permute-start | bytes 798728 | tf_op jit(solution)/shard_map/ppermute | solution.py:38
  242.4 20.4 %collective-permute-start.57 = (bf16[80,1664]{1,0:T(8,128)(2,1)S(1)}, bf16[80,1664]{1,0:T(8,128)(2,1)S(1)}, u32[]{:S(2)}, u32[]{:S(2)}) collective-permute-start(bf16[80,1664]{1,0:T(8,128)(2,1)S(1)} %get-tuple-element.94), channel_id=1, source_target_pairs={{0,1},{1,0},{2,3},{3,2},{4,5},{5,4},{6,7},{7,6},{8,9},{9,8},{10,11... | collective-permute-start | bytes 798728 | tf_op jit(solution)/shard_map/ppermute | solution.py:38
  242.8 22.5 %collective-permute-start.52 = (bf16[80,1664]{1,0:T(8,128)(2,1)S(1)}, bf16[80,1664]{1,0:T(8,128)(2,1)S(1)}, u32[]{:S(2)}, u32[]{:S(2)}) collective-permute-start(bf16[80,1664]{1,0:T(8,128)(2,1)S(1)} %get-tuple-element.88), channel_id=1, source_target_pairs={{0,1},{1,0},{2,3},{3,2},{4,5},{5,4},{6,7},{7,6},{8,9},{9,8},{10,11... | collective-permute-start | bytes 798728 | tf_op jit(solution)/shard_map/ppermute | solution.py:38
  252.2 15.1 %collective-permute-start.54 = (bf16[80,1664]{1,0:T(8,128)(2,1)}, bf16[80,1664]{1,0:T(8,128)(2,1)S(1)}, u32[]{:S(2)}, u32[]{:S(2)}) collective-permute-start(bf16[80,1664]{1,0:T(8,128)(2,1)} %shard_map.147), channel_id=1, source_target_pairs={{0,4},{1,5},{2,6},{3,7},{4,0},{5,1},{6,2},{7,3},{8,12},{9,13},{10,... | collective-permute-start | bytes 798728 | tf_op jit(solution)/shard_map/ppermute | solution.py:38
  259.4 8.8 %collective-permute-start.56 = (bf16[80,1664]{1,0:T(8,128)(2,1)}, bf16[80,1664]{1,0:T(8,128)(2,1)S(1)}, u32[]{:S(2)}, u32[]{:S(2)}) collective-permute-start(bf16[80,1664]{1,0:T(8,128)(2,1)} %shard_map.148), channel_id=1, source_target_pairs={{0,6},{1,7},{2,0},{3,1},{4,2},{5,3},{6,4},{7,5},{8,14},{9,15},{10,... | collective-permute-start | bytes 798728 | tf_op jit(solution)/shard_map/ppermute | solution.py:38
  265.3 11.0 %collective-permute-start.58 = (bf16[80,1664]{1,0:T(8,128)(2,1)}, bf16[80,1664]{1,0:T(8,128)(2,1)S(1)}, u32[]{:S(2)}, u32[]{:S(2)}) collective-permute-start(bf16[80,1664]{1,0:T(8,128)(2,1)} %shard_map.149), channel_id=1, source_target_pairs={{0,2},{1,3},{2,4},{3,5},{4,6},{5,7},{6,0},{7,1},{8,10},{9,11},{10,... | collective-permute-start | bytes 798728 | tf_op jit(solution)/shard_map/ppermute | solution.py:38
  277.7 9.5 %collective-permute-start.60 = (bf16[80,1664]{1,0:T(8,128)(2,1)S(1)}, bf16[80,1664]{1,0:T(8,128)(2,1)S(1)}, u32[]{:S(2)}, u32[]{:S(2)}) collective-permute-start(bf16[80,1664]{1,0:T(8,128)(2,1)S(1)} %get-tuple-element.106), channel_id=1, source_target_pairs={{0,6},{1,7},{2,0},{3,1},{4,2},{5,3},{6,4},{7,5},{8,14},{9,15},{10,... | collective-permute-start | bytes 798728 | tf_op jit(solution)/shard_map/ppermute | solution.py:38
  282.2 10.8 %collective-permute-start.62 = (bf16[80,1664]{1,0:T(8,128)(2,1)S(1)}, bf16[80,1664]{1,0:T(8,128)(2,1)S(1)}, u32[]{:S(2)}, u32[]{:S(2)}) collective-permute-start(bf16[80,1664]{1,0:T(8,128)(2,1)S(1)} %get-tuple-element.106), channel_id=1, source_target_pairs={{0,2},{1,3},{2,4},{3,5},{4,6},{5,7},{6,0},{7,1},{8,10},{9,11},{10,... | collective-permute-start | bytes 798728 | tf_op jit(solution)/shard_map/ppermute | solution.py:38
  282.7 14.4 %collective-permute-start.64 = (bf16[80,1664]{1,0:T(8,128)(2,1)S(1)}, bf16[80,1664]{1,0:T(8,128)(2,1)S(1)}, u32[]{:S(2)}, u32[]{:S(2)}) collective-permute-start(bf16[80,1664]{1,0:T(8,128)(2,1)S(1)} %get-tuple-element.106), channel_id=1, source_target_pairs={{0,4},{1,5},{2,6},{3,7},{4,0},{5,1},{6,2},{7,3},{8,12},{9,13},{10,... | collective-permute-start | bytes 798728 | tf_op jit(solution)/shard_map/ppermute | solution.py:38
  286.2 10.9 %collective-permute-start.59 = (bf16[80,1664]{1,0:T(8,128)(2,1)S(1)}, bf16[80,1664]{1,0:T(8,128)(2,1)S(1)}, u32[]{:S(2)}, u32[]{:S(2)}) collective-permute-start(bf16[80,1664]{1,0:T(8,128)(2,1)S(1)} %get-tuple-element.106), channel_id=1, source_target_pairs={{0,1},{1,0},{2,3},{3,2},{4,5},{5,4},{6,7},{7,6},{8,9},{9,8},{10,11... | collective-permute-start | bytes 798728 | tf_op jit(solution)/shard_map/ppermute | solution.py:38
  287.2 10.0 %collective-permute-start.61 = (bf16[80,1664]{1,0:T(8,128)(2,1)S(1)}, bf16[80,1664]{1,0:T(8,128)(2,1)S(1)}, u32[]{:S(2)}, u32[]{:S(2)}) collective-permute-start(bf16[80,1664]{1,0:T(8,128)(2,1)S(1)} %collective-permute-done.60), channel_id=1, source_target_pairs={{0,1},{1,0},{2,3},{3,2},{4,5},{5,4},{6,7},{7,6},{8,9},{9,8},{10,11... | collective-permute-start | bytes 798728 | tf_op jit(solution)/shard_map/ppermute | solution.py:38
  316.2 9.3 %collective-permute-start.69 = (bf16[80,1664]{1,0:T(8,128)(2,1)S(1)}, bf16[80,1664]{1,0:T(8,128)(2,1)S(1)}, u32[]{:S(2)}, u32[]{:S(2)}) collective-permute-start(bf16[80,1664]{1,0:T(8,128)(2,1)S(1)} %get-tuple-element.102), channel_id=1, source_target_pairs={{0,1},{1,0},{2,3},{3,2},{4,5},{5,4},{6,7},{7,6},{8,9},{9,8},{10,11... | collective-permute-start | bytes 798728 | tf_op jit(solution)/shard_map/ppermute | solution.py:38
  318.2 14.9 %collective-permute-start.71 = (bf16[80,1664]{1,0:T(8,128)(2,1)S(1)}, bf16[80,1664]{1,0:T(8,128)(2,1)S(1)}, u32[]{:S(2)}, u32[]{:S(2)}) collective-permute-start(bf16[80,1664]{1,0:T(8,128)(2,1)S(1)} %get-tuple-element.104), channel_id=1, source_target_pairs={{0,1},{1,0},{2,3},{3,2},{4,5},{5,4},{6,7},{7,6},{8,9},{9,8},{10,11... | collective-permute-start | bytes 798728 | tf_op jit(solution)/shard_map/ppermute | solution.py:38
  318.2 17.4 %collective-permute-start.66 = (bf16[80,1664]{1,0:T(8,128)(2,1)S(1)}, bf16[80,1664]{1,0:T(8,128)(2,1)S(1)}, u32[]{:S(2)}, u32[]{:S(2)}) collective-permute-start(bf16[80,1664]{1,0:T(8,128)(2,1)S(1)} %get-tuple-element.98), channel_id=1, source_target_pairs={{0,1},{1,0},{2,3},{3,2},{4,5},{5,4},{6,7},{7,6},{8,9},{9,8},{10,11... | collective-permute-start | bytes 798728 | tf_op jit(solution)/shard_map/ppermute | solution.py:38
  325.1 11.9 %collective-permute-start.68 = (bf16[80,1664]{1,0:T(8,128)(2,1)}, bf16[80,1664]{1,0:T(8,128)(2,1)S(1)}, u32[]{:S(2)}, u32[]{:S(2)}) collective-permute-start(bf16[80,1664]{1,0:T(8,128)(2,1)} %shard_map.151), channel_id=1, source_target_pairs={{0,4},{1,5},{2,6},{3,7},{4,0},{5,1},{6,2},{7,3},{8,12},{9,13},{10,... | collective-permute-start | bytes 798728 | tf_op jit(solution)/shard_map/ppermute | solution.py:38
  327.9 11.7 %collective-permute-start.70 = (bf16[80,1664]{1,0:T(8,128)(2,1)}, bf16[80,1664]{1,0:T(8,128)(2,1)S(1)}, u32[]{:S(2)}, u32[]{:S(2)}) collective-permute-start(bf16[80,1664]{1,0:T(8,128)(2,1)} %shard_map.152), channel_id=1, source_target_pairs={{0,6},{1,7},{2,0},{3,1},{4,2},{5,3},{6,4},{7,5},{8,14},{9,15},{10,... | collective-permute-start | bytes 798728 | tf_op jit(solution)/shard_map/ppermute | solution.py:38
  335.6 8.4 %collective-permute-start.72 = (bf16[80,1664]{1,0:T(8,128)(2,1)}, bf16[80,1664]{1,0:T(8,128)(2,1)S(1)}, u32[]{:S(2)}, u32[]{:S(2)}) collective-permute-start(bf16[80,1664]{1,0:T(8,128)(2,1)} %shard_map.153), channel_id=1, source_target_pairs={{0,2},{1,3},{2,4},{3,5},{4,6},{5,7},{6,0},{7,1},{8,10},{9,11},{10,... | collective-permute-start | bytes 798728 | tf_op jit(solution)/shard_map/ppermute | solution.py:38
  (58 other events, 357.7 us)
Sparse Core Ops, SparseCore 0:
  17.7 19.8 all-gather.7
  40.3 30.3 all-gather.9
  76.7 29.5 all-gather.11
  107.7 26.3 all-gather.13
  158.4 21.7 all-gather.15
  182.4 29.2 all-gather.17
  237.3 31.4 all-gather.19

commit v2 on v1

--- a/solution.py
+++ b/solution.py
@@ -185,13 +185,7 @@
         out_refs[step * tile + at][...] = value[at * rows : (at + 1) * rows].astype(BF)
 
 
-def block_kernel(norm, counts, tile, spots, rows_ref, gain_ref, *refs):
-    ups, downs = refs[: counts[0]], refs[counts[0] : sum(counts)]
-    out_refs, (up, down, up_sems, down_sems) = refs[sum(counts) : -4], refs[-4:]
-    up_copies = load_pieces(spots, ups, up, up_sems)
-    down_copies = load_pieces(spots, downs, down, down_sems)
-    for copy in up_copies + down_copies:
-        copy.wait()
+def block_kernel(norm, tile, rows_ref, gain_ref, up, down, *out_refs):
     for step in range(rows_ref.shape[0] // tile):
         normed = norm(rows_ref[step * tile : (step + 1) * tile, :], gain_ref[...]).astype(BF)
         raised = jnp.dot(normed, up[...], preferred_element_type=F32)
@@ -287,14 +281,19 @@
     )[0]
 
 
-def block_of(norm, rows, gain, ups, downs):
+def block_of(norm, rows, gain, up, down):
     count = lax.axis_size("gy")
     total, width = rows.shape
-    flops = 4 * rows.size * ups[0].shape[1]
-    outs = [(total // count, width)] * count
-    return pieces_call(
-        block_kernel, norm, rows, gain, [ups, downs], block_tile(total), outs, flops
-    )
+    return pl.pallas_call(
+        functools.partial(block_kernel, norm, block_tile(total)),
+        out_shape=[jax.ShapeDtypeStruct((total // count, width), BF)] * count,
+        compiler_params=pltpu.CompilerParams(vmem_limit_bytes=40 * 1024 * 1024),
+        cost_estimate=pl.CostEstimate(
+            flops=4 * rows.size * up.shape[1],
+            bytes_accessed=2 * (up.size + down.size + 2 * rows.size),
+            transcendentals=0,
+        ),
+    )(rows, gain[None, :], up, down)
 
 
 def weight_block(weight):
@@ -371,7 +370,7 @@
     mid_all = relative_gather(enc_mid)
     mid_all, down_block, merge_proj = tied(mid_all, down_block, merge_proj)
     merge_block = weight_block(merge_proj)
-    term = block_of(layer_norm, mid_all, norm_gains[1], [up_block], [down_block])
+    term = block_of(layer_norm, mid_all, norm_gains[1], up_block, down_block)
     enc_out = (enc_mid.astype(F32) + relative_scatter(term)).astype(BF)
     enc_out, merge_block, dec_qkv = tied(enc_out, merge_block, dec_qkv)
     dqkv_block = weight_block(dec_qkv)
@@ -399,7 +398,7 @@
     dec_mid = (dec_in.astype(F32) + summed).astype(BF)
 
     mid_all = relative_gather(dec_mid)
-    term = block_of(rms_norm, mid_all, norm_gains[4], [dup_block], [ddown_block])
+    term = block_of(rms_norm, mid_all, norm_gains[4], dup_block, ddown_block)
     return (dec_mid.astype(F32) + relative_scatter(term)).astype(BF)
 
 

time: 353 us -> 351 us (level)
    pallas_call x4 -> x2, Pallas kernels: 19.6 us -> 6.65 us  [pieces_call(): pl.pallas_call(functools.partial(kernel, norm, counts, tile), out_shape=[...]
    pallas_call x0 -> x2, Pallas kernels: none -> 10.9 us  [block_of(): pl.pallas_call(functools.partial(block_kernel, norm, block_tile(total)),...]
where the time goes in v2:
time: 351 us; the launch traced here: 350 us
  waiting for transfers between devices  148 us (42%)
  starting transfers between devices  97.4 us (28%)
  Pallas kernels  40.6 us (12%)
  local copies, waits for them, and re-layouts  33 us (9%)
  between operations  14.5 us (4%)
  matrix products  9.19 us (3%)
  other arithmetic  7.33 us (2%)
    ppermute x70, waiting for transfers between devices, moved(): return lax.ppermute(value, 'gy', pairs)  146 us
    ppermute x70, starting transfers between devices, moved(): return lax.ppermute(value, 'gy', pairs)  95.3 us
    unnamed x124, local copies, waits for them, and re-layouts  29.3 us
    pallas_call x12, Pallas kernels, added(): pl.pallas_call(add_kernel, out_shape=jax.ShapeDtypeStruct(values[0].shape...  21.6 us
    pallas_call x2, Pallas kernels, block_of(): pl.pallas_call(functools.partial(block_kernel, norm, block_tile(total)),...  10.9 us
  transfers between devices with their start and end apart: 80, of which 43 were waited for; matrix products, arithmetic and copies ran while one was open for 7% of the time, Pallas kernels for 10%

profile of v2, /device:TPU:0, one launch (start us, length us, event | category | flops | bytes accessed | tf_op | source)
XLA Modules:
  0.0 349.7 jit_solution(13033270946730196873)
XLA Ops:
  6.5 5.0 %collective-permute-start.1 = (bf16[64,1664]{1,0:T(8,128)(2,1)}, bf16[64,1664]{1,0:T(8,128)(2,1)S(1)}, u32[]{:S(2)}, u32[]{:S(2)}) collective-permute-start(bf16[64,1664]{1,0:T(8,128)(2,1)} %param.14), channel_id=1, source_target_pairs={{0,6},{1,7},{2,0},{3,1},{4,2},{5,3},{6,4},{7,5},{8,14},{9,15},{10,... | collective-permute-start | bytes 638984 | tf_op jit(solution)/shard_map/ppermute | solution.py:38
  15.6 2.0 pad_maximum_fusion
  21.5 1.8 collective-permute-done.3
  24.5 5.4 %collective-permute-done.5 = bf16[64,1664]{1,0:T(8,128)(2,1)S(1)} collective-permute-done((bf16[64,1664]{1,0:T(8,128)(2,1)}, bf16[64,1664]{1,0:T(8,128)(2,1)S(1)}, u32[]{:S(2)}, u32[]{:S(2)}) %collective-permute-start.5) | collective-permute-done | bytes 213024 | tf_op jit(solution)/shard_map/ppermute | solution.py:38
  32.7 4.0 %collective-permute-done.6 = bf16[64,1664]{1,0:T(8,128)(2,1)S(1)} collective-permute-done((bf16[64,1664]{1,0:T(8,128)(2,1)S(1)}, bf16[64,1664]{1,0:T(8,128)(2,1)S(1)}, u32[]{:S(2)}, u32[]{:S(2)}) %collective-permute-start.6) | collective-permute-done | bytes 213024 | tf_op jit(solution)/shard_map/ppermute | solution.py:38
  36.8 3.4 shard_map.136
  51.2 4.1 %collective-permute-done.11.refs_1_ = bf16[64,1664]{1,0:T(8,128)(2,1)S(1)} collective-permute-done((bf16[64,1664]{1,0:T(8,128)(2,1)S(1)}, bf16[64,1664]{1,0:T(8,128)(2,1)S(1)}, u32[]{:S(2)}, u32[]{:S(2)}) %collective-permute-start.11) | collective-permute-done | bytes 213024 | tf_op jit(solution)/shard_map/ppermute | solution.py:38
  56.0 1.8 shard_map.138
  57.8 1.9 collective-permute-start.12
  60.6 1.8 shard_map.139
  62.4 3.6 %collective-permute-start.14 = (bf16[64,1664]{1,0:T(8,128)(2,1)}, bf16[64,1664]{1,0:T(8,128)(2,1)S(1)}, u32[]{:S(2)}, u32[]{:S(2)}) collective-permute-start(bf16[64,1664]{1,0:T(8,128)(2,1)} %shard_map.139), channel_id=1, source_target_pairs={{0,6},{1,7},{2,0},{3,1},{4,2},{5,3},{6,4},{7,5},{8,14},{9,15},{10,... | collective-permute-start | bytes 638984 | tf_op jit(solution)/shard_map/ppermute | solution.py:38
  68.4 1.8 collective-permute-start.16
  71.9 4.5 %collective-permute-done.16 = bf16[64,1664]{1,0:T(8,128)(2,1)S(1)} collective-permute-done((bf16[64,1664]{1,0:T(8,128)(2,1)}, bf16[64,1664]{1,0:T(8,128)(2,1)S(1)}, u32[]{:S(2)}, u32[]{:S(2)}) %collective-permute-start.16) | collective-permute-done | bytes 213024 | tf_op jit(solution)/shard_map/ppermute | solution.py:38
  77.2 3.0 collective-permute-start.18
  81.4 4.5 %collective-permute-done.18 = bf16[64,1664]{1,0:T(8,128)(2,1)S(1)} collective-permute-done((bf16[64,1664]{1,0:T(8,128)(2,1)S(1)}, bf16[64,1664]{1,0:T(8,128)(2,1)S(1)}, u32[]{:S(2)}, u32[]{:S(2)}) %collective-permute-start.18) | collective-permute-done | bytes 213024 | tf_op jit(solution)/shard_map/ppermute | solution.py:38
  87.4 3.5 collective-permute-done.20
  92.2 6.2 %collective-permute-done.22 = bf16[64,1664]{1,0:T(8,128)(2,1)S(1)} collective-permute-done((bf16[64,1664]{1,0:T(8,128)(2,1)S(1)}, bf16[64,1664]{1,0:T(8,128)(2,1)S(1)}, u32[]{:S(2)}, u32[]{:S(2)}) %collective-permute-start.22) | collective-permute-done | bytes 213024 | tf_op jit(solution)/shard_map/ppermute | solution.py:38
  100.1 4.2 %collective-permute-done.23 = bf16[64,1664]{1,0:T(8,128)(2,1)S(1)} collective-permute-done((bf16[64,1664]{1,0:T(8,128)(2,1)S(1)}, bf16[64,1664]{1,0:T(8,128)(2,1)S(1)}, u32[]{:S(2)}, u32[]{:S(2)}) %collective-permute-start.23) | collective-permute-done | bytes 213024 | tf_op jit(solution)/shard_map/ppermute | solution.py:38
  104.3 2.0 all-gather.12.cloned.1.call-done.down
  106.5 2.0 copy-done.15
  108.5 2.0 copy-done.17
  110.4 5.5 %shard_map.141 = (bf16[64,1664]{1,0:T(8,128)(2,1)S(1)}, bf16[64,1664]{1,0:T(8,128)(2,1)S(1)}, bf16[64,1664]{1,0:T(8,128)(2,1)S(1)}, bf16[64,1664]{1,0:T(8,128)(2...) custom-call(bf16[512,1664]{1,0:T(8,128)(2,1)S(1)} %constant_dynamic-, ...), custom_call_target="tpu_custom_call" | custom-call | flops 3489660928 | bytes 10223616 | tf_op jit(solution)/shard_map/pallas_call | solution.py:287
  122.0 4.0 %collective-permute-done.25.refs_1_ = bf16[64,1664]{1,0:T(8,128)(2,1)S(1)} collective-permute-done((bf16[64,1664]{1,0:T(8,128)(2,1)S(1)}, bf16[64,1664]{1,0:T(8,128)(2,1)S(1)}, u32[]{:S(2)}, u32[]{:S(2)}) %collective-permute-start.25) | collective-permute-done | bytes 213024 | tf_op jit(solution)/shard_map/ppermute | solution.py:38
  128.5 2.4 collective-permute-start.26
  133.3 3.1 collective-permute-start.28
  142.8 4.3 %collective-permute-done.30 = bf16[64,1664]{1,0:T(8,128)(2,1)S(1)} collective-permute-done((bf16[64,1664]{1,0:T(8,128)(2,1)}, bf16[64,1664]{1,0:T(8,128)(2,1)S(1)}, u32[]{:S(2)}, u32[]{:S(2)}) %collective-permute-start.30) | collective-permute-done | bytes 213024 | tf_op jit(solution)/shard_map/ppermute | solution.py:38
  150.6 5.3 %collective-permute-start.32 = (bf16[16,6656]{1,0:T(8,128)(2,1)S(1)}, bf16[16,6656]{1,0:T(8,128)(2,1)}, u32[]{:S(2)}, u32[]{:S(2)}) collective-permute-start(bf16[16,6656]{1,0:T(8,128)(2,1)S(1)} %reshape.275), channel_id=1, source_target_pairs={{0,6},{1,7},{2,0},{3,1},{4,2},{5,3},{6,4},{7,5},{8,14},{9,15},{10,... | collective-permute-start | bytes 638984 | tf_op jit(solution)/shard_map/ppermute | solution.py:38
  157.3 4.4 %collective-permute-done.32 = bf16[16,6656]{1,0:T(8,128)(2,1)} collective-permute-done((bf16[16,6656]{1,0:T(8,128)(2,1)S(1)}, bf16[16,6656]{1,0:T(8,128)(2,1)}, u32[]{:S(2)}, u32[]{:S(2)}) %collective-permute-start.32) | collective-permute-done | bytes 213024 | tf_op jit(solution)/shard_map/ppermute | solution.py:38
  164.1 3.2 collective-permute-done.34
  167.9 6.0 %collective-permute-done.36 = bf16[16,6656]{1,0:T(8,128)(2,1)S(1)} collective-permute-done((bf16[16,6656]{1,0:T(8,128)(2,1)S(1)}, bf16[16,6656]{1,0:T(8,128)(2,1)S(1)}, u32[]{:S(2)}, u32[]{:S(2)}) %collective-permute-start.36) | collective-permute-done | bytes 213024 | tf_op jit(solution)/shard_map/ppermute | solution.py:38
  174.6 5.7 %collective-permute-done.37 = bf16[16,6656]{1,0:T(8,128)(2,1)S(1)} collective-permute-done((bf16[16,6656]{1,0:T(8,128)(2,1)S(1)}, bf16[16,6656]{1,0:T(8,128)(2,1)S(1)}, u32[]{:S(2)}, u32[]{:S(2)}) %collective-permute-start.37) | collective-permute-done | bytes 213024 | tf_op jit(solution)/shard_map/ppermute | solution.py:38
  181.7 2.5 collective-permute-start.39
  188.7 2.2 collective-permute-done.43
  193.0 3.5 %collective-permute-done.42 = bf16[208,128]{1,0:T(8,128)(2,1)S(1)} collective-permute-done((bf16[208,128]{1,0:T(8,128)(2,1)S(1)}, bf16[208,128]{1,0:T(8,128)(2,1)S(1)}, u32[]{:S(2)}, u32[]{:S(2)}) %collective-permute-start.42) | collective-permute-done | bytes 53280 | tf_op jit(solution)/shard_map/ppermute | solution.py:38
  201.4 8.4 %collective-permute-done.46 = bf16[80,1664]{1,0:T(8,128)(2,1)S(1)} collective-permute-done((bf16[80,1664]{1,0:T(8,128)(2,1)S(1)}, bf16[80,1664]{1,0:T(8,128)(2,1)S(1)}, u32[]{:S(2)}, u32[]{:S(2)}) %collective-permute-start.46) | collective-permute-done | bytes 266272 | tf_op jit(solution)/shard_map/ppermute | solution.py:38
  209.9 1.9 collective-permute-done.48
  212.7 7.3 %collective-permute-done.50 = bf16[80,1664]{1,0:T(8,128)(2,1)S(1)} collective-permute-done((bf16[80,1664]{1,0:T(8,128)(2,1)S(1)}, bf16[80,1664]{1,0:T(8,128)(2,1)S(1)}, u32[]{:S(2)}, u32[]{:S(2)}) %collective-permute-start.50) | collective-permute-done | bytes 266272 | tf_op jit(solution)/shard_map/ppermute | solution.py:38
  220.6 5.7 %collective-permute-done.51 = bf16[80,1664]{1,0:T(8,128)(2,1)S(1)} collective-permute-done((bf16[80,1664]{1,0:T(8,128)(2,1)S(1)}, bf16[80,1664]{1,0:T(8,128)(2,1)S(1)}, u32[]{:S(2)}, u32[]{:S(2)}) %collective-permute-start.51) | collective-permute-done | bytes 266272 | tf_op jit(solution)/shard_map/ppermute | solution.py:38
  226.4 3.3 shard_map.145
  230.6 3.1 fusion.39
  233.7 2.4 fusion.9
  243.4 5.3 %collective-permute-done.53.refs_1_ = bf16[80,1664]{1,0:T(8,128)(2,1)S(1)} collective-permute-done((bf16[80,1664]{1,0:T(8,128)(2,1)S(1)}, bf16[80,1664]{1,0:T(8,128)(2,1)S(1)}, u32[]{:S(2)}, u32[]{:S(2)}) %collective-permute-start.53) | collective-permute-done | bytes 266272 | tf_op jit(solution)/shard_map/ppermute | solution.py:38
  249.4 1.8 shard_map.147
  251.2 4.7 %collective-permute-start.54 = (bf16[80,1664]{1,0:T(8,128)(2,1)}, bf16[80,1664]{1,0:T(8,128)(2,1)S(1)}, u32[]{:S(2)}, u32[]{:S(2)}) collective-permute-start(bf16[80,1664]{1,0:T(8,128)(2,1)} %shard_map.147), channel_id=1, source_target_pairs={{0,4},{1,5},{2,6},{3,7},{4,0},{5,1},{6,2},{7,3},{8,12},{9,13},{10,... | collective-permute-start | bytes 798728 | tf_op jit(solution)/shard_map/ppermute | solution.py:38
  256.6 1.8 shard_map.148
  258.4 3.4 collective-permute-start.56
  262.5 1.8 shard_map.149
  264.3 2.0 collective-permute-done.54
  267.2 8.1 %collective-permute-done.58 = bf16[80,1664]{1,0:T(8,128)(2,1)S(1)} collective-permute-done((bf16[80,1664]{1,0:T(8,128)(2,1)}, bf16[80,1664]{1,0:T(8,128)(2,1)S(1)}, u32[]{:S(2)}, u32[]{:S(2)}) %collective-permute-start.58) | collective-permute-done | bytes 266272 | tf_op jit(solution)/shard_map/ppermute | solution.py:38
  276.6 4.5 %collective-permute-start.60 = (bf16[80,1664]{1,0:T(8,128)(2,1)S(1)}, bf16[80,1664]{1,0:T(8,128)(2,1)S(1)}, u32[]{:S(2)}, u32[]{:S(2)}) collective-permute-start(bf16[80,1664]{1,0:T(8,128)(2,1)S(1)} %get-tuple-element.106), channel_id=1, source_target_pairs={{0,6},{1,7},{2,0},{3,1},{4,2},{5,3},{6,4},{7,5},{8,14},{9,15},{10,... | collective-permute-start | bytes 798728 | tf_op jit(solution)/shard_map/ppermute | solution.py:38
  281.7 3.5 %collective-permute-start.64 = (bf16[80,1664]{1,0:T(8,128)(2,1)S(1)}, bf16[80,1664]{1,0:T(8,128)(2,1)S(1)}, u32[]{:S(2)}, u32[]{:S(2)}) collective-permute-start(bf16[80,1664]{1,0:T(8,128)(2,1)S(1)} %get-tuple-element.106), channel_id=1, source_target_pairs={{0,4},{1,5},{2,6},{3,7},{4,0},{5,1},{6,2},{7,3},{8,12},{9,13},{10,... | collective-permute-start | bytes 798728 | tf_op jit(solution)/shard_map/ppermute | solution.py:38
  287.2 4.7 %collective-permute-done.62 = bf16[80,1664]{1,0:T(8,128)(2,1)S(1)} collective-permute-done((bf16[80,1664]{1,0:T(8,128)(2,1)S(1)}, bf16[80,1664]{1,0:T(8,128)(2,1)S(1)}, u32[]{:S(2)}, u32[]{:S(2)}) %collective-permute-start.62) | collective-permute-done | bytes 266272 | tf_op jit(solution)/shard_map/ppermute | solution.py:38
  292.0 4.1 %collective-permute-done.64 = bf16[80,1664]{1,0:T(8,128)(2,1)S(1)} collective-permute-done((bf16[80,1664]{1,0:T(8,128)(2,1)S(1)}, bf16[80,1664]{1,0:T(8,128)(2,1)S(1)}, u32[]{:S(2)}, u32[]{:S(2)}) %collective-permute-start.64) | collective-permute-done | bytes 266272 | tf_op jit(solution)/shard_map/ppermute | solution.py:38
  296.3 2.1 collective-permute-done.63
  298.4 4.1 %collective-permute-done.65 = bf16[80,1664]{1,0:T(8,128)(2,1)S(1)} collective-permute-done((bf16[80,1664]{1,0:T(8,128)(2,1)S(1)}, bf16[80,1664]{1,0:T(8,128)(2,1)S(1)}, u32[]{:S(2)}, u32[]{:S(2)}) %collective-permute-start.65) | collective-permute-done | bytes 266272 | tf_op jit(solution)/shard_map/ppermute | solution.py:38
  302.6 2.0 copy-done.14
  304.6 2.0 copy-done.16
  306.5 5.4 %shard_map.150 = (bf16[80,1664]{1,0:T(8,128)(2,1)S(1)}, bf16[80,1664]{1,0:T(8,128)(2,1)S(1)}, bf16[80,1664]{1,0:T(8,128)(2,1)S(1)}, bf16[80,1664]{1,0:T(8,128)(2...) custom-call(bf16[640,1664]{1,0:T(8,128)(2,1)S(1)} %constant_dynamic-, ...), custom_call_target="tpu_custom_call" | custom-call | flops 4362076160 | bytes 11075584 | tf_op jit(solution)/shard_map/pallas_call | solution.py:287
  314.1 2.0 collective-permute-start.69
  316.2 2.0 collective-permute-start.66
  318.2 2.4 collective-permute-done.67.refs_1_
  325.9 5.1 %collective-permute-start.70 = (bf16[80,1664]{1,0:T(8,128)(2,1)}, bf16[80,1664]{1,0:T(8,128)(2,1)S(1)}, u32[]{:S(2)}, u32[]{:S(2)}) collective-permute-start(bf16[80,1664]{1,0:T(8,128)(2,1)} %shard_map.152), channel_id=1, source_target_pairs={{0,6},{1,7},{2,0},{3,1},{4,2},{5,3},{6,4},{7,5},{8,14},{9,15},{10,... | collective-permute-start | bytes 798728 | tf_op jit(solution)/shard_map/ppermute | solution.py:38
  334.9 2.6 collective-permute-done.70
  337.6 4.4 %collective-permute-done.72 = bf16[80,1664]{1,0:T(8,128)(2,1)S(1)} collective-permute-done((bf16[80,1664]{1,0:T(8,128)(2,1)}, bf16[80,1664]{1,0:T(8,128)(2,1)S(1)}, u32[]{:S(2)}, u32[]{:S(2)}) %collective-permute-start.72) | collective-permute-done | bytes 266272 | tf_op jit(solution)/shard_map/ppermute | solution.py:38
  (295 shorter events, 102.9 us)
Async XLA Ops:
  6.5 33.6 %all-gather.8.cloned.1.call-start = ((), (), s32[]{:S(2)}) async-start(), calls=%async_computation | async-start | bytes 2129920 | tf_op jit(solution)/shard_map/all_gather | solution.py:300
  6.5 13.3 %collective-permute-start.1 = (bf16[64,1664]{1,0:T(8,128)(2,1)}, bf16[64,1664]{1,0:T(8,128)(2,1)S(1)}, u32[]{:S(2)}, u32[]{:S(2)}) collective-permute-start(bf16[64,1664]{1,0:T(8,128)(2,1)} %param.14), channel_id=1, source_target_pairs={{0,6},{1,7},{2,0},{3,1},{4,2},{5,3},{6,4},{7,5},{8,14},{9,15},{10,... | collective-permute-start | bytes 638984 | tf_op jit(solution)/shard_map/ppermute | solution.py:38
  11.6 8.3 %collective-permute-start = (bf16[64,1664]{1,0:T(8,128)(2,1)}, bf16[64,1664]{1,0:T(8,128)(2,1)}, u32[]{:S(2)}, u32[]{:S(2)}) collective-permute-start(bf16[64,1664]{1,0:T(8,128)(2,1)} %param.14), channel_id=1, source_target_pairs={{0,1},{1,0},{2,3},{3,2},{4,5},{5,4},{6,7},{7,6},{8,9},{9,8},{10,11... | collective-permute-start | bytes 638984 | tf_op jit(solution)/shard_map/ppermute | solution.py:38
  13.1 10.3 %collective-permute-start.3 = (bf16[64,1664]{1,0:T(8,128)(2,1)}, bf16[64,1664]{1,0:T(8,128)(2,1)S(1)}, u32[]{:S(2)}, u32[]{:S(2)}) collective-permute-start(bf16[64,1664]{1,0:T(8,128)(2,1)} %param.14), channel_id=1, source_target_pairs={{0,2},{1,3},{2,4},{3,5},{4,6},{5,7},{6,0},{7,1},{8,10},{9,11},{10,... | collective-permute-start | bytes 638984 | tf_op jit(solution)/shard_map/ppermute | solution.py:38
  13.1 16.8 %collective-permute-start.5 = (bf16[64,1664]{1,0:T(8,128)(2,1)}, bf16[64,1664]{1,0:T(8,128)(2,1)S(1)}, u32[]{:S(2)}, u32[]{:S(2)}) collective-permute-start(bf16[64,1664]{1,0:T(8,128)(2,1)} %param.14), channel_id=1, source_target_pairs={{0,4},{1,5},{2,6},{3,7},{4,0},{5,1},{6,2},{7,3},{8,12},{9,13},{10,... | collective-permute-start | bytes 638984 | tf_op jit(solution)/shard_map/ppermute | solution.py:38
  14.1 17.4 %collective-permute-start.8 = (bf16[416,624]{1,0:T(8,128)(2,1)}, bf16[416,624]{1,0:T(8,128)(2,1)S(1)}, u32[]{:S(2)}, u32[]{:S(2)}) collective-permute-start(bf16[416,624]{1,0:T(8,128)(2,1)} %refs_0_.1), channel_id=1, source_target_pairs={{0,16},{8,24},{16,0},{24,8},{1,17},{9,25},{17,1},{25,9},{2,18},{10... | collective-permute-start | bytes 1557512 | tf_op jit(solution)/shard_map/ppermute | solution.py:136
  17.6 58.9 %all-gather.10.cloned.1.call-start = ((), (), s32[]{:S(2)}) async-start(), calls=%async_computation.1 | async-start | bytes 4259840 | tf_op jit(solution)/shard_map/all_gather | solution.py:300
  19.8 16.9 %collective-permute-start.7 = (bf16[416,624]{1,0:T(8,128)(2,1)}, bf16[416,624]{1,0:T(8,128)(2,1)S(1)}, u32[]{:S(2)}, u32[]{:S(2)}) collective-permute-start(bf16[416,624]{1,0:T(8,128)(2,1)} %refs_0_.1), channel_id=1, source_target_pairs={{0,8},{8,0},{16,24},{24,16},{1,9},{9,1},{17,25},{25,17},{2,10},{10... | collective-permute-start | bytes 1557512 | tf_op jit(solution)/shard_map/ppermute | solution.py:144
  19.9 11.5 %collective-permute-start.2 = (bf16[64,1664]{1,0:T(8,128)(2,1)S(1)}, bf16[64,1664]{1,0:T(8,128)(2,1)S(1)}, u32[]{:S(2)}, u32[]{:S(2)}) collective-permute-start(bf16[64,1664]{1,0:T(8,128)(2,1)S(1)} %collective-permute-done.1), channel_id=1, source_target_pairs={{0,1},{1,0},{2,3},{3,2},{4,5},{5,4},{6,7},{7,6},{8,9},{9,8},{10,11... | collective-permute-start | bytes 638984 | tf_op jit(solution)/shard_map/ppermute | solution.py:38
  23.3 9.3 %collective-permute-start.4 = (bf16[64,1664]{1,0:T(8,128)(2,1)S(1)}, bf16[64,1664]{1,0:T(8,128)(2,1)S(1)}, u32[]{:S(2)}, u32[]{:S(2)}) collective-permute-start(bf16[64,1664]{1,0:T(8,128)(2,1)S(1)} %collective-permute-done.3), channel_id=1, source_target_pairs={{0,1},{1,0},{2,3},{3,2},{4,5},{5,4},{6,7},{7,6},{8,9},{9,8},{10,11... | collective-permute-start | bytes 638984 | tf_op jit(solution)/shard_map/ppermute | solution.py:38
  40.2 66.0 %all-gather.12.cloned.1.call-start = ((), (), s32[]{:S(2)}) async-start(), calls=%async_computation.2 | async-start | bytes 4259840 | tf_op jit(solution)/shard_map/all_gather | solution.py:300
  47.1 8.2 %collective-permute-start.11 = (bf16[64,1664]{1,0:T(8,128)(2,1)S(1)}, bf16[64,1664]{1,0:T(8,128)(2,1)S(1)}, u32[]{:S(2)}, u32[]{:S(2)}) collective-permute-start(bf16[64,1664]{1,0:T(8,128)(2,1)S(1)} %get-tuple-element.60), channel_id=1, source_target_pairs={{0,1},{1,0},{2,3},{3,2},{4,5},{5,4},{6,7},{7,6},{8,9},{9,8},{10,11... | collective-permute-start | bytes 638984 | tf_op jit(solution)/shard_map/ppermute | solution.py:38
  48.0 11.9 %collective-permute-start.13 = (bf16[64,1664]{1,0:T(8,128)(2,1)S(1)}, bf16[64,1664]{1,0:T(8,128)(2,1)S(1)}, u32[]{:S(2)}, u32[]{:S(2)}) collective-permute-start(bf16[64,1664]{1,0:T(8,128)(2,1)S(1)} %get-tuple-element.62), channel_id=1, source_target_pairs={{0,1},{1,0},{2,3},{3,2},{4,5},{5,4},{6,7},{7,6},{8,9},{9,8},{10,11... | collective-permute-start | bytes 638984 | tf_op jit(solution)/shard_map/ppermute | solution.py:38
  49.1 16.8 %collective-permute-start.15 = (bf16[64,1664]{1,0:T(8,128)(2,1)S(1)}, bf16[64,1664]{1,0:T(8,128)(2,1)S(1)}, u32[]{:S(2)}, u32[]{:S(2)}) collective-permute-start(bf16[64,1664]{1,0:T(8,128)(2,1)S(1)} %get-tuple-element.64), channel_id=1, source_target_pairs={{0,1},{1,0},{2,3},{3,2},{4,5},{5,4},{6,7},{7,6},{8,9},{9,8},{10,11... | collective-permute-start | bytes 638984 | tf_op jit(solution)/shard_map/ppermute | solution.py:38
  50.0 20.2 %collective-permute-start.10 = (bf16[64,1664]{1,0:T(8,128)(2,1)S(1)}, bf16[64,1664]{1,0:T(8,128)(2,1)S(1)}, u32[]{:S(2)}, u32[]{:S(2)}) collective-permute-start(bf16[64,1664]{1,0:T(8,128)(2,1)S(1)} %get-tuple-element.58), channel_id=1, source_target_pairs={{0,1},{1,0},{2,3},{3,2},{4,5},{5,4},{6,7},{7,6},{8,9},{9,8},{10,11... | collective-permute-start | bytes 638984 | tf_op jit(solution)/shard_map/ppermute | solution.py:38
  57.8 12.4 %collective-permute-start.12 = (bf16[64,1664]{1,0:T(8,128)(2,1)}, bf16[64,1664]{1,0:T(8,128)(2,1)S(1)}, u32[]{:S(2)}, u32[]{:S(2)}) collective-permute-start(bf16[64,1664]{1,0:T(8,128)(2,1)} %shard_map.138), channel_id=1, source_target_pairs={{0,4},{1,5},{2,6},{3,7},{4,0},{5,1},{6,2},{7,3},{8,12},{9,13},{10,... | collective-permute-start | bytes 638984 | tf_op jit(solution)/shard_map/ppermute | solution.py:38
  62.4 9.5 %collective-permute-start.14 = (bf16[64,1664]{1,0:T(8,128)(2,1)}, bf16[64,1664]{1,0:T(8,128)(2,1)S(1)}, u32[]{:S(2)}, u32[]{:S(2)}) collective-permute-start(bf16[64,1664]{1,0:T(8,128)(2,1)} %shard_map.139), channel_id=1, source_target_pairs={{0,6},{1,7},{2,0},{3,1},{4,2},{5,3},{6,4},{7,5},{8,14},{9,15},{10,... | collective-permute-start | bytes 638984 | tf_op jit(solution)/shard_map/ppermute | solution.py:38
  68.4 7.9 %collective-permute-start.16 = (bf16[64,1664]{1,0:T(8,128)(2,1)}, bf16[64,1664]{1,0:T(8,128)(2,1)S(1)}, u32[]{:S(2)}, u32[]{:S(2)}) collective-permute-start(bf16[64,1664]{1,0:T(8,128)(2,1)} %shard_map.140), channel_id=1, source_target_pairs={{0,2},{1,3},{2,4},{3,5},{4,6},{5,7},{6,0},{7,1},{8,10},{9,11},{10,... | collective-permute-start | bytes 638984 | tf_op jit(solution)/shard_map/ppermute | solution.py:38
  76.5 71.6 %all-gather.14.cloned.1.call-start = ((), (), s32[]{:S(2)}) async-start(), calls=%async_computation.3 | async-start | bytes 3461120 | tf_op jit(solution)/shard_map/all_gather | solution.py:300
  76.6 23.3 %collective-permute-start.17 = (bf16[64,1664]{1,0:T(8,128)(2,1)S(1)}, bf16[64,1664]{1,0:T(8,128)(2,1)S(1)}, u32[]{:S(2)}, u32[]{:S(2)}) collective-permute-start(bf16[64,1664]{1,0:T(8,128)(2,1)S(1)} %add_convert_fusion.3), channel_id=1, source_target_pairs={{0,1},{1,0},{2,3},{3,2},{4,5},{5,4},{6,7},{7,6},{8,9},{9,8},{10,11... | collective-permute-start | bytes 638984 | tf_op jit(solution)/shard_map/ppermute | solution.py:38
  77.2 8.7 %collective-permute-start.18 = (bf16[64,1664]{1,0:T(8,128)(2,1)S(1)}, bf16[64,1664]{1,0:T(8,128)(2,1)S(1)}, u32[]{:S(2)}, u32[]{:S(2)}) collective-permute-start(bf16[64,1664]{1,0:T(8,128)(2,1)S(1)} %add_convert_fusion.3), channel_id=1, source_target_pairs={{0,6},{1,7},{2,0},{3,1},{4,2},{5,3},{6,4},{7,5},{8,14},{9,15},{10,... | collective-permute-start | bytes 638984 | tf_op jit(solution)/shard_map/ppermute | solution.py:38
  80.2 10.7 %collective-permute-start.20 = (bf16[64,1664]{1,0:T(8,128)(2,1)S(1)}, bf16[64,1664]{1,0:T(8,128)(2,1)S(1)}, u32[]{:S(2)}, u32[]{:S(2)}) collective-permute-start(bf16[64,1664]{1,0:T(8,128)(2,1)S(1)} %add_convert_fusion.3), channel_id=1, source_target_pairs={{0,2},{1,3},{2,4},{3,5},{4,6},{5,7},{6,0},{7,1},{8,10},{9,11},{10,... | collective-permute-start | bytes 638984 | tf_op jit(solution)/shard_map/ppermute | solution.py:38
  80.2 18.2 %collective-permute-start.22 = (bf16[64,1664]{1,0:T(8,128)(2,1)S(1)}, bf16[64,1664]{1,0:T(8,128)(2,1)S(1)}, u32[]{:S(2)}, u32[]{:S(2)}) collective-permute-start(bf16[64,1664]{1,0:T(8,128)(2,1)S(1)} %add_convert_fusion.3), channel_id=1, source_target_pairs={{0,4},{1,5},{2,6},{3,7},{4,0},{5,1},{6,2},{7,3},{8,12},{9,13},{10,... | collective-permute-start | bytes 638984 | tf_op jit(solution)/shard_map/ppermute | solution.py:38
  85.9 14.0 %collective-permute-start.19 = (bf16[64,1664]{1,0:T(8,128)(2,1)S(1)}, bf16[64,1664]{1,0:T(8,128)(2,1)S(1)}, u32[]{:S(2)}, u32[]{:S(2)}) collective-permute-start(bf16[64,1664]{1,0:T(8,128)(2,1)S(1)} %collective-permute-done.18), channel_id=1, source_target_pairs={{0,1},{1,0},{2,3},{3,2},{4,5},{5,4},{6,7},{7,6},{8,9},{9,8},{10,11... | collective-permute-start | bytes 638984 | tf_op jit(solution)/shard_map/ppermute | solution.py:38
  90.9 9.1 %collective-permute-start.21 = (bf16[64,1664]{1,0:T(8,128)(2,1)S(1)}, bf16[64,1664]{1,0:T(8,128)(2,1)S(1)}, u32[]{:S(2)}, u32[]{:S(2)}) collective-permute-start(bf16[64,1664]{1,0:T(8,128)(2,1)S(1)} %collective-permute-done.20), channel_id=1, source_target_pairs={{0,1},{1,0},{2,3},{3,2},{4,5},{5,4},{6,7},{7,6},{8,9},{9,8},{10,11... | collective-permute-start | bytes 638984 | tf_op jit(solution)/shard_map/ppermute | solution.py:38
  106.3 74.9 %all-gather.16.cloned.1.call-start = ((), (), s32[]{:S(2)}) async-start(), calls=%async_computation.4 | async-start | bytes 2662400 | tf_op jit(solution)/shard_map/all_gather | solution.py:300
  118.0 8.1 %collective-permute-start.25 = (bf16[64,1664]{1,0:T(8,128)(2,1)S(1)}, bf16[64,1664]{1,0:T(8,128)(2,1)S(1)}, u32[]{:S(2)}, u32[]{:S(2)}) collective-permute-start(bf16[64,1664]{1,0:T(8,128)(2,1)S(1)} %get-tuple-element.74), channel_id=1, source_target_pairs={{0,1},{1,0},{2,3},{3,2},{4,5},{5,4},{6,7},{7,6},{8,9},{9,8},{10,11... | collective-permute-start | bytes 638984 | tf_op jit(solution)/shard_map/ppermute | solution.py:38
  119.4 11.5 %collective-permute-start.27 = (bf16[64,1664]{1,0:T(8,128)(2,1)}, bf16[64,1664]{1,0:T(8,128)(2,1)S(1)}, u32[]{:S(2)}, u32[]{:S(2)}) collective-permute-start(bf16[64,1664]{1,0:T(8,128)(2,1)} %get-tuple-element.76), channel_id=1, source_target_pairs={{0,1},{1,0},{2,3},{3,2},{4,5},{5,4},{6,7},{7,6},{8,9},{9,8},{10,11... | collective-permute-start | bytes 638984 | tf_op jit(solution)/shard_map/ppermute | solution.py:38
  120.0 16.4 %collective-permute-start.29 = (bf16[64,1664]{1,0:T(8,128)(2,1)S(1)}, bf16[64,1664]{1,0:T(8,128)(2,1)S(1)}, u32[]{:S(2)}, u32[]{:S(2)}) collective-permute-start(bf16[64,1664]{1,0:T(8,128)(2,1)S(1)} %get-tuple-element.78), channel_id=1, source_target_pairs={{0,1},{1,0},{2,3},{3,2},{4,5},{5,4},{6,7},{7,6},{8,9},{9,8},{10,11... | collective-permute-start | bytes 638984 | tf_op jit(solution)/shard_map/ppermute | solution.py:38
  121.4 19.1 %collective-permute-start.24 = (bf16[64,1664]{1,0:T(8,128)(2,1)S(1)}, bf16[64,1664]{1,0:T(8,128)(2,1)S(1)}, u32[]{:S(2)}, u32[]{:S(2)}) collective-permute-start(bf16[64,1664]{1,0:T(8,128)(2,1)S(1)} %get-tuple-element.72), channel_id=1, source_target_pairs={{0,1},{1,0},{2,3},{3,2},{4,5},{5,4},{6,7},{7,6},{8,9},{9,8},{10,11... | collective-permute-start | bytes 638984 | tf_op jit(solution)/shard_map/ppermute | solution.py:38
  128.5 12.5 %collective-permute-start.26 = (bf16[64,1664]{1,0:T(8,128)(2,1)}, bf16[64,1664]{1,0:T(8,128)(2,1)S(1)}, u32[]{:S(2)}, u32[]{:S(2)}) collective-permute-start(bf16[64,1664]{1,0:T(8,128)(2,1)} %shard_map.142), channel_id=1, source_target_pairs={{0,4},{1,5},{2,6},{3,7},{4,0},{5,1},{6,2},{7,3},{8,12},{9,13},{10,... | collective-permute-start | bytes 638984 | tf_op jit(solution)/shard_map/ppermute | solution.py:38
  133.3 9.4 %collective-permute-start.28 = (bf16[64,1664]{1,0:T(8,128)(2,1)}, bf16[64,1664]{1,0:T(8,128)(2,1)S(1)}, u32[]{:S(2)}, u32[]{:S(2)}) collective-permute-start(bf16[64,1664]{1,0:T(8,128)(2,1)} %shard_map.143), channel_id=1, source_target_pairs={{0,6},{1,7},{2,0},{3,1},{4,2},{5,3},{6,4},{7,5},{8,14},{9,15},{10,... | collective-permute-start | bytes 638984 | tf_op jit(solution)/shard_map/ppermute | solution.py:38
  138.9 8.2 %collective-permute-start.30 = (bf16[64,1664]{1,0:T(8,128)(2,1)}, bf16[64,1664]{1,0:T(8,128)(2,1)S(1)}, u32[]{:S(2)}, u32[]{:S(2)}) collective-permute-start(bf16[64,1664]{1,0:T(8,128)(2,1)} %shard_map.144), channel_id=1, source_target_pairs={{0,2},{1,3},{2,4},{3,5},{4,6},{5,7},{6,0},{7,1},{8,10},{9,11},{10,... | collective-permute-start | bytes 638984 | tf_op jit(solution)/shard_map/ppermute | solution.py:38
  148.9 13.3 %collective-permute-start.31 = (bf16[16,6656]{1,0:T(8,128)(2,1)S(1)}, bf16[16,6656]{1,0:T(8,128)(2,1)}, u32[]{:S(2)}, u32[]{:S(2)}) collective-permute-start(bf16[16,6656]{1,0:T(8,128)(2,1)S(1)} %reshape.275), channel_id=1, source_target_pairs={{0,1},{1,0},{2,3},{3,2},{4,5},{5,4},{6,7},{7,6},{8,9},{9,8},{10,11... | collective-permute-start | bytes 638984 | tf_op jit(solution)/shard_map/ppermute | solution.py:38
  150.6 11.0 %collective-permute-start.32 = (bf16[16,6656]{1,0:T(8,128)(2,1)S(1)}, bf16[16,6656]{1,0:T(8,128)(2,1)}, u32[]{:S(2)}, u32[]{:S(2)}) collective-permute-start(bf16[16,6656]{1,0:T(8,128)(2,1)S(1)} %reshape.275), channel_id=1, source_target_pairs={{0,6},{1,7},{2,0},{3,1},{4,2},{5,3},{6,4},{7,5},{8,14},{9,15},{10,... | collective-permute-start | bytes 638984 | tf_op jit(solution)/shard_map/ppermute | solution.py:38
  156.0 11.4 %collective-permute-start.34 = (bf16[16,6656]{1,0:T(8,128)(2,1)S(1)}, bf16[16,6656]{1,0:T(8,128)(2,1)S(1)}, u32[]{:S(2)}, u32[]{:S(2)}) collective-permute-start(bf16[16,6656]{1,0:T(8,128)(2,1)S(1)} %reshape.275), channel_id=1, source_target_pairs={{0,2},{1,3},{2,4},{3,5},{4,6},{5,7},{6,0},{7,1},{8,10},{9,11},{10,... | collective-permute-start | bytes 638984 | tf_op jit(solution)/shard_map/ppermute | solution.py:38
  156.0 17.9 %collective-permute-start.36 = (bf16[16,6656]{1,0:T(8,128)(2,1)S(1)}, bf16[16,6656]{1,0:T(8,128)(2,1)S(1)}, u32[]{:S(2)}, u32[]{:S(2)}) collective-permute-start(bf16[16,6656]{1,0:T(8,128)(2,1)S(1)} %reshape.275), channel_id=1, source_target_pairs={{0,4},{1,5},{2,6},{3,7},{4,0},{5,1},{6,2},{7,3},{8,12},{9,13},{10,... | collective-permute-start | bytes 638984 | tf_op jit(solution)/shard_map/ppermute | solution.py:38
  157.2 78.9 %all-gather.18.cloned.1.call-start = ((), (), s32[]{:S(2)}) async-start(), calls=%async_computation.5 | async-start | bytes 4259840 | tf_op jit(solution)/shard_map/all_gather | solution.py:300
  161.6 12.9 %collective-permute-start.33 = (bf16[16,6656]{1,0:T(8,128)(2,1)}, bf16[16,6656]{1,0:T(8,128)(2,1)S(1)}, u32[]{:S(2)}, u32[]{:S(2)}) collective-permute-start(bf16[16,6656]{1,0:T(8,128)(2,1)} %collective-permute-done.32), channel_id=1, source_target_pairs={{0,1},{1,0},{2,3},{3,2},{4,5},{5,4},{6,7},{7,6},{8,9},{9,8},{10,11... | collective-permute-start | bytes 638984 | tf_op jit(solution)/shard_map/ppermute | solution.py:38
  181.2 121.3 %all-gather.20.cloned.1.call-start = ((), (), s32[]{:S(2)}) async-start(), calls=%async_computation.6 | async-start | bytes 4259840 | tf_op jit(solution)/shard_map/all_gather | solution.py:300
  197.3 12.6 %collective-permute-start.46 = (bf16[80,1664]{1,0:T(8,128)(2,1)S(1)}, bf16[80,1664]{1,0:T(8,128)(2,1)S(1)}, u32[]{:S(2)}, u32[]{:S(2)}) collective-permute-start(bf16[80,1664]{1,0:T(8,128)(2,1)S(1)} %get-tuple-element.117), channel_id=1, source_target_pairs={{0,6},{1,7},{2,0},{3,1},{4,2},{5,3},{6,4},{7,5},{8,14},{9,15},{10,... | collective-permute-start | bytes 798728 | tf_op jit(solution)/shard_map/ppermute | solution.py:38
  198.8 13.0 %collective-permute-start.48 = (bf16[80,1664]{1,0:T(8,128)(2,1)S(1)}, bf16[80,1664]{1,0:T(8,128)(2,1)S(1)}, u32[]{:S(2)}, u32[]{:S(2)}) collective-permute-start(bf16[80,1664]{1,0:T(8,128)(2,1)S(1)} %get-tuple-element.117), channel_id=1, source_target_pairs={{0,2},{1,3},{2,4},{3,5},{4,6},{5,7},{6,0},{7,1},{8,10},{9,11},{10,... | collective-permute-start | bytes 798728 | tf_op jit(solution)/shard_map/ppermute | solution.py:38
  199.3 20.6 %collective-permute-start.50 = (bf16[80,1664]{1,0:T(8,128)(2,1)S(1)}, bf16[80,1664]{1,0:T(8,128)(2,1)S(1)}, u32[]{:S(2)}, u32[]{:S(2)}) collective-permute-start(bf16[80,1664]{1,0:T(8,128)(2,1)S(1)} %get-tuple-element.117), channel_id=1, source_target_pairs={{0,4},{1,5},{2,6},{3,7},{4,0},{5,1},{6,2},{7,3},{8,12},{9,13},{10,... | collective-permute-start | bytes 798728 | tf_op jit(solution)/shard_map/ppermute | solution.py:38
  199.6 20.8 %collective-permute-start.45 = (bf16[80,1664]{1,0:T(8,128)(2,1)S(1)}, bf16[80,1664]{1,0:T(8,128)(2,1)S(1)}, u32[]{:S(2)}, u32[]{:S(2)}) collective-permute-start(bf16[80,1664]{1,0:T(8,128)(2,1)S(1)} %get-tuple-element.117), channel_id=1, source_target_pairs={{0,1},{1,0},{2,3},{3,2},{4,5},{5,4},{6,7},{7,6},{8,9},{9,8},{10,11... | collective-permute-start | bytes 798728 | tf_op jit(solution)/shard_map/ppermute | solution.py:38
  209.8 10.6 %collective-permute-start.47 = (bf16[80,1664]{1,0:T(8,128)(2,1)S(1)}, bf16[80,1664]{1,0:T(8,128)(2,1)S(1)}, u32[]{:S(2)}, u32[]{:S(2)}) collective-permute-start(bf16[80,1664]{1,0:T(8,128)(2,1)S(1)} %collective-permute-done.46), channel_id=1, source_target_pairs={{0,1},{1,0},{2,3},{3,2},{4,5},{5,4},{6,7},{7,6},{8,9},{9,8},{10,11... | collective-permute-start | bytes 798728 | tf_op jit(solution)/shard_map/ppermute | solution.py:38
  211.8 8.8 %collective-permute-start.49 = (bf16[80,1664]{1,0:T(8,128)(2,1)S(1)}, bf16[80,1664]{1,0:T(8,128)(2,1)S(1)}, u32[]{:S(2)}, u32[]{:S(2)}) collective-permute-start(bf16[80,1664]{1,0:T(8,128)(2,1)S(1)} %collective-permute-done.48), channel_id=1, source_target_pairs={{0,1},{1,0},{2,3},{3,2},{4,5},{5,4},{6,7},{7,6},{8,9},{9,8},{10,11... | collective-permute-start | bytes 798728 | tf_op jit(solution)/shard_map/ppermute | solution.py:38
  239.3 9.3 %collective-permute-start.53 = (bf16[80,1664]{1,0:T(8,128)(2,1)S(1)}, bf16[80,1664]{1,0:T(8,128)(2,1)S(1)}, u32[]{:S(2)}, u32[]{:S(2)}) collective-permute-start(bf16[80,1664]{1,0:T(8,128)(2,1)S(1)} %get-tuple-element.90), channel_id=1, source_target_pairs={{0,1},{1,0},{2,3},{3,2},{4,5},{5,4},{6,7},{7,6},{8,9},{9,8},{10,11... | collective-permute-start | bytes 798728 | tf_op jit(solution)/shard_map/ppermute | solution.py:38
  239.8 16.1 %collective-permute-start.55 = (bf16[80,1664]{1,0:T(8,128)(2,1)S(1)}, bf16[80,1664]{1,0:T(8,128)(2,1)S(1)}, u32[]{:S(2)}, u32[]{:S(2)}) collective-permute-start(bf16[80,1664]{1,0:T(8,128)(2,1)S(1)} %get-tuple-element.92), channel_id=1, source_target_pairs={{0,1},{1,0},{2,3},{3,2},{4,5},{5,4},{6,7},{7,6},{8,9},{9,8},{10,11... | collective-permute-start | bytes 798728 | tf_op jit(solution)/shard_map/ppermute | solution.py:38
  241.4 20.4 %collective-permute-start.57 = (bf16[80,1664]{1,0:T(8,128)(2,1)S(1)}, bf16[80,1664]{1,0:T(8,128)(2,1)S(1)}, u32[]{:S(2)}, u32[]{:S(2)}) collective-permute-start(bf16[80,1664]{1,0:T(8,128)(2,1)S(1)} %get-tuple-element.94), channel_id=1, source_target_pairs={{0,1},{1,0},{2,3},{3,2},{4,5},{5,4},{6,7},{7,6},{8,9},{9,8},{10,11... | collective-permute-start | bytes 798728 | tf_op jit(solution)/shard_map/ppermute | solution.py:38
  241.8 22.5 %collective-permute-start.52 = (bf16[80,1664]{1,0:T(8,128)(2,1)S(1)}, bf16[80,1664]{1,0:T(8,128)(2,1)S(1)}, u32[]{:S(2)}, u32[]{:S(2)}) collective-permute-start(bf16[80,1664]{1,0:T(8,128)(2,1)S(1)} %get-tuple-element.88), channel_id=1, source_target_pairs={{0,1},{1,0},{2,3},{3,2},{4,5},{5,4},{6,7},{7,6},{8,9},{9,8},{10,11... | collective-permute-start | bytes 798728 | tf_op jit(solution)/shard_map/ppermute | solution.py:38
  251.2 15.1 %collective-permute-start.54 = (bf16[80,1664]{1,0:T(8,128)(2,1)}, bf16[80,1664]{1,0:T(8,128)(2,1)S(1)}, u32[]{:S(2)}, u32[]{:S(2)}) collective-permute-start(bf16[80,1664]{1,0:T(8,128)(2,1)} %shard_map.147), channel_id=1, source_target_pairs={{0,4},{1,5},{2,6},{3,7},{4,0},{5,1},{6,2},{7,3},{8,12},{9,13},{10,... | collective-permute-start | bytes 798728 | tf_op jit(solution)/shard_map/ppermute | solution.py:38
  258.4 8.8 %collective-permute-start.56 = (bf16[80,1664]{1,0:T(8,128)(2,1)}, bf16[80,1664]{1,0:T(8,128)(2,1)S(1)}, u32[]{:S(2)}, u32[]{:S(2)}) collective-permute-start(bf16[80,1664]{1,0:T(8,128)(2,1)} %shard_map.148), channel_id=1, source_target_pairs={{0,6},{1,7},{2,0},{3,1},{4,2},{5,3},{6,4},{7,5},{8,14},{9,15},{10,... | collective-permute-start | bytes 798728 | tf_op jit(solution)/shard_map/ppermute | solution.py:38
  264.3 11.0 %collective-permute-start.58 = (bf16[80,1664]{1,0:T(8,128)(2,1)}, bf16[80,1664]{1,0:T(8,128)(2,1)S(1)}, u32[]{:S(2)}, u32[]{:S(2)}) collective-permute-start(bf16[80,1664]{1,0:T(8,128)(2,1)} %shard_map.149), channel_id=1, source_target_pairs={{0,2},{1,3},{2,4},{3,5},{4,6},{5,7},{6,0},{7,1},{8,10},{9,11},{10,... | collective-permute-start | bytes 798728 | tf_op jit(solution)/shard_map/ppermute | solution.py:38
  276.6 9.5 %collective-permute-start.60 = (bf16[80,1664]{1,0:T(8,128)(2,1)S(1)}, bf16[80,1664]{1,0:T(8,128)(2,1)S(1)}, u32[]{:S(2)}, u32[]{:S(2)}) collective-permute-start(bf16[80,1664]{1,0:T(8,128)(2,1)S(1)} %get-tuple-element.106), channel_id=1, source_target_pairs={{0,6},{1,7},{2,0},{3,1},{4,2},{5,3},{6,4},{7,5},{8,14},{9,15},{10,... | collective-permute-start | bytes 798728 | tf_op jit(solution)/shard_map/ppermute | solution.py:38
  281.2 10.8 %collective-permute-start.62 = (bf16[80,1664]{1,0:T(8,128)(2,1)S(1)}, bf16[80,1664]{1,0:T(8,128)(2,1)S(1)}, u32[]{:S(2)}, u32[]{:S(2)}) collective-permute-start(bf16[80,1664]{1,0:T(8,128)(2,1)S(1)} %get-tuple-element.106), channel_id=1, source_target_pairs={{0,2},{1,3},{2,4},{3,5},{4,6},{5,7},{6,0},{7,1},{8,10},{9,11},{10,... | collective-permute-start | bytes 798728 | tf_op jit(solution)/shard_map/ppermute | solution.py:38
  281.7 14.4 %collective-permute-start.64 = (bf16[80,1664]{1,0:T(8,128)(2,1)S(1)}, bf16[80,1664]{1,0:T(8,128)(2,1)S(1)}, u32[]{:S(2)}, u32[]{:S(2)}) collective-permute-start(bf16[80,1664]{1,0:T(8,128)(2,1)S(1)} %get-tuple-element.106), channel_id=1, source_target_pairs={{0,4},{1,5},{2,6},{3,7},{4,0},{5,1},{6,2},{7,3},{8,12},{9,13},{10,... | collective-permute-start | bytes 798728 | tf_op jit(solution)/shard_map/ppermute | solution.py:38
  285.2 10.9 %collective-permute-start.59 = (bf16[80,1664]{1,0:T(8,128)(2,1)S(1)}, bf16[80,1664]{1,0:T(8,128)(2,1)S(1)}, u32[]{:S(2)}, u32[]{:S(2)}) collective-permute-start(bf16[80,1664]{1,0:T(8,128)(2,1)S(1)} %get-tuple-element.106), channel_id=1, source_target_pairs={{0,1},{1,0},{2,3},{3,2},{4,5},{5,4},{6,7},{7,6},{8,9},{9,8},{10,11... | collective-permute-start | bytes 798728 | tf_op jit(solution)/shard_map/ppermute | solution.py:38
  286.2 10.0 %collective-permute-start.61 = (bf16[80,1664]{1,0:T(8,128)(2,1)S(1)}, bf16[80,1664]{1,0:T(8,128)(2,1)S(1)}, u32[]{:S(2)}, u32[]{:S(2)}) collective-permute-start(bf16[80,1664]{1,0:T(8,128)(2,1)S(1)} %collective-permute-done.60), channel_id=1, source_target_pairs={{0,1},{1,0},{2,3},{3,2},{4,5},{5,4},{6,7},{7,6},{8,9},{9,8},{10,11... | collective-permute-start | bytes 798728 | tf_op jit(solution)/shard_map/ppermute | solution.py:38
  314.1 9.3 %collective-permute-start.69 = (bf16[80,1664]{1,0:T(8,128)(2,1)S(1)}, bf16[80,1664]{1,0:T(8,128)(2,1)S(1)}, u32[]{:S(2)}, u32[]{:S(2)}) collective-permute-start(bf16[80,1664]{1,0:T(8,128)(2,1)S(1)} %get-tuple-element.102), channel_id=1, source_target_pairs={{0,1},{1,0},{2,3},{3,2},{4,5},{5,4},{6,7},{7,6},{8,9},{9,8},{10,11... | collective-permute-start | bytes 798728 | tf_op jit(solution)/shard_map/ppermute | solution.py:38
  316.1 14.9 %collective-permute-start.71 = (bf16[80,1664]{1,0:T(8,128)(2,1)S(1)}, bf16[80,1664]{1,0:T(8,128)(2,1)S(1)}, u32[]{:S(2)}, u32[]{:S(2)}) collective-permute-start(bf16[80,1664]{1,0:T(8,128)(2,1)S(1)} %get-tuple-element.104), channel_id=1, source_target_pairs={{0,1},{1,0},{2,3},{3,2},{4,5},{5,4},{6,7},{7,6},{8,9},{9,8},{10,11... | collective-permute-start | bytes 798728 | tf_op jit(solution)/shard_map/ppermute | solution.py:38
  316.2 17.4 %collective-permute-start.66 = (bf16[80,1664]{1,0:T(8,128)(2,1)S(1)}, bf16[80,1664]{1,0:T(8,128)(2,1)S(1)}, u32[]{:S(2)}, u32[]{:S(2)}) collective-permute-start(bf16[80,1664]{1,0:T(8,128)(2,1)S(1)} %get-tuple-element.98), channel_id=1, source_target_pairs={{0,1},{1,0},{2,3},{3,2},{4,5},{5,4},{6,7},{7,6},{8,9},{9,8},{10,11... | collective-permute-start | bytes 798728 | tf_op jit(solution)/shard_map/ppermute | solution.py:38
  323.0 11.9 %collective-permute-start.68 = (bf16[80,1664]{1,0:T(8,128)(2,1)}, bf16[80,1664]{1,0:T(8,128)(2,1)S(1)}, u32[]{:S(2)}, u32[]{:S(2)}) collective-permute-start(bf16[80,1664]{1,0:T(8,128)(2,1)} %shard_map.151), channel_id=1, source_target_pairs={{0,4},{1,5},{2,6},{3,7},{4,0},{5,1},{6,2},{7,3},{8,12},{9,13},{10,... | collective-permute-start | bytes 798728 | tf_op jit(solution)/shard_map/ppermute | solution.py:38
  325.9 11.7 %collective-permute-start.70 = (bf16[80,1664]{1,0:T(8,128)(2,1)}, bf16[80,1664]{1,0:T(8,128)(2,1)S(1)}, u32[]{:S(2)}, u32[]{:S(2)}) collective-permute-start(bf16[80,1664]{1,0:T(8,128)(2,1)} %shard_map.152), channel_id=1, source_target_pairs={{0,6},{1,7},{2,0},{3,1},{4,2},{5,3},{6,4},{7,5},{8,14},{9,15},{10,... | collective-permute-start | bytes 798728 | tf_op jit(solution)/shard_map/ppermute | solution.py:38
  333.5 8.4 %collective-permute-start.72 = (bf16[80,1664]{1,0:T(8,128)(2,1)}, bf16[80,1664]{1,0:T(8,128)(2,1)S(1)}, u32[]{:S(2)}, u32[]{:S(2)}) collective-permute-start(bf16[80,1664]{1,0:T(8,128)(2,1)} %shard_map.153), channel_id=1, source_target_pairs={{0,2},{1,3},{2,4},{3,5},{4,6},{5,7},{6,0},{7,1},{8,10},{9,11},{10,... | collective-permute-start | bytes 798728 | tf_op jit(solution)/shard_map/ppermute | solution.py:38
  (58 other events, 357.7 us)
Sparse Core Ops, SparseCore 0:
  17.7 19.8 all-gather.7
  40.3 30.3 all-gather.9
  76.7 29.5 all-gather.11
  107.7 26.3 all-gather.13
  157.3 21.7 all-gather.15
  181.4 29.2 all-gather.17
  236.3 31.5 all-gather.19
